TPU v7x, 512 devices: a whole 4x8x8 slice. The times are simulated.
512 devices in a mesh: gx: 16 (over y, core), gy: 4 (over x), gz: 8 (over z).
Axes of the slice: x: 4, y: 8, z: 8, core: 2. Of those that a mesh axis runs over, the one named last changes fastest.
Arguments:
- right_side: float32 [64, 512, 512], P('gz', 'gx', 'gy'), may hold values from -6 to 6
- acoef: float32 [64, 512, 512], P('gz', 'gx', 'gy'), may hold values from 0.02 to 0.2
- beta: float32 [64, 512, 512], P('gz', 'gx', 'gy'), may hold values from 0.5 to 4
Outputs:
- solution: float32 [64, 512, 512], P('gz', 'gx', 'gy')
- residual: float32 [64, 512, 512], P('gz', 'gx', 'gy')
All inputs are finite; a program needn't handle non-finite values.
Results may differ from a plain program's by a relative error of at most 0.0003.
Values sent between devices are 32-bit elements; how exact they have to be, the bound alone decides.
No kernel may reach another device: no remote copies, remote signals or barrier semaphores. Data moves between devices by JAX's collectives and lax.ppermute only.
A program may use at most 64 MiB of HBM per device.

v0:
```python
import jax
import jax.numpy as jnp
from jax import lax
from jax.sharding import PartitionSpec as P

LEVELS = 4
SWEEPS = 2
BOTTOM = 16


smooth_low = 0.3
bottom_low = 0.05
upper_bound = 2.0
face_scale = 1.0 / 6.0


def with_halo(value, sides, width):
    for axis, dim in sides:
        peers, length = (lax.axis_size(axis), value.shape[dim])
        up = [(i, (i + 1) % peers) for i in range(peers - 1)]
        down = [(j, i) for i, j in up]
        last = lax.slice_in_dim(value, length - width, length, axis=dim)
        first = lax.slice_in_dim(value, 0, width, axis=dim)
        before = lax.ppermute(last, axis, up)
        after = lax.ppermute(first, axis, down)
        value = jnp.concatenate([before, value, after], axis=dim)
    return value


def neighbours(padded):
    return [
        padded[:-2, 1:-1, 1:-1],
        padded[2:, 1:-1, 1:-1],
        padded[1:-1, :-2, 1:-1],
        padded[1:-1, 2:, 1:-1],
        padded[1:-1, 1:-1, :-2],
        padded[1:-1, 1:-1, 2:],
    ]


def restrict(values):
    shape = values.shape
    return values.reshape(shape[0] // 2, 2, shape[1] // 2, 2, shape[2] // 2, 2).mean(axis=(1, 3, 5))


def prolong(values):
    return jnp.repeat(jnp.repeat(jnp.repeat(values, 2, axis=0), 2, axis=1), 2, axis=2)


def level_weights(acoef_level, beta_padded, grid_level):
    beta_inner = beta_padded[1:-1, 1:-1, 1:-1]
    scale = face_scale * 0.25**grid_level
    weights = [scale * 0.5 * (beta_inner + other) for other in neighbours(beta_padded)]
    diagonal = acoef_level
    for weight in weights:
        diagonal = diagonal + weight
    return (weights, diagonal, 1.0 / diagonal)


def operate(iterate, padded, weights, diagonal):
    result = diagonal * iterate
    for weight, other in zip(weights, neighbours(padded)):
        result = result - weight * other
    return result


def smooth(iterate, source, apply_level, inverse, sweeps, lower):
    centre = (upper_bound + lower) / 2.0
    half_width = (upper_bound - lower) / 2.0
    sigma_ratio = centre / half_width
    rho_prev = 1.0 / sigma_ratio
    if iterate is None:
        defect = source
    else:
        defect = source - apply_level(iterate)
    update = defect * inverse * (1.0 / centre)
    iterate = update if iterate is None else iterate + update
    for sweep_index in range(1, sweeps):
        defect = source - apply_level(iterate)
        rho_next = 1.0 / (2.0 * sigma_ratio - rho_prev)
        update = rho_next * rho_prev * update + 2.0 * rho_next / half_width * (defect * inverse)
        rho_prev = rho_next
        iterate = iterate + update
    return iterate


def face_halo(values):
    return with_halo(values, (("gx", 1), ("gy", 2), ("gz", 0)), 1)


def coefficient_halo(values):
    return with_halo(values, (("gx", 1), ("gy", 2), ("gz", 0)), 1)


def on_device(right_side, acoef, beta):
    coarse_list = [(acoef, beta)]
    for grid_level in range(1, LEVELS):
        coarse_list.append((restrict(coarse_list[-1][0]), restrict(coarse_list[-1][1])))
    halo_levels = LEVELS
    level_ops = []
    for grid_level in range(halo_levels):
        level_ops.append(
            level_weights(
                coarse_list[grid_level][0], coefficient_halo(coarse_list[grid_level][1]), grid_level
            )
        )

    def make_apply(grid_level):
        weights, diagonal, inverse = level_ops[grid_level]

        def apply_level(values):
            return operate(values, face_halo(values), weights, diagonal)

        return apply_level

    def vcycle(source, grid_level):
        if grid_level == LEVELS - 1:
            return smooth(
                None, source, make_apply(grid_level), level_ops[grid_level][2], BOTTOM, bottom_low
            )
        apply_level = make_apply(grid_level)
        inverse = level_ops[grid_level][2]
        iterate = smooth(None, source, apply_level, inverse, SWEEPS, smooth_low)
        defect = source - apply_level(iterate)
        iterate = iterate + prolong(vcycle(restrict(defect), grid_level + 1))
        return smooth(iterate, source, apply_level, inverse, SWEEPS, smooth_low)

    solution = vcycle(right_side, 0)
    residual = right_side - make_apply(0)(solution)
    return (solution, residual)


def solution(mesh):
    return jax.shard_map(
        on_device,
        mesh=mesh,
        in_specs=(P("gz", "gx", "gy"), P("gz", "gx", "gy"), P("gz", "gx", "gy")),
        out_specs=(P("gz", "gx", "gy"), P("gz", "gx", "gy")),
        check_vma=False,
    )
```

profile of v0, /device:TPU:1, one launch (start us, length us, event | category | flops | bytes accessed | tf_op | source)
XLA Modules:
  0.0 826.6 jit_solution(5734609862080263079)
XLA Ops:
  1.4 8.8 %collective-permute-start.1 = (f32[8,1,128]{2,1,0:T(1,128)S(1)}, f32[8,1,128]{2,1,0:T(1,128)S(1)}, u32[]{:S(2)}, u32[]{:S(2)}) collective-permute-start(f32[8,1,128]{2,1,0:T(1,128)S(1)} %get-tuple-element.101), channel_id=1, source_target_pairs={{32,0},{64,32},{96,64},{128,96},{160,128},{192,160},{224,192},{256... | collective-permute-start | bytes 12296 | tf_op jit(solution)/shard_map/ppermute | solution.py:25
  12.3 10.5 %reshape.91 = f32[4,2,16,2,64,2]{5,4,3,2,1,0:T(8,128)} reshape(f32[8,32,128]{2,1,0:T(8,128)} %param.5) | data formatting | bytes 262144 | tf_op jit(solution)/shard_map/reshape | solution.py:43
  35.9 9.8 %reshape.90 = f32[4,2,16,2,64,2]{5,4,3,2,1,0:T(8,128)} reshape(f32[8,32,128]{2,1,0:T(8,128)S(1)} %copy-done.1) | data formatting | bytes 262144 | tf_op jit(solution)/shard_map/reshape | solution.py:43
  134.5 9.8 %reshape.89 = f32[4,2,16,2,64,2]{5,4,3,2,1,0:T(8,128)} reshape(f32[8,32,128]{2,1,0:T(8,128)S(1)} %fusion.46) | data formatting | bytes 262144 | tf_op jit(solution)/shard_map/reshape | solution.py:43
  178.2 7.2 collective-permute-start.30
  208.7 6.3 collective-permute-start.42
  234.9 6.1 collective-permute-start.58
  269.3 6.3 collective-permute-start.60
  287.8 5.5 collective-permute-start.64
  358.8 5.5 collective-permute-start.82
  365.1 5.5 collective-permute-start.84
  382.9 5.7 collective-permute-start.88
  389.5 5.5 collective-permute-start.90
  407.3 5.7 collective-permute-start.94
  413.9 5.5 collective-permute-start.96
  431.7 5.7 collective-permute-start.100
  438.2 5.5 collective-permute-start.102
  456.0 5.7 collective-permute-start.106
  462.6 5.5 collective-permute-start.108
  480.4 5.7 collective-permute-start.112
  487.0 5.5 collective-permute-start.114
  504.7 5.7 collective-permute-start.118
  529.1 5.7 collective-permute-start.124
  553.5 5.7 collective-permute-start.130
  577.8 5.7 collective-permute-start.136
  584.4 5.5 collective-permute-start.138
  602.2 5.7 collective-permute-start.142
  608.8 5.5 collective-permute-start.144
  626.5 5.7 collective-permute-start.148
  742.9 6.0 collective-permute-start.174
  770.9 5.7 collective-permute-start.180
  798.4 5.7 collective-permute-start.186
  (627 shorter events, 622.8 us)
Async XLA Ops:
  1.4 48.2 %collective-permute-start.1 = (f32[8,1,128]{2,1,0:T(1,128)S(1)}, f32[8,1,128]{2,1,0:T(1,128)S(1)}, u32[]{:S(2)}, u32[]{:S(2)}) collective-permute-start(f32[8,1,128]{2,1,0:T(1,128)S(1)} %get-tuple-element.101), channel_id=1, source_target_pairs={{32,0},{64,32},{96,64},{128,96},{160,128},{192,160},{224,192},{256... | collective-permute-start | bytes 12296 | tf_op jit(solution)/shard_map/ppermute | solution.py:25
  10.2 43.1 %collective-permute-start = (f32[8,1,128]{2,1,0:T(1,128)S(1)}, f32[8,1,128]{2,1,0:T(1,128)S(1)}, u32[]{:S(2)}, u32[]{:S(2)}) collective-permute-start(f32[8,1,128]{2,1,0:T(1,128)S(1)} %get-tuple-element.102), channel_id=1, source_target_pairs={{0,32},{32,64},{64,96},{96,128},{128,160},{160,192},{192,224},{224... | collective-permute-start | bytes 12296 | tf_op jit(solution)/shard_map/ppermute | solution.py:24
  26.8 60.6 %collective-permute-start.19 = (f32[4,1,64]{2,1,0:T(1,128)S(1)}, f32[4,1,64]{2,1,0:T(1,128)S(1)}, u32[]{:S(2)}, u32[]{:S(2)}) collective-permute-start(f32[4,1,64]{2,1,0:T(1,128)S(1)} %get-tuple-element.142), channel_id=1, source_target_pairs={{32,0},{64,32},{96,64},{128,96},{160,128},{192,160},{224,192},{256... | collective-permute-start | bytes 3080 | tf_op jit(solution)/shard_map/ppermute | solution.py:25
  29.2 58.2 %collective-permute-start.18 = (f32[4,1,64]{2,1,0:T(1,128)S(1)}, f32[4,1,64]{2,1,0:T(1,128)S(1)}, u32[]{:S(2)}, u32[]{:S(2)}) collective-permute-start(f32[4,1,64]{2,1,0:T(1,128)S(1)} %get-tuple-element.143), channel_id=1, source_target_pairs={{0,32},{32,64},{64,96},{96,128},{128,160},{160,192},{192,224},{224... | collective-permute-start | bytes 3080 | tf_op jit(solution)/shard_map/ppermute | solution.py:24
  33.7 42.1 %collective-permute-start.37 = (f32[2,1,32]{2,1,0:T(1,128)S(1)}, f32[2,1,32]{2,1,0:T(1,128)S(1)}, u32[]{:S(2)}, u32[]{:S(2)}) collective-permute-start(f32[2,1,32]{2,1,0:T(1,128)S(1)} %get-tuple-element.174), channel_id=1, source_target_pairs={{32,0},{64,32},{96,64},{128,96},{160,128},{192,160},{224,192},{256... | collective-permute-start | bytes 776 | tf_op jit(solution)/shard_map/ppermute | solution.py:25
  66.0 7.6 collective-permute-start.4
  70.1 7.9 collective-permute-start.36
  73.6 159.9 %collective-permute-start.56 = (f32[1,6,1]{2,1,0:T(8,128)S(1)}, f32[1,6,1]{2,1,0:T(8,128)S(1)}, u32[]{:S(2)}, u32[]{:S(2)}) collective-permute-start(f32[1,6,1]{2,1,0:T(8,128)S(1)} %get-tuple-element.206), channel_id=1, source_target_pairs={{0,8},{8,16},{16,24},{1,9},{9,17},{17,25},{2,10},{10,18},{18,26},{... | collective-permute-start | bytes 80 | tf_op jit(solution)/shard_map/ppermute | solution.py:24
  92.9 8.6 %collective-permute-start.10 = (f32[1,34,130]{2,1,0:T(8,128)S(1)}, f32[1,34,130]{2,1,0:T(8,128)S(1)}, u32[]{:S(2)}, u32[]{:S(2)}) collective-permute-start(f32[1,34,130]{2,1,0:T(8,128)S(1)} %get-tuple-element.75), channel_id=1, source_target_pairs={{0,1},{1,2},{2,3},{3,4},{4,5},{5,6},{6,7},{8,9},{9,10},{10,11},{11... | collective-permute-start | bytes 53048 | tf_op jit(solution)/shard_map/ppermute | solution.py:24
  98.3 11.3 %collective-permute-start.20 = (f32[4,18,1]{2,0,1:T(4,128)S(1)}, f32[4,18,1]{2,0,1:T(4,128)S(1)}, u32[]{:S(2)}, u32[]{:S(2)}) collective-permute-start(f32[4,18,1]{2,0,1:T(4,128)S(1)} %get-tuple-element.131), channel_id=1, source_target_pairs={{0,8},{8,16},{16,24},{1,9},{9,17},{17,25},{2,10},{10,18},{18,26},{... | collective-permute-start | bytes 872 | tf_op jit(solution)/shard_map/ppermute | solution.py:24
  100.3 9.4 %collective-permute-start.21 = (f32[4,18,1]{2,0,1:T(4,128)S(1)}, f32[4,18,1]{2,0,1:T(4,128)S(1)}, u32[]{:S(2)}, u32[]{:S(2)}) collective-permute-start(f32[4,18,1]{2,0,1:T(4,128)S(1)} %get-tuple-element.132), channel_id=1, source_target_pairs={{8,0},{16,8},{24,16},{9,1},{17,9},{25,17},{10,2},{18,10},{26,18},{... | collective-permute-start | bytes 872 | tf_op jit(solution)/shard_map/ppermute | solution.py:25
  112.7 10.8 %collective-permute-start.14 = (f32[8,34,1]{2,1,0:T(8,128)S(1)}, f32[8,34,1]{2,1,0:T(8,128)S(1)}, u32[]{:S(2)}, u32[]{:S(2)}) collective-permute-start(f32[8,34,1]{2,1,0:T(8,128)S(1)} %get-tuple-element.85), channel_id=1, source_target_pairs={{0,8},{8,16},{16,24},{1,9},{9,17},{17,25},{2,10},{10,18},{18,26},{... | collective-permute-start | bytes 3272 | tf_op jit(solution)/shard_map/ppermute | solution.py:24
  115.7 7.9 collective-permute-start.15
  117.0 13.4 %collective-permute-start.23 = (f32[1,18,66]{2,0,1:T(1,128)S(1)}, f32[1,18,66]{2,0,1:T(1,128)S(1)}, u32[]{:S(2)}, u32[]{:S(2)}) collective-permute-start(f32[1,18,66]{2,0,1:T(1,128)S(1)} %get-tuple-element.129), channel_id=1, source_target_pairs={{1,0},{2,1},{3,2},{4,3},{5,4},{6,5},{7,6},{9,8},{10,9},{11,10},{12... | collective-permute-start | bytes 14264 | tf_op jit(solution)/shard_map/ppermute | solution.py:25
  118.3 13.4 %collective-permute-start.22 = (f32[1,18,66]{2,0,1:T(1,128)S(1)}, f32[1,18,66]{2,0,1:T(1,128)S(1)}, u32[]{:S(2)}, u32[]{:S(2)}) collective-permute-start(f32[1,18,66]{2,0,1:T(1,128)S(1)} %get-tuple-element.130), channel_id=1, source_target_pairs={{0,1},{1,2},{2,3},{3,4},{4,5},{5,6},{6,7},{8,9},{9,10},{10,11},{11... | collective-permute-start | bytes 14264 | tf_op jit(solution)/shard_map/ppermute | solution.py:24
  123.7 8.0 collective-permute-start.16
  130.4 103.2 %collective-permute-start.57 = (f32[1,6,1]{2,1,0:T(8,128)S(1)}, f32[1,6,1]{2,1,0:T(8,128)S(1)}, u32[]{:S(2)}, u32[]{:S(2)}) collective-permute-start(f32[1,6,1]{2,1,0:T(8,128)S(1)} %get-tuple-element.207), channel_id=1, source_target_pairs={{8,0},{16,8},{24,16},{9,1},{17,9},{25,17},{10,2},{18,10},{26,18},{... | collective-permute-start | bytes 80 | tf_op jit(solution)/shard_map/ppermute | solution.py:25
  148.4 10.0 %collective-permute-start.24 = (f32[4,1,64]{2,1,0:T(1,128)S(1)}, f32[4,1,64]{2,1,0:T(1,128)S(1)}, u32[]{:S(2)}, u32[]{:S(2)}) collective-permute-start(f32[4,1,64]{2,1,0:T(1,128)S(1)} %get-tuple-element.140), channel_id=1, source_target_pairs={{0,32},{32,64},{64,96},{96,128},{128,160},{160,192},{192,224},{224... | collective-permute-start | bytes 3080 | tf_op jit(solution)/shard_map/ppermute | solution.py:24
  155.0 8.8 %collective-permute-start.38 = (f32[2,10,1]{2,1,0:T(8,128)S(1)}, f32[2,10,1]{2,1,0:T(8,128)S(1)}, u32[]{:S(2)}, u32[]{:S(2)}) collective-permute-start(f32[2,10,1]{2,1,0:T(8,128)S(1)} %get-tuple-element.162), channel_id=1, source_target_pairs={{0,8},{8,16},{16,24},{1,9},{9,17},{17,25},{2,10},{10,18},{18,26},{... | collective-permute-start | bytes 248 | tf_op jit(solution)/shard_map/ppermute | solution.py:24
  178.2 9.2 %collective-permute-start.30 = (f32[4,1,64]{2,1,0:T(1,128)S(1)}, f32[4,1,64]{2,1,0:T(1,128)S(1)}, u32[]{:S(2)}, u32[]{:S(2)}) collective-permute-start(f32[4,1,64]{2,1,0:T(1,128)S(1)} %get-tuple-element.137), channel_id=1, source_target_pairs={{0,32},{32,64},{64,96},{96,128},{128,160},{160,192},{192,224},{224... | collective-permute-start | bytes 3080 | tf_op jit(solution)/shard_map/ppermute | solution.py:24
  193.2 15.3 %collective-permute-start.41 = (f32[1,10,34]{2,1,0:T(8,128)S(1)}, f32[1,10,34]{2,1,0:T(8,128)S(1)}, u32[]{:S(2)}, u32[]{:S(2)}) collective-permute-start(f32[1,10,34]{2,1,0:T(8,128)S(1)} %get-tuple-element.160), channel_id=1, source_target_pairs={{1,0},{2,1},{3,2},{4,3},{5,4},{6,5},{7,6},{9,8},{10,9},{11,10},{12... | collective-permute-start | bytes 4088 | tf_op jit(solution)/shard_map/ppermute | solution.py:25
  208.7 8.2 collective-permute-start.42
  227.6 13.4 %collective-permute-start.46 = (f32[1,10,34]{2,1,0:T(8,128)S(1)}, f32[1,10,34]{2,1,0:T(8,128)S(1)}, u32[]{:S(2)}, u32[]{:S(2)}) collective-permute-start(f32[1,10,34]{2,1,0:T(8,128)S(1)} %get-tuple-element.156), channel_id=1, source_target_pairs={{0,1},{1,2},{2,3},{3,4},{4,5},{5,6},{6,7},{8,9},{9,10},{10,11},{11... | collective-permute-start | bytes 4088 | tf_op jit(solution)/shard_map/ppermute | solution.py:24
  232.2 8.8 %collective-permute-start.47 = (f32[1,10,34]{2,1,0:T(8,128)S(1)}, f32[1,10,34]{2,1,0:T(8,128)S(1)}, u32[]{:S(2)}, u32[]{:S(2)}) collective-permute-start(f32[1,10,34]{2,1,0:T(8,128)S(1)} %get-tuple-element.157), channel_id=1, source_target_pairs={{1,0},{2,1},{3,2},{4,3},{5,4},{6,5},{7,6},{9,8},{10,9},{11,10},{12... | collective-permute-start | bytes 4088 | tf_op jit(solution)/shard_map/ppermute | solution.py:25
  233.6 35.6 %collective-permute-start.59 = (f32[1,6,18]{2,1,0:T(8,128)S(1)}, f32[1,6,18]{2,1,0:T(8,128)S(1)}, u32[]{:S(2)}, u32[]{:S(2)}) collective-permute-start(f32[1,6,18]{2,1,0:T(8,128)S(1)} %pad_maximum_fusion.305), channel_id=1, source_target_pairs={{1,0},{2,1},{3,2},{4,3},{5,4},{6,5},{7,6},{9,8},{10,9},{11,10},{12... | collective-permute-start | bytes 1304 | tf_op jit(solution)/shard_map/ppermute | solution.py:25
  234.9 34.3 %collective-permute-start.58 = (f32[1,6,18]{2,1,0:T(8,128)S(1)}, f32[1,6,18]{2,1,0:T(8,128)S(1)}, u32[]{:S(2)}, u32[]{:S(2)}) collective-permute-start(f32[1,6,18]{2,1,0:T(8,128)S(1)} %pad_maximum_fusion.305), channel_id=1, source_target_pairs={{0,1},{1,2},{2,3},{3,4},{4,5},{5,6},{6,7},{8,9},{9,10},{10,11},{11... | collective-permute-start | bytes 1304 | tf_op jit(solution)/shard_map/ppermute | solution.py:24
  269.3 8.2 collective-permute-start.60
  365.1 7.4 collective-permute-start.84
  690.3 7.4 collective-permute-start.162
  742.9 7.9 collective-permute-start.174
  770.9 7.6 collective-permute-start.180
  798.4 7.6 collective-permute-start.186
  (164 other events, 969.5 us)
where the time goes:
time: 837 us; the launch traced here: 827 us
  starting transfers between devices  535 us (64%)
  waiting for transfers between devices  226 us (27%)
  local copies, waits for them, and re-layouts  38.2 us (5%)
  other arithmetic  22.9 us (3%)
    ppermute x96, starting transfers between devices, with_halo(): before = lax.ppermute(last, axis, up)  383 us
    ppermute x96, waiting for transfers between devices, with_halo(): after = lax.ppermute(first, axis, down)  211 us
    ppermute x96, starting transfers between devices, with_halo(): after = lax.ppermute(first, axis, down)  152 us
    reshape x4, local copies, waits for them, and re-layouts, restrict(): values.reshape(shape[0] // 2, 2, shape[1] // 2, 2, shape[2] // 2, 2)  31.2 us
  transfers between devices with their start and end apart: 192, of which 86 were waited for; matrix products, arithmetic and copies ran while one was open for 6% of the time, Pallas kernels for 0%

commit v1 on v0

v1 whole, which is shorter than its diff:
```python
import functools

import jax
import jax.numpy as jnp
from jax import lax
from jax.experimental import pallas as pl
from jax.experimental.pallas import tpu as pltpu
from jax.sharding import PartitionSpec as P

LEVELS = 4
SWEEPS = 2
BOTTOM = 16

smooth_low = 0.3
bottom_low = 0.05
upper_bound = 2.0
face_scale = 1.0 / 6.0

F32 = jnp.float32
AXES = ("gx", "gy", "gz")
DEEP = 5


def chebyshev(steps, lower):
    centre = (upper_bound + lower) / 2.0
    half_width = (upper_bound - lower) / 2.0
    sigma = centre / half_width
    rho = 1.0 / sigma
    out = [(0.0, 1.0 / centre)]
    for _ in range(1, steps):
        rho_next = 1.0 / (2.0 * sigma - rho)
        out.append((rho_next * rho, 2.0 * rho_next / half_width))
        rho = rho_next
    return out


(_, FIRST), (CARRY, GAIN) = chebyshev(SWEEPS, smooth_low)


def roll(value, shift, axis):
    shift %= value.shape[axis]
    return pltpu.roll(value, shift, axis) if shift else value


def lane_of(shape):
    return lax.broadcasted_iota(jnp.int32, shape, 1)


def row_of(shape):
    return lax.broadcasted_iota(jnp.int32, shape, 0)


def sides(value):
    return [roll(value, 1, 0), roll(value, -1, 0), roll(value, 1, 1), roll(value, -1, 1)]


def scale_of(level):
    return face_scale * 0.25**level * 0.5


def coefficients(beta, below, above, acoef, level):
    weights = [scale_of(level) * (beta + other) for other in [below, above] + sides(beta)]
    diagonal = acoef
    for weight in weights:
        diagonal = diagonal + weight
    inside = beta > 0.0
    inverse = jnp.where(inside, 1.0 / jnp.where(inside, diagonal, 1.0), 0.0)
    return [weight * inverse for weight in weights], diagonal, inverse


def defect(scaled, weights, value, below, above):
    result = scaled - value
    for weight, other in zip(weights, [below, above] + sides(value)):
        result = result + weight * other
    return result


def dot(left, right):
    return jnp.dot(left, right, precision=lax.Precision.HIGHEST, preferred_element_type=F32)


def matrix(shape, rule, value=1.0):
    return jnp.where(rule(row_of(shape), lane_of(shape)), value, 0.0).astype(F32)


def copies(ref, value):
    for index in range(ref.shape[0]):
        ref[index] = value


def pack0(pos, f_ref, a_ref, b_ref, zb, za, xb, xa, whole, left, right):
    planes = f_ref.shape[0]
    has_before, has_after = pos[0] > 0, pos[0] < pos[3] - 1
    for index, ref in enumerate((f_ref, a_ref, b_ref)):
        whole[index, 0:DEEP, 0:32, :] = zb[index]
        whole[index, DEEP : DEEP + planes, 0:32, :] = ref[...]
        whole[index, DEEP + planes :, 0:32, :] = za[index]
        whole[index, :, 32:40, :] = jnp.where(has_after, xa[index], 0.0)
        whole[index, :, 40:48, :] = jnp.where(has_before, xb[index], 0.0)
    depth = planes + 2 * DEEP
    slot = lane_of((48, 128)) // 8
    for tile in range(left.shape[0]):
        low = high = jnp.zeros((48, 128), F32)
        for place in range(min(16, 3 * depth - 16 * tile)):
            index, plane = divmod(16 * tile + place, depth)
            value = whole[index, plane]
            low = jnp.where(slot == place, roll(value, 8 * place, 1), low)
            high = jnp.where(slot == place, roll(value, 8 * place + 8, 1), high)
        left[tile] = low
        right[tile] = high


def unpack0(whole, before, after, ext):
    depth = whole.shape[1]
    lane = lane_of((48, 128))
    for index in range(3):
        for plane in range(depth):
            tile, place = divmod(index * depth + plane, 16)
            ahead = jnp.where(lane < 8, roll(after[tile], -8 * place, 1), 0.0)
            ext[index, plane, :, 0:128] = whole[index, plane]
            ext[index, plane, :, 128:256] = jnp.where(lane >= 120, roll(before[tile], 120 - 8 * place, 1), ahead)


def prepare0(ext, weights, diagonal, scaled):
    @pl.loop(0, diagonal.shape[0])
    def _(plane):
        got, middle, inverse = coefficients(
            ext[2, plane + 1], ext[2, plane], ext[2, plane + 2], ext[1, plane + 1], 0
        )
        for index in range(6):
            weights[index, plane] = got[index]
        diagonal[plane] = middle
        scaled[plane] = ext[0, plane + 1] * inverse


def residual0(weights, diagonal, scaled, value, below, above, at):
    cut = lambda array: array[0:32, 0:128]
    result = scaled[at, 0:32, 0:128] - cut(value)
    for index, other in enumerate([below, above] + sides(value)):
        result = result + weights[index, at, 0:32, 0:128] * cut(other)
    return diagonal[at, 0:32, 0:128] * result


def down0(whole, before, after, iterate, message, ext, weights, diagonal, scaled, start, sums):
    unpack0(whole, before, after, ext)
    prepare0(ext, weights, diagonal, scaled)

    @pl.loop(0, start.shape[0])
    def _(plane):
        start[plane] = FIRST * scaled[plane]

    @pl.loop(0, iterate.shape[0])
    def _(plane):
        value = start[plane + 1]
        got = defect(
            scaled[plane + 1],
            [weights[index, plane + 1] for index in range(6)],
            value,
            start[plane],
            start[plane + 2],
        )
        iterate[plane] = value + (CARRY * value + GAIN * got)

    planes = whole.shape[1] - 2 * DEEP

    def left_over(plane):
        return residual0(
            weights, diagonal, scaled, iterate[plane + 3], iterate[plane + 2], iterate[plane + 4], plane + 4
        )

    half = planes // 2

    @pl.loop(0, half)
    def _(plane):
        sums[plane] = left_over(2 * plane) + left_over(2 * plane + 1)
        for index in (1, 2):
            low = whole[index, DEEP + 2 * plane, 0:32, :]
            sums[index * half + plane] = low + whole[index, DEEP + 2 * plane + 1, 0:32, :]

    count = 3 * half
    tall = [sums[plane, pl.ds(0, 16, stride=2), :] + sums[plane, pl.ds(1, 16, stride=2), :] for plane in range(count)]
    first = jnp.concatenate([value[0:8] for value in tall], axis=0)
    second = jnp.concatenate([value[8:16] for value in tall], axis=0)
    pair = matrix((128, 128), lambda row, lane: lane == row // 2, 0.125)
    other = matrix((128, 128), lambda row, lane: lane == row // 2 + 64, 0.125)
    copies(message, dot(first, pair) + dot(second, other))


def pack1(pos, own, xb, xa, whole, left, right):
    has_before, has_after = pos[0] > 0, pos[0] < pos[3] - 1
    lane = lane_of((8, 128))
    sources, rows = own.shape[0], own.shape[1]
    per = rows // 24
    depth = sources * per

    def spread(value):
        return jnp.where(lane < 64, value, 0.0), jnp.where(lane < 64, roll(value, 64, 1), 0.0)

    @pl.loop(0, sources)
    def _(source):
        for index in range(3):
            for plane in range(per):
                at = (index * per + plane) * 8
                to = index * depth + source * per + plane
                whole[to, 0:8, :], whole[to, 8:16, :] = spread(own[source, at : at + 8, :])
                value = jnp.where(has_after, xa[source, at : at + 8, :], 0.0)
                whole[to, 16:24, :], whole[to, 24:32, :] = spread(value)
                value = jnp.where(has_before, xb[source, at : at + 8, :], 0.0)
                whole[to, 32:40, :], whole[to, 40:48, :] = spread(value)

    slot = lane_of((48, 128)) // 16

    @pl.loop(0, left.shape[0])
    def _(tile):
        low = high = jnp.zeros((48, 128), F32)
        for place in range(8):
            value = whole[8 * tile + place]
            low = jnp.where(slot == place, roll(value, 16 * place, 1), low)
            high = jnp.where(slot == place, roll(value, 16 * place - 48, 1), high)
        left[tile] = low
        right[tile] = high


def pass_all(weights, scaled, value, out, count, combine):
    @pl.loop(0, count)
    def _(plane):
        middle = value[plane + 1]
        got = defect(
            scaled[plane],
            [weights[index, plane] for index in range(6)],
            middle,
            value[plane],
            value[plane + 2],
        )
        out(plane, combine(middle, got))


def prepare(ext, weights, diagonal, scaled, level, offset):
    @pl.loop(0, diagonal.shape[0])
    def _(plane):
        at = plane + offset
        got, middle, inverse = coefficients(ext[2, at], ext[2, at - 1], ext[2, at + 1], ext[1, at], level)
        for index in range(6):
            weights[index, plane] = got[index]
        diagonal[plane] = middle
        scaled[plane] = ext[0, at] * inverse


def down1(
    pos, whole, before, after, window1, window2, message,
    ext1, weights1, diagonal1, scaled1, start1, iterate1, sums1,
    ext2, weights2, diagonal2, scaled2, start2, iterate2, sums2, thin, thick,
):
    depth = whole.shape[0] // 3
    lane = lane_of((48, 128))
    for index in range(3):
        for end in (0, depth + 4):
            for plane in range(4):
                ext1[index, end + plane] = jnp.zeros((48, 128), F32)

    @pl.loop(0, before.shape[0])
    def _(tile):
        for place in range(8):
            at = 8 * tile + place
            index, plane = at // depth, lax.rem(at, depth)
            value = whole[at]
            value = jnp.where((lane >= 64) & (lane < 80), roll(after[tile], 64 - 16 * place, 1), value)
            value = jnp.where(lane >= 112, roll(before[tile], 112 - 16 * place, 1), value)
            ext1[index, plane + 4] = value

    prepare(ext1, weights1, diagonal1, scaled1, 1, 4)
    start1[0] = jnp.zeros((48, 128), F32)
    start1[depth + 1] = jnp.zeros((48, 128), F32)

    @pl.loop(0, depth)
    def _(plane):
        start1[plane + 1] = FIRST * scaled1[plane]

    for end in (0, depth + 4):
        for plane in range(4):
            iterate1[end + plane] = jnp.zeros((48, 128), F32)

    def put1(plane, value):
        iterate1[plane + 4] = value

    pass_all(weights1, scaled1, start1, put1, depth, lambda value, got: value + (CARRY * value + GAIN * got))

    half = depth // 2

    @pl.loop(0, half)
    def _(pair):
        total = None
        for plane in (2 * pair, 2 * pair + 1):
            got = diagonal1[plane] * defect(
                scaled1[plane],
                [weights1[index, plane] for index in range(6)],
                iterate1[plane + 4],
                iterate1[plane + 3],
                iterate1[plane + 5],
            )
            total = got if total is None else total + got
        sums1[pair] = total
        for index in (1, 2):
            sums1[index * half + pair] = ext1[index, 2 * pair + 4] + ext1[index, 2 * pair + 5]

    @pl.loop(0, 3 * half)
    def _(plane):
        thin[plane] = sums1[plane, pl.ds(0, 24, stride=2), :] + sums1[plane, pl.ds(1, 24, stride=2), :]

    def to_level2(row, lane):
        place = jnp.where(lane < 64, lane, lane - 128)
        source = lax.shift_right_arithmetic(jnp.where(row < 96, row, row - 128), 1)
        return (source == place) & ((row < 80) | (row >= 112))

    level2 = matrix((128, 128), to_level2, 0.125)
    for index in range(3):
        values = thin[index * half : (index + 1) * half].reshape(half * 24, 128)
        ext2[index, 4 : 4 + half] = dot(values, level2).reshape(half, 24, 128)
        for end in (0, half + 4):
            for plane in range(4):
                ext2[index, end + plane] = jnp.zeros((24, 128), F32)

    prepare(ext2, weights2, diagonal2, scaled2, 2, 4)
    start2[0] = jnp.zeros((24, 128), F32)
    start2[half + 1] = jnp.zeros((24, 128), F32)

    @pl.loop(0, half)
    def _(plane):
        start2[plane + 1] = FIRST * scaled2[plane]

    for end in (0, half + 4):
        for plane in range(4):
            iterate2[end + plane] = jnp.zeros((24, 128), F32)

    def put2(plane, value):
        iterate2[plane + 4] = value

    pass_all(weights2, scaled2, start2, put2, half, lambda value, got: value + (CARRY * value + GAIN * got))

    quarter = half // 2
    group = quarter // 2
    place2 = [
        matrix((128, 128), lambda row, lane, at=at: (row < 32) & (lane == row // 2 + 16 * at), 0.125)
        for at in range(6)
    ]
    for index in range(3):
        for plane in range(quarter):
            if index == 0:
                total = None
                for at in (2 * plane, 2 * plane + 1):
                    got = diagonal2[at] * defect(
                        scaled2[at],
                        [weights2[face, at] for face in range(6)],
                        iterate2[at + 4],
                        iterate2[at + 3],
                        iterate2[at + 5],
                    )
                    total = got if total is None else total + got
                total = total[0:8]
            else:
                total = ext2[index, 2 * plane + 4, 0:8, :] + ext2[index, 2 * plane + 5, 0:8, :]
            at = index * quarter + plane
            sums2[at] = total
            side, within = divmod(plane, group)
            thick[index * 2 + side, pl.ds(within, 4, stride=group), :] = (
                sums2[at, pl.ds(0, 4, stride=2), :] + sums2[at, pl.ds(1, 4, stride=2), :]
            )
    result = dot(thick[0], place2[0])
    for at in range(1, 6):
        result = result + dot(thick[at], place2[at])
    copies(message, result)

    at1, at2 = pos[2] * 4, pos[2] * 2
    for index in range(3):
        window1[index] = ext1[index, pl.ds(at1, 12)]
        window2[index] = ext2[index, pl.ds(at2, 10)]
    window1[3] = iterate1[pl.ds(at1, 12)]
    window2[3] = iterate2[pl.ds(at2, 10)]


def bottom(gathered, whole, weights, scaled, update, values):
    group = weights.shape[1]
    rows = weights.shape[2]
    for index in range(3):
        total = None
        lane = lane_of(gathered.shape[1:])
        for source in range(4):
            value = gathered[source]
            for side in range(2):
                to = 64 * side + 16 * source
                moved = roll(value, to - 16 * (2 * index + side), 1)
                moved = jnp.where((lane >= to) & (lane < to + 16), moved, 0.0)
                total = moved if total is None else total + moved
        whole[index] = total
    shape = (rows, 128)
    row, lane = row_of(shape), lane_of(shape)
    column = lax.rem(lane, 64)

    def plane_at(index, plane):
        return whole[index, pl.ds(plane, rows, stride=group), :]

    def around(get, plane):
        middle = get(plane)
        below = get(plane - 1) if plane else roll(get(group - 1), 64, 1)
        above = get(plane + 1) if plane < group - 1 else roll(get(0), 64, 1)
        return [below, above] + sides(middle)

    for plane in range(group):
        beta = plane_at(2, plane)
        masks = [
            (lane >= 64) if plane == 0 else None,
            (lane < 64) if plane == group - 1 else None,
            row > 0,
            row < rows - 1,
            column > 0,
            column < 63,
        ]
        near = around(lambda at: plane_at(2, at), plane)
        near = [other if mask is None else jnp.where(mask, other, 0.0) for other, mask in zip(near, masks)]
        faces = [scale_of(3) * (beta + other) for other in near]
        diagonal = plane_at(1, plane)
        for face in faces:
            diagonal = diagonal + face
        inverse = 1.0 / diagonal
        for index, (face, mask) in enumerate(zip(faces, masks)):
            face = face * inverse
            weights[index, plane] = face if mask is None else jnp.where(mask, face, 0.0)
        scaled[plane] = plane_at(0, plane) * inverse

    steps = chebyshev(BOTTOM, bottom_low)
    for plane in range(group):
        value = steps[0][1] * scaled[plane]
        update[plane] = value
        values[0, plane] = value
    for step, (carry, gain) in enumerate(steps[1:]):
        now, later = step % 2, (step + 1) % 2
        for plane in range(group):
            middle = values[now, plane]
            got = scaled[plane] - middle
            for index, other in enumerate(around(lambda at: values[now, at], plane)):
                got = got + weights[index, plane] * other
            moved = carry * update[plane] + gain * got
            update[plane] = moved
            values[later, plane] = middle + moved


def finish(ext, iterate, weights, diagonal, scaled, level, update, middle, put):
    count = iterate.shape[0]
    prepare(ext, weights, diagonal, scaled, level, 1)

    @pl.loop(0, count - 2)
    def _(plane):
        value = iterate[plane + 1]
        got = FIRST * defect(
            scaled[plane],
            [weights[index, plane] for index in range(6)],
            value,
            iterate[plane],
            iterate[plane + 2],
        )
        update[plane] = got
        middle[plane] = value + got

    @pl.loop(0, count - 4)
    def _(plane):
        value = middle[plane + 1]
        got = defect(
            scaled[plane + 1],
            [weights[index, plane + 1] for index in range(6)],
            value,
            middle[plane],
            middle[plane + 2],
        )
        put(plane, value + (CARRY * update[plane + 1] + GAIN * got))


def up(
    pos, gathered, window2, window1, whole0, before0, after0, iterate0, solved, left_over,
    whole3, weights3, scaled3, update3, values3,
    error2, value2, weights2, diagonal2, scaled2, update2, middle2, out2,
    tall1, value1, weights1, diagonal1, scaled1, update1, middle1, out1,
    tall0, ext0, value0, weights0, diagonal0, scaled0, update0, middle0, out0,
):
    bottom(gathered, whole3, weights3, scaled3, update3, values3)
    group, rows = weights3.shape[1], weights3.shape[2]
    at_x, at_y, at_z = 4 * pos[0], 16 * pos[1], pos[2]
    last = (BOTTOM - 1) % 2

    def rows_rule(row, lane):
        place = jnp.where(row < 16, row, row - 24)
        return lane == at_x + lax.shift_right_arithmetic(place, 1)

    pick = matrix((24, rows), rows_rule)
    for plane in range(group):
        got = dot(pick, values3[last, plane])
        for side in range(2):

            def lanes_rule(row, lane, side=side):
                place = jnp.where(lane < 64, lane, lane - 128)
                source = at_y + lax.shift_right_arithmetic(place, 1)
                return (row - 64 * side == source) & (source >= 0) & (source < 64) & ((lane < 40) | (lane >= 120))

            error2[side * group + plane + 2] = dot(got, matrix((128, 128), lanes_rule))
    for end in (0, 2 * group + 2):
        for plane in range(2):
            error2[end + plane] = jnp.zeros((24, 128), F32)

    for plane in range(10):
        value2[plane] = window2[3, plane] + error2[at_z + plane // 2]

    def put2(plane, value):
        out2[plane] = value

    finish(window2, value2, weights2, diagonal2, scaled2, 2, update2, middle2, put2)

    def to_level1(row, lane):
        place = jnp.where(lane < 96, lane, lane - 128)
        source = lax.shift_right_arithmetic(place, 1)
        return (jnp.where(row < 64, row, row - 128) == source) & ((lane < 80) | (lane >= 112))

    wide1 = matrix((128, 128), to_level1)
    for plane in range(6):
        tall1[plane, pl.ds(0, 24, stride=2), :] = out2[plane]
        tall1[plane, pl.ds(1, 24, stride=2), :] = out2[plane]
    spread = dot(tall1[...].reshape(6 * 48, 128), wide1).reshape(6, 48, 128)
    for plane in range(12):
        value1[plane] = window1[3, plane] + spread[plane // 2]

    def put1(plane, value):
        out1[plane] = value

    finish(window1, value1, weights1, diagonal1, scaled1, 1, update1, middle1, put1)

    def to_level0(row, lane):
        place = jnp.where(lane < 192, lane, lane - 256)
        source = lax.shift_right_arithmetic(place, 1)
        return (jnp.where(row < 96, row, row - 128) == source) & ((lane < 136) | (lane >= 248))

    wide0 = matrix((128, 256), to_level0)
    for plane in range(8):
        value = out1[plane]
        tall0[plane, pl.ds(0, 24, stride=2), :] = value[0:24]
        tall0[plane, pl.ds(1, 24, stride=2), :] = value[0:24]
        tall0[plane, pl.ds(40, 4, stride=2), :] = value[44:48]
        tall0[plane, pl.ds(41, 4, stride=2), :] = value[44:48]

    @pl.loop(0, 8)
    def _(plane):
        value = dot(tall0[plane], wide0)
        out0[2 * plane] = value
        out0[2 * plane + 1] = value

    @pl.loop(0, iterate0.shape[0])
    def _(plane):
        value0[plane] = iterate0[plane] + out0[plane + 1]

    unpack0(whole0, before0, after0, ext0)
    prepare0(ext0, weights0, diagonal0, scaled0)
    count = iterate0.shape[0]

    @pl.loop(0, count - 2)
    def _(plane):
        value = value0[plane + 1]
        got = FIRST * defect(
            scaled0[plane + 2],
            [weights0[index, plane + 2] for index in range(6)],
            value,
            value0[plane],
            value0[plane + 2],
        )
        update0[plane] = got
        middle0[plane] = value + got

    @pl.loop(0, count - 4)
    def _(plane):
        value = middle0[plane + 1]
        got = defect(
            scaled0[plane + 3],
            [weights0[index, plane + 3] for index in range(6)],
            value,
            middle0[plane],
            middle0[plane + 2],
        )
        out0[plane] = value + (CARRY * update0[plane + 1] + GAIN * got)

    @pl.loop(0, count - 6)
    def _(plane):
        value = out0[plane + 1]
        solved[plane] = value[0:32, 0:128]
        left_over[plane] = residual0(
            weights0, diagonal0, scaled0, value, out0[plane], out0[plane + 2], plane + 4
        )


def call(body, name, outs, scratch, pos, args):
    vmem = pl.BlockSpec(memory_space=pltpu.VMEM)
    smem = [pl.BlockSpec(memory_space=pltpu.SMEM)] if pos is not None else []
    operands = ([pos] if pos is not None else []) + list(args)
    return pl.pallas_call(
        body,
        name=name,
        out_shape=[jax.ShapeDtypeStruct(shape, F32) for shape in outs],
        in_specs=smem + [vmem] * len(args),
        out_specs=[vmem] * len(outs),
        scratch_shapes=[pltpu.VMEM(shape, F32) for shape in scratch],
        compiler_params=pltpu.CompilerParams(vmem_limit_bytes=40 * 2**20),
    )(*operands)


def exchange(up_values, down_values, axis, ring):
    peers = lax.axis_size(axis)
    up_pairs = [(i, (i + 1) % peers) for i in range(peers if ring else peers - 1)]
    down_pairs = [(j, i) for i, j in up_pairs]
    return lax.ppermute(up_values, axis, up_pairs), lax.ppermute(down_values, axis, down_pairs)


def coefficient_scratch(planes, rows, lanes):
    shape = (planes, rows, lanes)
    return [(6,) + shape, shape, shape]


def on_device(right_side, acoef, beta):
    ranks, turns, files = [lax.axis_size(axis) for axis in AXES]
    pos = jnp.stack([lax.axis_index(axis) for axis in AXES] + [jnp.int32(ranks)]).astype(jnp.int32)
    planes = right_side.shape[0]
    arrays = (right_side, acoef, beta)

    last = jnp.stack([value[planes - DEEP :] for value in arrays])
    first = jnp.stack([value[:DEEP] for value in arrays])
    zb, za = exchange(last, first, "gz", False)
    last = jnp.stack([jnp.concatenate([zb[i, :, 24:], arrays[i][:, 24:], za[i, :, 24:]]) for i in range(3)])
    first = jnp.stack([jnp.concatenate([zb[i, :, :8], arrays[i][:, :8], za[i, :, :8]]) for i in range(3)])
    xb, xa = exchange(last, first, "gx", True)
    depth = planes + 2 * DEEP
    tiles = -(-3 * depth // 16)
    whole0, left, right = call(
        pack0, "pack0", [(3, depth, 48, 128)] + [(tiles, 48, 128)] * 2, [], pos, arrays + (zb, za, xb, xa)
    )
    before0, after0 = exchange(right, left, "gy", False)
    plane0 = (48, 256)
    half = planes // 2
    iterate0, message = call(
        down0,
        "down0",
        [(depth - 4,) + plane0, (files, 3 * half * 8, 128)],
        [(3, depth) + plane0] + coefficient_scratch(depth - 2, *plane0) + [(depth - 2,) + plane0, (3 * half, 32, 128)],
        None,
        (whole0, before0, after0),
    )

    own = lax.all_to_all(message, "gz", 0, 0)
    xb, xa = exchange(own, own, "gx", True)
    depth1 = files * half
    tiles = 3 * depth1 // 8
    whole1, left, right = call(
        pack1, "pack1", [(3 * depth1, 48, 128)] + [(tiles, 48, 128)] * 2, [], pos, (own, xb, xa)
    )
    before1, after1 = exchange(right, left, "gy", False)
    plane1, plane2 = (48, 128), (24, 128)
    depth2 = depth1 // 2
    group = depth2 // 4
    window1, window2, message = call(
        down1,
        "down1",
        [(4, 12) + plane1, (4, 10) + plane2, (ranks, 4 * group, 128)],
        [(3, depth1 + 8) + plane1]
        + coefficient_scratch(depth1, *plane1)
        + [(depth1 + 2,) + plane1, (depth1 + 8,) + plane1, (3 * depth2,) + plane1, (3, depth2 + 8) + plane2]
        + coefficient_scratch(depth2, *plane2)
        + [(depth2 + 2,) + plane2, (depth2 + 8,) + plane2, (3 * depth2 // 2, 8, 128)]
        + [(3 * depth2,) + plane2, (6, 4 * group, 128)],
        pos,
        (whole1, before1, after1),
    )

    gathered = lax.all_to_all(message, "gx", 0, 0)
    gathered = gathered.reshape(1, ranks * 4 * group, 128)
    gathered = jnp.broadcast_to(gathered, (turns,) + gathered.shape[1:])
    gathered = lax.all_to_all(gathered, "gy", 0, 0)

    rows3 = 4 * ranks
    plane3 = (rows3, 128)
    solved, left_over = call(
        up,
        "up",
        [right_side.shape, right_side.shape],
        [(3, rows3 * group, 128), (6, group) + plane3, (group,) + plane3, (group,) + plane3, (2, group) + plane3]
        + [(2 * group + 4,) + plane2, (10,) + plane2]
        + coefficient_scratch(8, *plane2)
        + [(8,) + plane2, (8,) + plane2, (6,) + plane2, (6,) + plane1, (12,) + plane1]
        + coefficient_scratch(10, *plane1)
        + [(10,) + plane1, (10,) + plane1, (8,) + plane1, (8,) + plane1]
        + [(3, depth) + plane0, (depth - 4,) + plane0]
        + coefficient_scratch(depth - 2, *plane0)
        + [(depth - 6,) + plane0, (depth - 6,) + plane0, (depth - 2,) + plane0],
        pos,
        (gathered, window2, window1, whole0, before0, after0, iterate0),
    )
    return solved, left_over


def solution(mesh):
    spec = P("gz", "gx", "gy")
    return jax.shard_map(
        on_device, mesh=mesh, in_specs=(spec, spec, spec), out_specs=(spec, spec), check_vma=False
    )
```

time: 837 us -> 149 us (0.18); the launches traced: 827 us -> 148 us
  starting transfers between devices: 535 us -> 22.8 us
  waiting for transfers between devices: 226 us -> 28.2 us
  blocking collectives: 0 us -> 53.3 us
  Pallas kernels: 0 us -> 40.7 us
  local copies, waits for them, and re-layouts: 38.2 us -> 2.14 us
  other arithmetic: 22.9 us -> 0.19 us
    ppermute x192 -> x10, starting transfers between devices: 535 us -> 22.8 us  [the longest x5 16.6 us: exchange(): lax.ppermute(up_values, axis, up_pairs)]
    ppermute x192 -> x10, waiting for transfers between devices: 226 us -> 28.2 us  [the longest x5 20.5 us: exchange(): lax.ppermute(down_values, axis, down_pairs)]
    all_to_all x0 -> x3, blocking collectives: none -> 53.3 us  [the longest x1 21.8 us: on_device(): own = lax.all_to_all(message, 'gz', 0, 0)]
    pallas_call x0 -> x5, Pallas kernels: none -> 40.7 us  [call(): pl.pallas_call(body, name=name, out_shape=[jax.ShapeDtypeStruct(shape, F3...]
    reshape x8 -> x0, local copies, waits for them, and re-layouts: 31.7 us -> none  [the longest x4 31.2 us: restrict(): values.reshape(shape[0] // 2, 2, shape[1] // 2, 2, shape[2] // 2, 2)]
    reduce_sum x12 -> x0, other arithmetic: 12.9 us -> none  [restrict(): values.reshape(shape[0] // 2, 2, shape[1] // 2, 2, shape[2] // 2, 2)]
  transfers between devices with their start and end apart: 192 -> 10, of which waited for: 86 -> 9; matrix products, arithmetic and copies ran while one was open for 6% -> 0% of each run, Pallas kernels for 0% -> 0%
where the time goes in v1:
time: 149 us; the launch traced here: 148 us
  blocking collectives  53.3 us (36%)
  Pallas kernels  40.7 us (27%)
  waiting for transfers between devices  28.2 us (19%)
  starting transfers between devices  22.8 us (15%)
  local copies, waits for them, and re-layouts  2.14 us (1%)
    pallas_call x5, Pallas kernels, call(): pl.pallas_call(body, name=name, out_shape=[jax.ShapeDtypeStruct(shape, F3...  40.7 us
    all_to_all x1, blocking collectives, on_device(): own = lax.all_to_all(message, 'gz', 0, 0)  21.8 us
    ppermute x5, waiting for transfers between devices, exchange(): lax.ppermute(down_values, axis, down_pairs)  20.5 us
    all_to_all x1, blocking collectives, on_device(): gathered = lax.all_to_all(message, 'gx', 0, 0)  19.2 us
    ppermute x5, starting transfers between devices, exchange(): lax.ppermute(up_values, axis, up_pairs)  16.6 us
    all_to_all x1, blocking collectives, on_device(): gathered = lax.all_to_all(gathered, 'gy', 0, 0)  12.3 us
    ppermute x5, waiting for transfers between devices, exchange(): lax.ppermute(up_values, axis, up_pairs)  7.7 us
    ppermute x5, starting transfers between devices, exchange(): lax.ppermute(down_values, axis, down_pairs)  6.29 us
  transfers between devices with their start and end apart: 10, of which 9 were waited for; matrix products, arithmetic and copies ran while one was open for 0% of the time, Pallas kernels for 0%

profile of v1, /device:TPU:1, one launch (start us, length us, event | category | flops | bytes accessed | tf_op | source)
XLA Modules:
  0.0 148.3 jit_solution(4617409784080048531)
XLA Ops:
  0.6 0.0 copy-start.1
  0.7 0.0 copy-start
  0.7 1.0 slice_bitcast_fusion.2
  1.7 1.0 slice_bitcast_fusion
  2.7 4.8 %collective-permute-start = (f32[3,5,32,128]{3,2,1,0:T(8,128)S(1)}, f32[3,5,32,128]{3,2,1,0:T(8,128)S(1)}, u32[]{:S(2)}, u32[]{:S(2)}) collective-permute-start(f32[3,5,32,128]{3,2,1,0:T(8,128)S(1)} %pad_maximum_fusion), channel_id=1, source_target_pairs={{0,1},{1,2},{2,3},{3,4},{4,5},{5,6},{6,7},{8,9},{9,10},{10,11},{11... | collective-permute-start | bytes 737288 | tf_op jit(solution)/shard_map/ppermute | solution.py:614
  7.6 1.3 collective-permute-start.1
  9.0 1.7 %collective-permute-done.zb = f32[3,5,32,128]{3,2,1,0:T(8,128)S(1)} collective-permute-done((f32[3,5,32,128]{3,2,1,0:T(8,128)S(1)}, f32[3,5,32,128]{3,2,1,0:T(8,128)S(1)}, u32[]{:S(2)}, u32[]{:S(2)}) %collective-permute-start) | collective-permute-done | bytes 245792 | tf_op jit(solution)/shard_map/ppermute | solution.py:614
  10.7 4.5 %collective-permute-done.1.za = f32[3,5,32,128]{3,2,1,0:T(8,128)S(1)} collective-permute-done((f32[3,5,32,128]{3,2,1,0:T(8,128)S(1)}, f32[3,5,32,128]{3,2,1,0:T(8,128)S(1)}, u32[]{:S(2)}, u32[]{:S(2)}) %collective-permute-start.1) | collective-permute-done | bytes 245792 | tf_op jit(solution)/shard_map/ppermute | solution.py:614
  15.3 4.5 %collective-permute-start.2 = (f32[3,18,8,128]{3,2,1,0:T(8,128)S(1)}, f32[3,18,8,128]{3,2,1,0:T(8,128)S(1)}, u32[]{:S(2)}, u32[]{:S(2)}) collective-permute-start(f32[3,18,8,128]{3,2,1,0:T(8,128)S(1)} %pad_maximum_fusion.2), channel_id=1, source_target_pairs={{0,32},{32,64},{64,96},{96,128},{128,160},{160,192},{192,224},{224... | collective-permute-start | bytes 663560 | tf_op jit(solution)/shard_map/ppermute | solution.py:614
  19.8 0.0 collective-permute-start.3
  19.9 0.1 pad_add_fusion.pos
  20.0 2.7 %collective-permute-done.2.xb = f32[3,18,8,128]{3,2,1,0:T(8,128)S(1)} collective-permute-done((f32[3,18,8,128]{3,2,1,0:T(8,128)S(1)}, f32[3,18,8,128]{3,2,1,0:T(8,128)S(1)}, u32[]{:S(2)}, u32[]{:S(2)}) %collective-permute-start.2) | collective-permute-done | bytes 221216 | tf_op jit(solution)/shard_map/ppermute | solution.py:614
  22.7 2.7 %collective-permute-done.3.xa = f32[3,18,8,128]{3,2,1,0:T(8,128)S(1)} collective-permute-done((f32[3,18,8,128]{3,2,1,0:T(8,128)S(1)}, f32[3,18,8,128]{3,2,1,0:T(8,128)S(1)}, u32[]{:S(2)}, u32[]{:S(2)}) %collective-permute-start.3) | collective-permute-done | bytes 221216 | tf_op jit(solution)/shard_map/ppermute | solution.py:614
  25.3 1.3 pack0.1
  26.6 3.0 %collective-permute-start.4 = (f32[4,48,128]{2,1,0:T(8,128)S(1)}, f32[4,48,128]{2,1,0:T(8,128)S(1)}, u32[]{:S(2)}, u32[]{:S(2)}) collective-permute-start(f32[4,48,128]{2,1,0:T(8,128)S(1)} %get-tuple-element.14), channel_id=1, source_target_pairs={{0,8},{8,16},{16,24},{1,9},{9,17},{17,25},{2,10},{10,18},{18,26},{... | collective-permute-start | bytes 294920 | tf_op jit(solution)/shard_map/ppermute | solution.py:614
  29.6 1.3 collective-permute-start.5
  30.9 0.9 collective-permute-done.4.before.before0
  31.9 3.8 %collective-permute-done.5.after.after0 = f32[4,48,128]{2,1,0:T(8,128)S(1)} collective-permute-done((f32[4,48,128]{2,1,0:T(8,128)S(1)}, f32[4,48,128]{2,1,0:T(8,128)S(1)}, u32[]{:S(2)}, u32[]{:S(2)}) %collective-permute-start.5) | collective-permute-done | bytes 98336 | tf_op jit(solution)/shard_map/ppermute | solution.py:614
  35.6 5.1 %down0.1 = (f32[14,48,256]{2,1,0:T(8,128)S(1)}, f32[8,96,128]{2,1,0:T(8,128)S(1)}) custom-call(f32[3,18,48,128]{3,2,1,0:T(8,128)S(1)} %get-tuple-element.13.whole.whole0, f32[4,48,128]{2,1,0:T(8,128)S(1)} %collective-permute-done.4.before.before0, f32[4,48,128]{2,1,0:T(8,128)S(1)} %collective-permute-done.5.after.after0), custom_call_target="tpu_custom_call" | custom-call | tf_op jit(solution)/shard_map/down0/pallas_call | solution.py:599
  40.7 21.8 %all_to_all.15.own = f32[8,96,128]{2,1,0:T(8,128)S(1)} all-to-all(f32[8,96,128]{2,1,0:T(8,128)S(1)} %get-tuple-element.16), channel_id=1, replica_groups=mesh['gx'=16,'gy'=4,'gz'=8] {'gz'}, dimensions={0} | all-to-all | bytes 786432 | tf_op jit(solution)/shard_map/all_to_all | solution.py:651
  62.5 2.4 %collective-permute-start.7 = (f32[8,96,128]{2,1,0:T(8,128)S(1)}, f32[8,96,128]{2,1,0:T(8,128)S(1)}, u32[]{:S(2)}, u32[]{:S(2)}) collective-permute-start(f32[8,96,128]{2,1,0:T(8,128)S(1)} %all_to_all.15.own), channel_id=1, source_target_pairs={{32,0},{64,32},{96,64},{128,96},{160,128},{192,160},{224,192},{256... | collective-permute-start | bytes 1179656 | tf_op jit(solution)/shard_map/ppermute | solution.py:614
  64.9 1.0 collective-permute-start.6
  66.0 5.8 %collective-permute-done.7.xa = f32[8,96,128]{2,1,0:T(8,128)S(1)} collective-permute-done((f32[8,96,128]{2,1,0:T(8,128)S(1)}, f32[8,96,128]{2,1,0:T(8,128)S(1)}, u32[]{:S(2)}, u32[]{:S(2)}) %collective-permute-start.7) | collective-permute-done | bytes 393248 | tf_op jit(solution)/shard_map/ppermute | solution.py:614
  71.7 3.3 %pack1.1 = (f32[96,48,128]{2,1,0:T(8,128)S(1)}, f32[12,48,128]{2,1,0:T(8,128)S(1)}, f32[12,48,128]{2,1,0:T(8,128)S(1)}) custom-call(s32[4]{0:T(128)S(1)} %pad_add_fusion.pos, f32[8,96,128]{2,1,0:T(8,128)S(1)} %all_to_all.15.own, f32[8,96,128]{2,1,0:T(8,128)S(1)} %collective-permute-done.6.xb, f32[8,96,128]{2,1,0:T(8,128)S(1)} %collective-permute-done.7.xa), custom_call_target="tpu_custom_call" | custom-call | tf_op jit(solution)/shard_map/pack1/pallas_call | solution.py:599
  75.0 3.1 %collective-permute-start.8 = (f32[12,48,128]{2,1,0:T(8,128)S(1)}, f32[12,48,128]{2,1,0:T(8,128)S(1)}, u32[]{:S(2)}, u32[]{:S(2)}) collective-permute-start(f32[12,48,128]{2,1,0:T(8,128)S(1)} %get-tuple-element.18), channel_id=1, source_target_pairs={{0,8},{8,16},{16,24},{1,9},{9,17},{17,25},{2,10},{10,18},{18,26},{... | collective-permute-start | bytes 884744 | tf_op jit(solution)/shard_map/ppermute | solution.py:614
  78.2 1.3 collective-permute-start.9
  79.5 2.3 %collective-permute-done.8.before = f32[12,48,128]{2,1,0:T(8,128)S(1)} collective-permute-done((f32[12,48,128]{2,1,0:T(8,128)S(1)}, f32[12,48,128]{2,1,0:T(8,128)S(1)}, u32[]{:S(2)}, u32[]{:S(2)}) %collective-permute-start.8) | collective-permute-done | bytes 294944 | tf_op jit(solution)/shard_map/ppermute | solution.py:614
  81.8 3.8 %collective-permute-done.9.after = f32[12,48,128]{2,1,0:T(8,128)S(1)} collective-permute-done((f32[12,48,128]{2,1,0:T(8,128)S(1)}, f32[12,48,128]{2,1,0:T(8,128)S(1)}, u32[]{:S(2)}, u32[]{:S(2)}) %collective-permute-start.9) | collective-permute-done | bytes 294944 | tf_op jit(solution)/shard_map/ppermute | solution.py:614
  85.6 14.2 %down1.1 = (f32[4,12,48,128]{3,2,1,0:T(8,128)S(1)}, f32[4,10,24,128]{3,2,1,0:T(8,128)S(1)}, f32[16,16,128]{2,1,0:T(8,128)S(1)}) custom-call(s32[4]{0:T(128)S(1)} %pad_add_fusion.pos, f32[96,48,128]{2,1,0:T(8,128)S(1)} %get-tuple-element.17.whole, f32[12,48,128]{2,1,0:T(8,128)S(1)} %collective-permute-done.8.before, ...), custom_call_target="tpu_custom_call" | custom-call | tf_op jit(solution)/shard_map/down1/pallas_call | solution.py:599
  99.8 19.2 %all_to_all.16 = f32[16,16,128]{2,1,0:T(8,128)S(1)} all-to-all(f32[16,16,128]{2,1,0:T(8,128)S(1)} %get-tuple-element.20), channel_id=1, replica_groups=mesh['gx'=16,'gy'=4,'gz'=8] {'gx'}, dimensions={0} | all-to-all | bytes 262144 | tf_op jit(solution)/shard_map/all_to_all | solution.py:676
  119.1 12.3 %all_to_all.17.gathered = f32[4,256,128]{2,1,0:T(8,128)S(1)} all-to-all(f32[4,256,128]{2,1,0:T(8,128)S(1)} %broadcast_in_dim.8), channel_id=1, replica_groups=mesh['gx'=16,'gy'=4,'gz'=8] {'gy'}, dimensions={0} | all-to-all | bytes 1048576 | tf_op jit(solution)/shard_map/all_to_all | solution.py:679
  131.4 16.9 %up.1 = (f32[8,32,128]{2,1,0:T(8,128)}, f32[8,32,128]{2,1,0:T(8,128)}) custom-call(s32[4]{0:T(128)S(1)} %pad_add_fusion.pos, f32[4,256,128]{2,1,0:T(8,128)S(1)} %all_to_all.17.gathered, f32[4,10,24,128]{3,2,1,0:T(8,128)S(1)} %get-tuple-element.21.window2, f32[4,12,48,128]{3,2,1,0:T(8,128)S(1)} %get-tuple-element.22.window1, ...), custom_call_target="tpu_custom_call" | custom-call | tf_op jit(solution)/shard_map/up/pallas_call | solution.py:599
  (21 shorter events, 0.2 us)
Async XLA Ops:
  0.6 8.3 %copy-start.2 = (f32[8,32,128]{2,1,0:T(8,128)S(1)}, f32[8,32,128]{2,1,0:T(8,128)}, u32[]{:S(2)}) copy-start(f32[8,32,128]{2,1,0:T(8,128)} %f_ref.1) | copy-start | bytes 393220
  0.6 8.3 %copy-start.1 = (f32[8,32,128]{2,1,0:T(8,128)S(1)}, f32[8,32,128]{2,1,0:T(8,128)}, u32[]{:S(2)}) copy-start(f32[8,32,128]{2,1,0:T(8,128)} %b_ref.1) | copy-start | bytes 393220
  0.7 8.3 %copy-start = (f32[8,32,128]{2,1,0:T(8,128)S(1)}, f32[8,32,128]{2,1,0:T(8,128)}, u32[]{:S(2)}) copy-start(f32[8,32,128]{2,1,0:T(8,128)} %a_ref.1) | copy-start | bytes 393220
  2.7 8.0 %collective-permute-start = (f32[3,5,32,128]{3,2,1,0:T(8,128)S(1)}, f32[3,5,32,128]{3,2,1,0:T(8,128)S(1)}, u32[]{:S(2)}, u32[]{:S(2)}) collective-permute-start(f32[3,5,32,128]{3,2,1,0:T(8,128)S(1)} %pad_maximum_fusion), channel_id=1, source_target_pairs={{0,1},{1,2},{2,3},{3,4},{4,5},{5,6},{6,7},{8,9},{9,10},{10,11},{11... | collective-permute-start | bytes 737288 | tf_op jit(solution)/shard_map/ppermute | solution.py:614
  7.6 7.6 %collective-permute-start.1 = (f32[3,5,32,128]{3,2,1,0:T(8,128)S(1)}, f32[3,5,32,128]{3,2,1,0:T(8,128)S(1)}, u32[]{:S(2)}, u32[]{:S(2)}) collective-permute-start(f32[3,5,32,128]{3,2,1,0:T(8,128)S(1)} %pad_maximum_fusion.1), channel_id=1, source_target_pairs={{1,0},{2,1},{3,2},{4,3},{5,4},{6,5},{7,6},{9,8},{10,9},{11,10},{12... | collective-permute-start | bytes 737288 | tf_op jit(solution)/shard_map/ppermute | solution.py:614
  15.3 7.4 %collective-permute-start.2 = (f32[3,18,8,128]{3,2,1,0:T(8,128)S(1)}, f32[3,18,8,128]{3,2,1,0:T(8,128)S(1)}, u32[]{:S(2)}, u32[]{:S(2)}) collective-permute-start(f32[3,18,8,128]{3,2,1,0:T(8,128)S(1)} %pad_maximum_fusion.2), channel_id=1, source_target_pairs={{0,32},{32,64},{64,96},{96,128},{128,160},{160,192},{192,224},{224... | collective-permute-start | bytes 663560 | tf_op jit(solution)/shard_map/ppermute | solution.py:614
  19.8 5.5 %collective-permute-start.3 = (f32[3,18,8,128]{3,2,1,0:T(8,128)S(1)}, f32[3,18,8,128]{3,2,1,0:T(8,128)S(1)}, u32[]{:S(2)}, u32[]{:S(2)}) collective-permute-start(f32[3,18,8,128]{3,2,1,0:T(8,128)S(1)} %pad_maximum_fusion.3), channel_id=1, source_target_pairs={{32,0},{64,32},{96,64},{128,96},{160,128},{192,160},{224,192},{256... | collective-permute-start | bytes 663560 | tf_op jit(solution)/shard_map/ppermute | solution.py:614
  26.6 5.3 %collective-permute-start.4 = (f32[4,48,128]{2,1,0:T(8,128)S(1)}, f32[4,48,128]{2,1,0:T(8,128)S(1)}, u32[]{:S(2)}, u32[]{:S(2)}) collective-permute-start(f32[4,48,128]{2,1,0:T(8,128)S(1)} %get-tuple-element.14), channel_id=1, source_target_pairs={{0,8},{8,16},{16,24},{1,9},{9,17},{17,25},{2,10},{10,18},{18,26},{... | collective-permute-start | bytes 294920 | tf_op jit(solution)/shard_map/ppermute | solution.py:614
  29.6 6.0 %collective-permute-start.5 = (f32[4,48,128]{2,1,0:T(8,128)S(1)}, f32[4,48,128]{2,1,0:T(8,128)S(1)}, u32[]{:S(2)}, u32[]{:S(2)}) collective-permute-start(f32[4,48,128]{2,1,0:T(8,128)S(1)} %get-tuple-element.15), channel_id=1, source_target_pairs={{8,0},{16,8},{24,16},{9,1},{17,9},{25,17},{10,2},{18,10},{26,18},{... | collective-permute-start | bytes 294920 | tf_op jit(solution)/shard_map/ppermute | solution.py:614
  62.5 9.2 %collective-permute-start.7 = (f32[8,96,128]{2,1,0:T(8,128)S(1)}, f32[8,96,128]{2,1,0:T(8,128)S(1)}, u32[]{:S(2)}, u32[]{:S(2)}) collective-permute-start(f32[8,96,128]{2,1,0:T(8,128)S(1)} %all_to_all.15.own), channel_id=1, source_target_pairs={{32,0},{64,32},{96,64},{128,96},{160,128},{192,160},{224,192},{256... | collective-permute-start | bytes 1179656 | tf_op jit(solution)/shard_map/ppermute | solution.py:614
  64.9 6.8 %collective-permute-start.6 = (f32[8,96,128]{2,1,0:T(8,128)S(1)}, f32[8,96,128]{2,1,0:T(8,128)S(1)}, u32[]{:S(2)}, u32[]{:S(2)}) collective-permute-start(f32[8,96,128]{2,1,0:T(8,128)S(1)} %all_to_all.15.own), channel_id=1, source_target_pairs={{0,32},{32,64},{64,96},{96,128},{128,160},{160,192},{192,224},{224... | collective-permute-start | bytes 1179656 | tf_op jit(solution)/shard_map/ppermute | solution.py:614
  75.0 6.8 %collective-permute-start.8 = (f32[12,48,128]{2,1,0:T(8,128)S(1)}, f32[12,48,128]{2,1,0:T(8,128)S(1)}, u32[]{:S(2)}, u32[]{:S(2)}) collective-permute-start(f32[12,48,128]{2,1,0:T(8,128)S(1)} %get-tuple-element.18), channel_id=1, source_target_pairs={{0,8},{8,16},{16,24},{1,9},{9,17},{17,25},{2,10},{10,18},{18,26},{... | collective-permute-start | bytes 884744 | tf_op jit(solution)/shard_map/ppermute | solution.py:614
  78.2 7.5 %collective-permute-start.9 = (f32[12,48,128]{2,1,0:T(8,128)S(1)}, f32[12,48,128]{2,1,0:T(8,128)S(1)}, u32[]{:S(2)}, u32[]{:S(2)}) collective-permute-start(f32[12,48,128]{2,1,0:T(8,128)S(1)} %get-tuple-element.19), channel_id=1, source_target_pairs={{8,0},{16,8},{24,16},{9,1},{17,9},{25,17},{10,2},{18,10},{26,18},{... | collective-permute-start | bytes 884744 | tf_op jit(solution)/shard_map/ppermute | solution.py:614

commit v2 on v1

--- a/solution.py
+++ b/solution.py
@@ -121,8 +121,11 @@
             ext[index, plane, :, 128:256] = jnp.where(lane >= 120, roll(before[tile], 120 - 8 * place, 1), ahead)
 
 
+U0, U1, U2 = 4, 8, 16
+
+
 def prepare0(ext, weights, diagonal, scaled):
-    @pl.loop(0, diagonal.shape[0])
+    @pl.loop(0, diagonal.shape[0], unroll=U0)
     def _(plane):
         got, middle, inverse = coefficients(
             ext[2, plane + 1], ext[2, plane], ext[2, plane + 2], ext[1, plane + 1], 0
@@ -149,7 +152,7 @@
     def _(plane):
         start[plane] = FIRST * scaled[plane]
 
-    @pl.loop(0, iterate.shape[0])
+    @pl.loop(0, iterate.shape[0], unroll=U0)
     def _(plane):
         value = start[plane + 1]
         got = defect(
@@ -170,7 +173,7 @@
 
     half = planes // 2
 
-    @pl.loop(0, half)
+    @pl.loop(0, half, unroll=U0)
     def _(plane):
         sums[plane] = left_over(2 * plane) + left_over(2 * plane + 1)
         for index in (1, 2):
@@ -221,8 +224,8 @@
         right[tile] = high
 
 
-def pass_all(weights, scaled, value, out, count, combine):
-    @pl.loop(0, count)
+def pass_all(weights, scaled, value, out, count, combine, unroll):
+    @pl.loop(0, count, unroll=unroll)
     def _(plane):
         middle = value[plane + 1]
         got = defect(
@@ -236,7 +239,7 @@
 
 
 def prepare(ext, weights, diagonal, scaled, level, offset):
-    @pl.loop(0, diagonal.shape[0])
+    @pl.loop(0, diagonal.shape[0], unroll=(U0, U1, U2)[level])
     def _(plane):
         at = plane + offset
         got, middle, inverse = coefficients(ext[2, at], ext[2, at - 1], ext[2, at + 1], ext[1, at], level)
@@ -272,7 +275,7 @@
     start1[0] = jnp.zeros((48, 128), F32)
     start1[depth + 1] = jnp.zeros((48, 128), F32)
 
-    @pl.loop(0, depth)
+    @pl.loop(0, depth, unroll=U1)
     def _(plane):
         start1[plane + 1] = FIRST * scaled1[plane]
 
@@ -283,11 +286,11 @@
     def put1(plane, value):
         iterate1[plane + 4] = value
 
-    pass_all(weights1, scaled1, start1, put1, depth, lambda value, got: value + (CARRY * value + GAIN * got))
+    pass_all(weights1, scaled1, start1, put1, depth, lambda value, got: value + (CARRY * value + GAIN * got), U1)
 
     half = depth // 2
 
-    @pl.loop(0, half)
+    @pl.loop(0, half, unroll=max(1, U1 // 2))
     def _(pair):
         total = None
         for plane in (2 * pair, 2 * pair + 1):
@@ -303,7 +306,7 @@
         for index in (1, 2):
             sums1[index * half + pair] = ext1[index, 2 * pair + 4] + ext1[index, 2 * pair + 5]
 
-    @pl.loop(0, 3 * half)
+    @pl.loop(0, 3 * half, unroll=8)
     def _(plane):
         thin[plane] = sums1[plane, pl.ds(0, 24, stride=2), :] + sums1[plane, pl.ds(1, 24, stride=2), :]
 
@@ -335,7 +338,7 @@
     def put2(plane, value):
         iterate2[plane + 4] = value
 
-    pass_all(weights2, scaled2, start2, put2, half, lambda value, got: value + (CARRY * value + GAIN * got))
+    pass_all(weights2, scaled2, start2, put2, half, lambda value, got: value + (CARRY * value + GAIN * got), U2)
 
     quarter = half // 2
     group = quarter // 2
@@ -448,7 +451,7 @@
     count = iterate.shape[0]
     prepare(ext, weights, diagonal, scaled, level, 1)
 
-    @pl.loop(0, count - 2)
+    @pl.loop(0, count - 2, unroll=(U0, U1, U2)[level])
     def _(plane):
         value = iterate[plane + 1]
         got = FIRST * defect(
@@ -461,7 +464,7 @@
         update[plane] = got
         middle[plane] = value + got
 
-    @pl.loop(0, count - 4)
+    @pl.loop(0, count - 4, unroll=(U0, U1, U2)[level])
     def _(plane):
         value = middle[plane + 1]
         got = defect(
@@ -558,7 +561,7 @@
     prepare0(ext0, weights0, diagonal0, scaled0)
     count = iterate0.shape[0]
 
-    @pl.loop(0, count - 2)
+    @pl.loop(0, count - 2, unroll=U0)
     def _(plane):
         value = value0[plane + 1]
         got = FIRST * defect(
@@ -571,7 +574,7 @@
         update0[plane] = got
         middle0[plane] = value + got
 
-    @pl.loop(0, count - 4)
+    @pl.loop(0, count - 4, unroll=U0)
     def _(plane):
         value = middle0[plane + 1]
         got = defect(
@@ -583,7 +586,7 @@
         )
         out0[plane] = value + (CARRY * update0[plane + 1] + GAIN * got)
 
-    @pl.loop(0, count - 6)
+    @pl.loop(0, count - 6, unroll=U0)
     def _(plane):
         value = out0[plane + 1]
         solved[plane] = value[0:32, 0:128]

time: 149 us -> 135 us (0.906)
  Pallas kernels: 40.7 us -> 27.4 us
    pallas_call x5, Pallas kernels: 40.7 us -> 27.4 us  [call(): pl.pallas_call(body, name=name, out_shape=[jax.ShapeDtypeStruct(shape, F3...]
where the time goes in v2:
time: 135 us
  blocking collectives  53.3 us (39%)
  waiting for transfers between devices  28.2 us (21%)
  Pallas kernels  27.4 us (20%)
  starting transfers between devices  22.8 us (17%)
  local copies, waits for them, and re-layouts  2.14 us (2%)
    pallas_call x5, Pallas kernels, call(): pl.pallas_call(body, name=name, out_shape=[jax.ShapeDtypeStruct(shape, F3...  27.4 us
    all_to_all x1, blocking collectives, on_device(): own = lax.all_to_all(message, 'gz', 0, 0)  21.8 us
    ppermute x5, waiting for transfers between devices, exchange(): lax.ppermute(down_values, axis, down_pairs)  20.5 us
    all_to_all x1, blocking collectives, on_device(): gathered = lax.all_to_all(message, 'gx', 0, 0)  19.2 us
    ppermute x5, starting transfers between devices, exchange(): lax.ppermute(up_values, axis, up_pairs)  16.5 us
    all_to_all x1, blocking collectives, on_device(): gathered = lax.all_to_all(gathered, 'gy', 0, 0)  12.3 us
    ppermute x5, waiting for transfers between devices, exchange(): lax.ppermute(up_values, axis, up_pairs)  7.7 us
    ppermute x5, starting transfers between devices, exchange(): lax.ppermute(down_values, axis, down_pairs)  6.29 us
  transfers between devices with their start and end apart: 10, of which 9 were waited for; matrix products, arithmetic and copies ran while one was open for 0% of the time, Pallas kernels for 0%

profile of v2, /device:TPU:1, one launch (start us, length us, event | category | flops | bytes accessed | tf_op | source)
XLA Modules:
  0.0 135.0 jit_solution(11997744999523629290)
XLA Ops:
  0.6 0.0 copy-start.1
  0.7 0.0 copy-start
  0.7 1.0 slice_bitcast_fusion.2
  1.7 1.0 slice_bitcast_fusion
  2.7 4.8 %collective-permute-start = (f32[3,5,32,128]{3,2,1,0:T(8,128)S(1)}, f32[3,5,32,128]{3,2,1,0:T(8,128)S(1)}, u32[]{:S(2)}, u32[]{:S(2)}) collective-permute-start(f32[3,5,32,128]{3,2,1,0:T(8,128)S(1)} %pad_maximum_fusion), channel_id=1, source_target_pairs={{0,1},{1,2},{2,3},{3,4},{4,5},{5,6},{6,7},{8,9},{9,10},{10,11},{11... | collective-permute-start | bytes 737288 | tf_op jit(solution)/shard_map/ppermute | solution.py:617
  7.6 1.3 collective-permute-start.1
  9.0 1.7 %collective-permute-done.zb = f32[3,5,32,128]{3,2,1,0:T(8,128)S(1)} collective-permute-done((f32[3,5,32,128]{3,2,1,0:T(8,128)S(1)}, f32[3,5,32,128]{3,2,1,0:T(8,128)S(1)}, u32[]{:S(2)}, u32[]{:S(2)}) %collective-permute-start) | collective-permute-done | bytes 245792 | tf_op jit(solution)/shard_map/ppermute | solution.py:617
  10.7 4.5 %collective-permute-done.1.za = f32[3,5,32,128]{3,2,1,0:T(8,128)S(1)} collective-permute-done((f32[3,5,32,128]{3,2,1,0:T(8,128)S(1)}, f32[3,5,32,128]{3,2,1,0:T(8,128)S(1)}, u32[]{:S(2)}, u32[]{:S(2)}) %collective-permute-start.1) | collective-permute-done | bytes 245792 | tf_op jit(solution)/shard_map/ppermute | solution.py:617
  15.3 4.5 %collective-permute-start.2 = (f32[3,18,8,128]{3,2,1,0:T(8,128)S(1)}, f32[3,18,8,128]{3,2,1,0:T(8,128)S(1)}, u32[]{:S(2)}, u32[]{:S(2)}) collective-permute-start(f32[3,18,8,128]{3,2,1,0:T(8,128)S(1)} %pad_maximum_fusion.2), channel_id=1, source_target_pairs={{0,32},{32,64},{64,96},{96,128},{128,160},{160,192},{192,224},{224... | collective-permute-start | bytes 663560 | tf_op jit(solution)/shard_map/ppermute | solution.py:617
  19.8 0.0 collective-permute-start.3
  19.9 0.1 pad_add_fusion.pos
  20.0 2.7 %collective-permute-done.2.xb = f32[3,18,8,128]{3,2,1,0:T(8,128)S(1)} collective-permute-done((f32[3,18,8,128]{3,2,1,0:T(8,128)S(1)}, f32[3,18,8,128]{3,2,1,0:T(8,128)S(1)}, u32[]{:S(2)}, u32[]{:S(2)}) %collective-permute-start.2) | collective-permute-done | bytes 221216 | tf_op jit(solution)/shard_map/ppermute | solution.py:617
  22.7 2.7 %collective-permute-done.3.xa = f32[3,18,8,128]{3,2,1,0:T(8,128)S(1)} collective-permute-done((f32[3,18,8,128]{3,2,1,0:T(8,128)S(1)}, f32[3,18,8,128]{3,2,1,0:T(8,128)S(1)}, u32[]{:S(2)}, u32[]{:S(2)}) %collective-permute-start.3) | collective-permute-done | bytes 221216 | tf_op jit(solution)/shard_map/ppermute | solution.py:617
  25.3 1.3 pack0.1
  26.6 3.0 %collective-permute-start.4 = (f32[4,48,128]{2,1,0:T(8,128)S(1)}, f32[4,48,128]{2,1,0:T(8,128)S(1)}, u32[]{:S(2)}, u32[]{:S(2)}) collective-permute-start(f32[4,48,128]{2,1,0:T(8,128)S(1)} %get-tuple-element.14), channel_id=1, source_target_pairs={{0,8},{8,16},{16,24},{1,9},{9,17},{17,25},{2,10},{10,18},{18,26},{... | collective-permute-start | bytes 294920 | tf_op jit(solution)/shard_map/ppermute | solution.py:617
  29.6 1.3 collective-permute-start.5
  30.9 0.9 collective-permute-done.4.before.before0
  31.9 3.8 %collective-permute-done.5.after.after0 = f32[4,48,128]{2,1,0:T(8,128)S(1)} collective-permute-done((f32[4,48,128]{2,1,0:T(8,128)S(1)}, f32[4,48,128]{2,1,0:T(8,128)S(1)}, u32[]{:S(2)}, u32[]{:S(2)}) %collective-permute-start.5) | collective-permute-done | bytes 98336 | tf_op jit(solution)/shard_map/ppermute | solution.py:617
  35.6 3.3 %down0.1 = (f32[14,48,256]{2,1,0:T(8,128)S(1)}, f32[8,96,128]{2,1,0:T(8,128)S(1)}) custom-call(f32[3,18,48,128]{3,2,1,0:T(8,128)S(1)} %get-tuple-element.13.whole.whole0, f32[4,48,128]{2,1,0:T(8,128)S(1)} %collective-permute-done.4.before.before0, f32[4,48,128]{2,1,0:T(8,128)S(1)} %collective-permute-done.5.after.after0), custom_call_target="tpu_custom_call" | custom-call | tf_op jit(solution)/shard_map/down0/pallas_call | solution.py:602
  39.0 21.8 %all_to_all.15.own = f32[8,96,128]{2,1,0:T(8,128)S(1)} all-to-all(f32[8,96,128]{2,1,0:T(8,128)S(1)} %get-tuple-element.16), channel_id=1, replica_groups=mesh['gx'=16,'gy'=4,'gz'=8] {'gz'}, dimensions={0} | all-to-all | bytes 786432 | tf_op jit(solution)/shard_map/all_to_all | solution.py:654
  60.8 2.4 %collective-permute-start.7 = (f32[8,96,128]{2,1,0:T(8,128)S(1)}, f32[8,96,128]{2,1,0:T(8,128)S(1)}, u32[]{:S(2)}, u32[]{:S(2)}) collective-permute-start(f32[8,96,128]{2,1,0:T(8,128)S(1)} %all_to_all.15.own), channel_id=1, source_target_pairs={{32,0},{64,32},{96,64},{128,96},{160,128},{192,160},{224,192},{256... | collective-permute-start | bytes 1179656 | tf_op jit(solution)/shard_map/ppermute | solution.py:617
  63.2 1.0 collective-permute-start.6
  64.2 5.8 %collective-permute-done.7.xa = f32[8,96,128]{2,1,0:T(8,128)S(1)} collective-permute-done((f32[8,96,128]{2,1,0:T(8,128)S(1)}, f32[8,96,128]{2,1,0:T(8,128)S(1)}, u32[]{:S(2)}, u32[]{:S(2)}) %collective-permute-start.7) | collective-permute-done | bytes 393248 | tf_op jit(solution)/shard_map/ppermute | solution.py:617
  70.0 3.3 %pack1.1 = (f32[96,48,128]{2,1,0:T(8,128)S(1)}, f32[12,48,128]{2,1,0:T(8,128)S(1)}, f32[12,48,128]{2,1,0:T(8,128)S(1)}) custom-call(s32[4]{0:T(128)S(1)} %pad_add_fusion.pos, f32[8,96,128]{2,1,0:T(8,128)S(1)} %all_to_all.15.own, f32[8,96,128]{2,1,0:T(8,128)S(1)} %collective-permute-done.6.xb, f32[8,96,128]{2,1,0:T(8,128)S(1)} %collective-permute-done.7.xa), custom_call_target="tpu_custom_call" | custom-call | tf_op jit(solution)/shard_map/pack1/pallas_call | solution.py:602
  73.3 3.1 %collective-permute-start.8 = (f32[12,48,128]{2,1,0:T(8,128)S(1)}, f32[12,48,128]{2,1,0:T(8,128)S(1)}, u32[]{:S(2)}, u32[]{:S(2)}) collective-permute-start(f32[12,48,128]{2,1,0:T(8,128)S(1)} %get-tuple-element.18), channel_id=1, source_target_pairs={{0,8},{8,16},{16,24},{1,9},{9,17},{17,25},{2,10},{10,18},{18,26},{... | collective-permute-start | bytes 884744 | tf_op jit(solution)/shard_map/ppermute | solution.py:617
  76.4 1.3 collective-permute-start.9
  77.7 2.3 %collective-permute-done.8.before = f32[12,48,128]{2,1,0:T(8,128)S(1)} collective-permute-done((f32[12,48,128]{2,1,0:T(8,128)S(1)}, f32[12,48,128]{2,1,0:T(8,128)S(1)}, u32[]{:S(2)}, u32[]{:S(2)}) %collective-permute-start.8) | collective-permute-done | bytes 294944 | tf_op jit(solution)/shard_map/ppermute | solution.py:617
  80.1 3.8 %collective-permute-done.9.after = f32[12,48,128]{2,1,0:T(8,128)S(1)} collective-permute-done((f32[12,48,128]{2,1,0:T(8,128)S(1)}, f32[12,48,128]{2,1,0:T(8,128)S(1)}, u32[]{:S(2)}, u32[]{:S(2)}) %collective-permute-start.9) | collective-permute-done | bytes 294944 | tf_op jit(solution)/shard_map/ppermute | solution.py:617
  83.9 6.7 %down1.1 = (f32[4,12,48,128]{3,2,1,0:T(8,128)S(1)}, f32[4,10,24,128]{3,2,1,0:T(8,128)S(1)}, f32[16,16,128]{2,1,0:T(8,128)S(1)}) custom-call(s32[4]{0:T(128)S(1)} %pad_add_fusion.pos, f32[96,48,128]{2,1,0:T(8,128)S(1)} %get-tuple-element.17.whole, f32[12,48,128]{2,1,0:T(8,128)S(1)} %collective-permute-done.8.before, ...), custom_call_target="tpu_custom_call" | custom-call | tf_op jit(solution)/shard_map/down1/pallas_call | solution.py:602
  90.6 19.2 %all_to_all.16 = f32[16,16,128]{2,1,0:T(8,128)S(1)} all-to-all(f32[16,16,128]{2,1,0:T(8,128)S(1)} %get-tuple-element.20), channel_id=1, replica_groups=mesh['gx'=16,'gy'=4,'gz'=8] {'gx'}, dimensions={0} | all-to-all | bytes 262144 | tf_op jit(solution)/shard_map/all_to_all | solution.py:679
  109.9 12.3 %all_to_all.17.gathered = f32[4,256,128]{2,1,0:T(8,128)S(1)} all-to-all(f32[4,256,128]{2,1,0:T(8,128)S(1)} %broadcast_in_dim.8), channel_id=1, replica_groups=mesh['gx'=16,'gy'=4,'gz'=8] {'gy'}, dimensions={0} | all-to-all | bytes 1048576 | tf_op jit(solution)/shard_map/all_to_all | solution.py:682
  122.2 12.8 %up.1 = (f32[8,32,128]{2,1,0:T(8,128)}, f32[8,32,128]{2,1,0:T(8,128)}) custom-call(s32[4]{0:T(128)S(1)} %pad_add_fusion.pos, f32[4,256,128]{2,1,0:T(8,128)S(1)} %all_to_all.17.gathered, f32[4,10,24,128]{3,2,1,0:T(8,128)S(1)} %get-tuple-element.21.window2, f32[4,12,48,128]{3,2,1,0:T(8,128)S(1)} %get-tuple-element.22.window1, ...), custom_call_target="tpu_custom_call" | custom-call | tf_op jit(solution)/shard_map/up/pallas_call | solution.py:602
  (21 shorter events, 0.2 us)
Async XLA Ops:
  0.6 8.3 %copy-start.2 = (f32[8,32,128]{2,1,0:T(8,128)S(1)}, f32[8,32,128]{2,1,0:T(8,128)}, u32[]{:S(2)}) copy-start(f32[8,32,128]{2,1,0:T(8,128)} %f_ref.1) | copy-start | bytes 393220
  0.6 8.3 %copy-start.1 = (f32[8,32,128]{2,1,0:T(8,128)S(1)}, f32[8,32,128]{2,1,0:T(8,128)}, u32[]{:S(2)}) copy-start(f32[8,32,128]{2,1,0:T(8,128)} %b_ref.1) | copy-start | bytes 393220
  0.7 8.3 %copy-start = (f32[8,32,128]{2,1,0:T(8,128)S(1)}, f32[8,32,128]{2,1,0:T(8,128)}, u32[]{:S(2)}) copy-start(f32[8,32,128]{2,1,0:T(8,128)} %a_ref.1) | copy-start | bytes 393220
  2.7 8.0 %collective-permute-start = (f32[3,5,32,128]{3,2,1,0:T(8,128)S(1)}, f32[3,5,32,128]{3,2,1,0:T(8,128)S(1)}, u32[]{:S(2)}, u32[]{:S(2)}) collective-permute-start(f32[3,5,32,128]{3,2,1,0:T(8,128)S(1)} %pad_maximum_fusion), channel_id=1, source_target_pairs={{0,1},{1,2},{2,3},{3,4},{4,5},{5,6},{6,7},{8,9},{9,10},{10,11},{11... | collective-permute-start | bytes 737288 | tf_op jit(solution)/shard_map/ppermute | solution.py:617
  7.6 7.6 %collective-permute-start.1 = (f32[3,5,32,128]{3,2,1,0:T(8,128)S(1)}, f32[3,5,32,128]{3,2,1,0:T(8,128)S(1)}, u32[]{:S(2)}, u32[]{:S(2)}) collective-permute-start(f32[3,5,32,128]{3,2,1,0:T(8,128)S(1)} %pad_maximum_fusion.1), channel_id=1, source_target_pairs={{1,0},{2,1},{3,2},{4,3},{5,4},{6,5},{7,6},{9,8},{10,9},{11,10},{12... | collective-permute-start | bytes 737288 | tf_op jit(solution)/shard_map/ppermute | solution.py:617
  15.3 7.4 %collective-permute-start.2 = (f32[3,18,8,128]{3,2,1,0:T(8,128)S(1)}, f32[3,18,8,128]{3,2,1,0:T(8,128)S(1)}, u32[]{:S(2)}, u32[]{:S(2)}) collective-permute-start(f32[3,18,8,128]{3,2,1,0:T(8,128)S(1)} %pad_maximum_fusion.2), channel_id=1, source_target_pairs={{0,32},{32,64},{64,96},{96,128},{128,160},{160,192},{192,224},{224... | collective-permute-start | bytes 663560 | tf_op jit(solution)/shard_map/ppermute | solution.py:617
  19.8 5.5 %collective-permute-start.3 = (f32[3,18,8,128]{3,2,1,0:T(8,128)S(1)}, f32[3,18,8,128]{3,2,1,0:T(8,128)S(1)}, u32[]{:S(2)}, u32[]{:S(2)}) collective-permute-start(f32[3,18,8,128]{3,2,1,0:T(8,128)S(1)} %pad_maximum_fusion.3), channel_id=1, source_target_pairs={{32,0},{64,32},{96,64},{128,96},{160,128},{192,160},{224,192},{256... | collective-permute-start | bytes 663560 | tf_op jit(solution)/shard_map/ppermute | solution.py:617
  26.6 5.3 %collective-permute-start.4 = (f32[4,48,128]{2,1,0:T(8,128)S(1)}, f32[4,48,128]{2,1,0:T(8,128)S(1)}, u32[]{:S(2)}, u32[]{:S(2)}) collective-permute-start(f32[4,48,128]{2,1,0:T(8,128)S(1)} %get-tuple-element.14), channel_id=1, source_target_pairs={{0,8},{8,16},{16,24},{1,9},{9,17},{17,25},{2,10},{10,18},{18,26},{... | collective-permute-start | bytes 294920 | tf_op jit(solution)/shard_map/ppermute | solution.py:617
  29.6 6.0 %collective-permute-start.5 = (f32[4,48,128]{2,1,0:T(8,128)S(1)}, f32[4,48,128]{2,1,0:T(8,128)S(1)}, u32[]{:S(2)}, u32[]{:S(2)}) collective-permute-start(f32[4,48,128]{2,1,0:T(8,128)S(1)} %get-tuple-element.15), channel_id=1, source_target_pairs={{8,0},{16,8},{24,16},{9,1},{17,9},{25,17},{10,2},{18,10},{26,18},{... | collective-permute-start | bytes 294920 | tf_op jit(solution)/shard_map/ppermute | solution.py:617
  60.8 9.2 %collective-permute-start.7 = (f32[8,96,128]{2,1,0:T(8,128)S(1)}, f32[8,96,128]{2,1,0:T(8,128)S(1)}, u32[]{:S(2)}, u32[]{:S(2)}) collective-permute-start(f32[8,96,128]{2,1,0:T(8,128)S(1)} %all_to_all.15.own), channel_id=1, source_target_pairs={{32,0},{64,32},{96,64},{128,96},{160,128},{192,160},{224,192},{256... | collective-permute-start | bytes 1179656 | tf_op jit(solution)/shard_map/ppermute | solution.py:617
  63.2 6.8 %collective-permute-start.6 = (f32[8,96,128]{2,1,0:T(8,128)S(1)}, f32[8,96,128]{2,1,0:T(8,128)S(1)}, u32[]{:S(2)}, u32[]{:S(2)}) collective-permute-start(f32[8,96,128]{2,1,0:T(8,128)S(1)} %all_to_all.15.own), channel_id=1, source_target_pairs={{0,32},{32,64},{64,96},{96,128},{128,160},{160,192},{192,224},{224... | collective-permute-start | bytes 1179656 | tf_op jit(solution)/shard_map/ppermute | solution.py:617
  73.3 6.8 %collective-permute-start.8 = (f32[12,48,128]{2,1,0:T(8,128)S(1)}, f32[12,48,128]{2,1,0:T(8,128)S(1)}, u32[]{:S(2)}, u32[]{:S(2)}) collective-permute-start(f32[12,48,128]{2,1,0:T(8,128)S(1)} %get-tuple-element.18), channel_id=1, source_target_pairs={{0,8},{8,16},{16,24},{1,9},{9,17},{17,25},{2,10},{10,18},{18,26},{... | collective-permute-start | bytes 884744 | tf_op jit(solution)/shard_map/ppermute | solution.py:617
  76.4 7.5 %collective-permute-start.9 = (f32[12,48,128]{2,1,0:T(8,128)S(1)}, f32[12,48,128]{2,1,0:T(8,128)S(1)}, u32[]{:S(2)}, u32[]{:S(2)}) collective-permute-start(f32[12,48,128]{2,1,0:T(8,128)S(1)} %get-tuple-element.19), channel_id=1, source_target_pairs={{8,0},{16,8},{24,16},{9,1},{17,9},{25,17},{10,2},{18,10},{26,18},{... | collective-permute-start | bytes 884744 | tf_op jit(solution)/shard_map/ppermute | solution.py:617

commit v3 on v1

--- a/solution.py
+++ b/solution.py
@@ -121,8 +121,13 @@
             ext[index, plane, :, 128:256] = jnp.where(lane >= 120, roll(before[tile], 120 - 8 * place, 1), ahead)
 
 
+def planes_of(count, level, start=0):
+    most = (7, 10, 16)[level]
+    return pl.loop(start, start + count, unroll=max(n for n in range(1, most + 1) if count % n == 0))
+
+
 def prepare0(ext, weights, diagonal, scaled):
-    @pl.loop(0, diagonal.shape[0])
+    @planes_of(diagonal.shape[0], 0)
     def _(plane):
         got, middle, inverse = coefficients(
             ext[2, plane + 1], ext[2, plane], ext[2, plane + 2], ext[1, plane + 1], 0
@@ -141,15 +146,15 @@
     return diagonal[at, 0:32, 0:128] * result
 
 
-def down0(whole, before, after, iterate, message, ext, weights, diagonal, scaled, start, sums):
+def down0(whole, before, after, iterate, message, weights, diagonal, scaled, ext, start, sums):
     unpack0(whole, before, after, ext)
     prepare0(ext, weights, diagonal, scaled)
 
-    @pl.loop(0, start.shape[0])
+    @planes_of(start.shape[0], 0)
     def _(plane):
         start[plane] = FIRST * scaled[plane]
 
-    @pl.loop(0, iterate.shape[0])
+    @planes_of(iterate.shape[0], 0)
     def _(plane):
         value = start[plane + 1]
         got = defect(
@@ -170,7 +175,7 @@
 
     half = planes // 2
 
-    @pl.loop(0, half)
+    @planes_of(half, 0)
     def _(plane):
         sums[plane] = left_over(2 * plane) + left_over(2 * plane + 1)
         for index in (1, 2):
@@ -196,7 +201,7 @@
     def spread(value):
         return jnp.where(lane < 64, value, 0.0), jnp.where(lane < 64, roll(value, 64, 1), 0.0)
 
-    @pl.loop(0, sources)
+    @pl.loop(0, sources, unroll=2)
     def _(source):
         for index in range(3):
             for plane in range(per):
@@ -210,7 +215,7 @@
 
     slot = lane_of((48, 128)) // 16
 
-    @pl.loop(0, left.shape[0])
+    @pl.loop(0, left.shape[0], unroll=2)
     def _(tile):
         low = high = jnp.zeros((48, 128), F32)
         for place in range(8):
@@ -221,13 +226,13 @@
         right[tile] = high
 
 
-def pass_all(weights, scaled, value, out, count, combine):
-    @pl.loop(0, count)
+def pass_all(weights, scaled, value, out, count, combine, level):
+    @planes_of(count, level)
     def _(plane):
         middle = value[plane + 1]
         got = defect(
-            scaled[plane],
-            [weights[index, plane] for index in range(6)],
+            scaled[plane + 4],
+            [weights[index, plane + 4] for index in range(6)],
             middle,
             value[plane],
             value[plane + 2],
@@ -235,21 +240,27 @@
         out(plane, combine(middle, got))
 
 
-def prepare(ext, weights, diagonal, scaled, level, offset):
-    @pl.loop(0, diagonal.shape[0])
-    def _(plane):
-        at = plane + offset
+def prepare(ext, weights, diagonal, scaled, level):
+    shape = scaled.shape[1:]
+    count = scaled.shape[0] - 8
+    for end in (0, count + 4):
+        for plane in range(4):
+            scaled[end + plane] = jnp.zeros(shape, F32)
+            for index in range(6):
+                weights[index, end + plane] = jnp.zeros(shape, F32)
+
+    @planes_of(count, level, 4)
+    def _(at):
         got, middle, inverse = coefficients(ext[2, at], ext[2, at - 1], ext[2, at + 1], ext[1, at], level)
         for index in range(6):
-            weights[index, plane] = got[index]
-        diagonal[plane] = middle
-        scaled[plane] = ext[0, at] * inverse
+            weights[index, at] = got[index]
+        diagonal[at] = middle
+        scaled[at] = ext[0, at] * inverse
 
 
 def down1(
-    pos, whole, before, after, window1, window2, message,
-    ext1, weights1, diagonal1, scaled1, start1, iterate1, sums1,
-    ext2, weights2, diagonal2, scaled2, start2, iterate2, sums2, thin, thick,
+    whole, before, after, message, weights1, scaled1, iterate1, weights2, scaled2, iterate2,
+    ext1, diagonal1, start1, sums1, ext2, diagonal2, start2, sums2, thin, thick,
 ):
     depth = whole.shape[0] // 3
     lane = lane_of((48, 128))
@@ -258,7 +269,7 @@
             for plane in range(4):
                 ext1[index, end + plane] = jnp.zeros((48, 128), F32)
 
-    @pl.loop(0, before.shape[0])
+    @pl.loop(0, before.shape[0], unroll=2)
     def _(tile):
         for place in range(8):
             at = 8 * tile + place
@@ -268,13 +279,13 @@
             value = jnp.where(lane >= 112, roll(before[tile], 112 - 16 * place, 1), value)
             ext1[index, plane + 4] = value
 
-    prepare(ext1, weights1, diagonal1, scaled1, 1, 4)
+    prepare(ext1, weights1, diagonal1, scaled1, 1)
     start1[0] = jnp.zeros((48, 128), F32)
     start1[depth + 1] = jnp.zeros((48, 128), F32)
 
-    @pl.loop(0, depth)
-    def _(plane):
-        start1[plane + 1] = FIRST * scaled1[plane]
+    @planes_of(depth, 1)
+    def _(plane):
+        start1[plane + 1] = FIRST * scaled1[plane + 4]
 
     for end in (0, depth + 4):
         for plane in range(4):
@@ -283,17 +294,17 @@
     def put1(plane, value):
         iterate1[plane + 4] = value
 
-    pass_all(weights1, scaled1, start1, put1, depth, lambda value, got: value + (CARRY * value + GAIN * got))
+    pass_all(weights1, scaled1, start1, put1, depth, lambda value, got: value + (CARRY * value + GAIN * got), 1)
 
     half = depth // 2
 
-    @pl.loop(0, half)
+    @planes_of(half, 1)
     def _(pair):
         total = None
         for plane in (2 * pair, 2 * pair + 1):
-            got = diagonal1[plane] * defect(
-                scaled1[plane],
-                [weights1[index, plane] for index in range(6)],
+            got = diagonal1[plane + 4] * defect(
+                scaled1[plane + 4],
+                [weights1[index, plane + 4] for index in range(6)],
                 iterate1[plane + 4],
                 iterate1[plane + 3],
                 iterate1[plane + 5],
@@ -303,7 +314,7 @@
         for index in (1, 2):
             sums1[index * half + pair] = ext1[index, 2 * pair + 4] + ext1[index, 2 * pair + 5]
 
-    @pl.loop(0, 3 * half)
+    @planes_of(3 * half, 1)
     def _(plane):
         thin[plane] = sums1[plane, pl.ds(0, 24, stride=2), :] + sums1[plane, pl.ds(1, 24, stride=2), :]
 
@@ -320,13 +331,13 @@
             for plane in range(4):
                 ext2[index, end + plane] = jnp.zeros((24, 128), F32)
 
-    prepare(ext2, weights2, diagonal2, scaled2, 2, 4)
+    prepare(ext2, weights2, diagonal2, scaled2, 2)
     start2[0] = jnp.zeros((24, 128), F32)
     start2[half + 1] = jnp.zeros((24, 128), F32)
 
     @pl.loop(0, half)
     def _(plane):
-        start2[plane + 1] = FIRST * scaled2[plane]
+        start2[plane + 1] = FIRST * scaled2[plane + 4]
 
     for end in (0, half + 4):
         for plane in range(4):
@@ -335,7 +346,7 @@
     def put2(plane, value):
         iterate2[plane + 4] = value
 
-    pass_all(weights2, scaled2, start2, put2, half, lambda value, got: value + (CARRY * value + GAIN * got))
+    pass_all(weights2, scaled2, start2, put2, half, lambda value, got: value + (CARRY * value + GAIN * got), 2)
 
     quarter = half // 2
     group = quarter // 2
@@ -348,9 +359,9 @@
             if index == 0:
                 total = None
                 for at in (2 * plane, 2 * plane + 1):
-                    got = diagonal2[at] * defect(
-                        scaled2[at],
-                        [weights2[face, at] for face in range(6)],
+                    got = diagonal2[at + 4] * defect(
+                        scaled2[at + 4],
+                        [weights2[face, at + 4] for face in range(6)],
                         iterate2[at + 4],
                         iterate2[at + 3],
                         iterate2[at + 5],
@@ -369,13 +380,6 @@
     for at in range(1, 6):
         result = result + dot(thick[at], place2[at])
     copies(message, result)
-
-    at1, at2 = pos[2] * 4, pos[2] * 2
-    for index in range(3):
-        window1[index] = ext1[index, pl.ds(at1, 12)]
-        window2[index] = ext2[index, pl.ds(at2, 10)]
-    window1[3] = iterate1[pl.ds(at1, 12)]
-    window2[3] = iterate2[pl.ds(at2, 10)]
 
 
 def bottom(gathered, whole, weights, scaled, update, values):
@@ -444,16 +448,15 @@
             values[later, plane] = middle + moved
 
 
-def finish(ext, iterate, weights, diagonal, scaled, level, update, middle, put):
+def finish(at, iterate, weights, scaled, level, update, middle, put):
     count = iterate.shape[0]
-    prepare(ext, weights, diagonal, scaled, level, 1)
-
-    @pl.loop(0, count - 2)
+
+    @planes_of(count - 2, level)
     def _(plane):
         value = iterate[plane + 1]
         got = FIRST * defect(
-            scaled[plane],
-            [weights[index, plane] for index in range(6)],
+            scaled[at + plane + 1],
+            [weights[index, at + plane + 1] for index in range(6)],
             value,
             iterate[plane],
             iterate[plane + 2],
@@ -461,12 +464,12 @@
         update[plane] = got
         middle[plane] = value + got
 
-    @pl.loop(0, count - 4)
+    @planes_of(count - 4, level)
     def _(plane):
         value = middle[plane + 1]
         got = defect(
-            scaled[plane + 1],
-            [weights[index, plane + 1] for index in range(6)],
+            scaled[at + plane + 2],
+            [weights[index, at + plane + 2] for index in range(6)],
             value,
             middle[plane],
             middle[plane + 2],
@@ -475,43 +478,56 @@
 
 
 def up(
-    pos, gathered, window2, window1, whole0, before0, after0, iterate0, solved, left_over,
+    pos, gathered, weights2, scaled2, iterate2, weights1, scaled1, iterate1,
+    weights0, diagonal0, scaled0, iterate0, solved, left_over,
     whole3, weights3, scaled3, update3, values3,
-    error2, value2, weights2, diagonal2, scaled2, update2, middle2, out2,
-    tall1, value1, weights1, diagonal1, scaled1, update1, middle1, out1,
-    tall0, ext0, value0, weights0, diagonal0, scaled0, update0, middle0, out0,
+    thin3, error2, value2, update2, middle2, out2,
+    tall1, value1, update1, middle1, out1,
+    tall0, value0, update0, middle0, out0,
 ):
     bottom(gathered, whole3, weights3, scaled3, update3, values3)
     group, rows = weights3.shape[1], weights3.shape[2]
     at_x, at_y, at_z = 4 * pos[0], 16 * pos[1], pos[2]
     last = (BOTTOM - 1) % 2
 
-    def rows_rule(row, lane):
-        place = jnp.where(row < 16, row, row - 24)
-        return lane == at_x + lax.shift_right_arithmetic(place, 1)
-
-    pick = matrix((24, rows), rows_rule)
+    lane = lane_of((8, 128))
+    near = lax.rem(lane, 64)
+    fits = ((near < 16) | ((near < 20) & (pos[1] < 3)) | ((near >= 60) & (pos[1] > 0))).astype(F32)
+    first_row, last_row = (pos[0] > 0).astype(F32), (pos[0] < pos[3] - 1).astype(F32)
+    low = row_of((8, 128)) < 4
+    own = jnp.where(low, fits, fits * last_row)
+    left = jnp.where(low, 0.0, fits * first_row)
     for plane in range(group):
-        got = dot(pick, values3[last, plane])
+        moved = pltpu.roll(values3[last, plane], lax.rem(rows - at_x, rows), 0)
+        both = jnp.concatenate([moved[0:8], moved[rows - 8 :]], axis=0)
+        both = pltpu.roll(both, lax.rem(128 - at_y, 128), 1)
+        ahead, behind = both[0:8] * own, both[8:16] * left
+        for start in (0, 1):
+            thin3[plane, pl.ds(start, 8, stride=2), :] = ahead
+            thin3[plane, pl.ds(16 + start, 4, stride=2), :] = behind[4:8]
+
+    def to_level2(row, lane):
+        side, within = lane // 128, lax.rem(lane, 128)
+        place = jnp.where(within < 64, within, within - 128)
+        source = jnp.where(side == 0, lax.rem(row, 128), lax.rem(row + 64, 128))
+        source = jnp.where(source < 64, source, source - 128)
+        return (source == lax.shift_right_arithmetic(place, 1)) & ((within < 40) | (within >= 120))
+
+    spread = dot(thin3[...].reshape(group * 24, 128), matrix((128, 256), to_level2)).reshape(group, 24, 256)
+    for plane in range(group):
         for side in range(2):
-
-            def lanes_rule(row, lane, side=side):
-                place = jnp.where(lane < 64, lane, lane - 128)
-                source = at_y + lax.shift_right_arithmetic(place, 1)
-                return (row - 64 * side == source) & (source >= 0) & (source < 64) & ((lane < 40) | (lane >= 120))
-
-            error2[side * group + plane + 2] = dot(got, matrix((128, 128), lanes_rule))
+            error2[side * group + plane + 2] = spread[plane, :, 128 * side : 128 * side + 128]
     for end in (0, 2 * group + 2):
         for plane in range(2):
             error2[end + plane] = jnp.zeros((24, 128), F32)
 
     for plane in range(10):
-        value2[plane] = window2[3, plane] + error2[at_z + plane // 2]
+        value2[plane] = iterate2[2 * at_z + plane] + error2[at_z + plane // 2]
 
     def put2(plane, value):
         out2[plane] = value
 
-    finish(window2, value2, weights2, diagonal2, scaled2, 2, update2, middle2, put2)
+    finish(2 * at_z, value2, weights2, scaled2, 2, update2, middle2, put2)
 
     def to_level1(row, lane):
         place = jnp.where(lane < 96, lane, lane - 128)
@@ -524,12 +540,12 @@
         tall1[plane, pl.ds(1, 24, stride=2), :] = out2[plane]
     spread = dot(tall1[...].reshape(6 * 48, 128), wide1).reshape(6, 48, 128)
     for plane in range(12):
-        value1[plane] = window1[3, plane] + spread[plane // 2]
+        value1[plane] = iterate1[4 * at_z + plane] + spread[plane // 2]
 
     def put1(plane, value):
         out1[plane] = value
 
-    finish(window1, value1, weights1, diagonal1, scaled1, 1, update1, middle1, put1)
+    finish(4 * at_z, value1, weights1, scaled1, 1, update1, middle1, put1)
 
     def to_level0(row, lane):
         place = jnp.where(lane < 192, lane, lane - 256)
@@ -544,21 +560,19 @@
         tall0[plane, pl.ds(40, 4, stride=2), :] = value[44:48]
         tall0[plane, pl.ds(41, 4, stride=2), :] = value[44:48]
 
-    @pl.loop(0, 8)
+    @planes_of(8, 1)
     def _(plane):
         value = dot(tall0[plane], wide0)
         out0[2 * plane] = value
         out0[2 * plane + 1] = value
 
-    @pl.loop(0, iterate0.shape[0])
+    @planes_of(iterate0.shape[0], 0)
     def _(plane):
         value0[plane] = iterate0[plane] + out0[plane + 1]
 
-    unpack0(whole0, before0, after0, ext0)
-    prepare0(ext0, weights0, diagonal0, scaled0)
     count = iterate0.shape[0]
 
-    @pl.loop(0, count - 2)
+    @planes_of(count - 2, 0)
     def _(plane):
         value = value0[plane + 1]
         got = FIRST * defect(
@@ -571,7 +585,7 @@
         update0[plane] = got
         middle0[plane] = value + got
 
-    @pl.loop(0, count - 4)
+    @planes_of(count - 4, 0)
     def _(plane):
         value = middle0[plane + 1]
         got = defect(
@@ -583,7 +597,7 @@
         )
         out0[plane] = value + (CARRY * update0[plane + 1] + GAIN * got)
 
-    @pl.loop(0, count - 6)
+    @planes_of(count - 6, 0)
     def _(plane):
         value = out0[plane + 1]
         solved[plane] = value[0:32, 0:128]
@@ -603,7 +617,7 @@
         in_specs=smem + [vmem] * len(args),
         out_specs=[vmem] * len(outs),
         scratch_shapes=[pltpu.VMEM(shape, F32) for shape in scratch],
-        compiler_params=pltpu.CompilerParams(vmem_limit_bytes=40 * 2**20),
+        compiler_params=pltpu.CompilerParams(vmem_limit_bytes=32 * 2**20),
     )(*operands)
 
 
@@ -612,11 +626,6 @@
     up_pairs = [(i, (i + 1) % peers) for i in range(peers if ring else peers - 1)]
     down_pairs = [(j, i) for i, j in up_pairs]
     return lax.ppermute(up_values, axis, up_pairs), lax.ppermute(down_values, axis, down_pairs)
-
-
-def coefficient_scratch(planes, rows, lanes):
-    shape = (planes, rows, lanes)
-    return [(6,) + shape, shape, shape]
 
 
 def on_device(right_side, acoef, beta):
@@ -639,11 +648,11 @@
     before0, after0 = exchange(right, left, "gy", False)
     plane0 = (48, 256)
     half = planes // 2
-    iterate0, message = call(
+    iterate0, message, weights0, diagonal0, scaled0 = call(
         down0,
         "down0",
-        [(depth - 4,) + plane0, (files, 3 * half * 8, 128)],
-        [(3, depth) + plane0] + coefficient_scratch(depth - 2, *plane0) + [(depth - 2,) + plane0, (3 * half, 32, 128)],
+        [(depth - 4,) + plane0, (files, 3 * half * 8, 128), (6, depth - 2) + plane0] + [(depth - 2,) + plane0] * 2,
+        [(3, depth) + plane0, (depth - 2,) + plane0, (3 * half, 32, 128)],
         None,
         (whole0, before0, after0),
     )
@@ -659,17 +668,15 @@
     plane1, plane2 = (48, 128), (24, 128)
     depth2 = depth1 // 2
     group = depth2 // 4
-    window1, window2, message = call(
+    tall1, tall2 = (depth1 + 8,) + plane1, (depth2 + 8,) + plane2
+    message, weights1, scaled1, iterate1, weights2, scaled2, iterate2 = call(
         down1,
         "down1",
-        [(4, 12) + plane1, (4, 10) + plane2, (ranks, 4 * group, 128)],
-        [(3, depth1 + 8) + plane1]
-        + coefficient_scratch(depth1, *plane1)
-        + [(depth1 + 2,) + plane1, (depth1 + 8,) + plane1, (3 * depth2,) + plane1, (3, depth2 + 8) + plane2]
-        + coefficient_scratch(depth2, *plane2)
-        + [(depth2 + 2,) + plane2, (depth2 + 8,) + plane2, (3 * depth2 // 2, 8, 128)]
+        [(ranks, 4 * group, 128), (6,) + tall1, tall1, tall1, (6,) + tall2, tall2, tall2],
+        [(3,) + tall1, tall1, (depth1 + 2,) + plane1, (3 * depth2,) + plane1]
+        + [(3,) + tall2, tall2, (depth2 + 2,) + plane2, (3 * depth2 // 2, 8, 128)]
         + [(3 * depth2,) + plane2, (6, 4 * group, 128)],
-        pos,
+        None,
         (whole1, before1, after1),
     )
 
@@ -685,16 +692,12 @@
         "up",
         [right_side.shape, right_side.shape],
         [(3, rows3 * group, 128), (6, group) + plane3, (group,) + plane3, (group,) + plane3, (2, group) + plane3]
-        + [(2 * group + 4,) + plane2, (10,) + plane2]
-        + coefficient_scratch(8, *plane2)
-        + [(8,) + plane2, (8,) + plane2, (6,) + plane2, (6,) + plane1, (12,) + plane1]
-        + coefficient_scratch(10, *plane1)
-        + [(10,) + plane1, (10,) + plane1, (8,) + plane1, (8,) + plane1]
-        + [(3, depth) + plane0, (depth - 4,) + plane0]
-        + coefficient_scratch(depth - 2, *plane0)
-        + [(depth - 6,) + plane0, (depth - 6,) + plane0, (depth - 2,) + plane0],
+        + [(group,) + plane2, (2 * group + 4,) + plane2, (10,) + plane2, (8,) + plane2, (8,) + plane2, (6,) + plane2]
+        + [(6,) + plane1, (12,) + plane1, (10,) + plane1, (10,) + plane1, (8,) + plane1]
+        + [(8,) + plane1, (depth - 4,) + plane0, (depth - 6,) + plane0, (depth - 6,) + plane0, (depth - 2,) + plane0],
         pos,
-        (gathered, window2, window1, whole0, before0, after0, iterate0),
+        (gathered, weights2, scaled2, iterate2, weights1, scaled1, iterate1)
+        + (weights0, diagonal0, scaled0, iterate0),
     )
     return solved, left_over
 

time: 149 us -> 128 us (0.86)
  Pallas kernels: 40.7 us -> 20.1 us
  local copies, waits for them, and re-layouts: 2.14 us -> 4.46 us
  waiting for transfers between devices: 28.2 us -> 25.9 us
    pallas_call x5, Pallas kernels: 40.7 us -> 20.1 us  [call(): pl.pallas_call(body, name=name, out_shape=[jax.ShapeDtypeStruct(shape, F3...]
    slice x3, local copies, waits for them, and re-layouts: 0.02 us -> 2.34 us  [on_device(): arrays[i][:, :8]]
    ppermute x5, waiting for transfers between devices: 7.7 us -> 5.99 us  [exchange(): lax.ppermute(up_values, axis, up_pairs)]
  transfers between devices with their start and end apart: 10 -> 10, of which waited for: 9 -> 8; matrix products, arithmetic and copies ran while one was open for 0% -> 2% of each run, Pallas kernels for 0% -> 0%
where the time goes in v3:
time: 128 us
  blocking collectives  53.3 us (42%)
  waiting for transfers between devices  25.9 us (20%)
  starting transfers between devices  22.9 us (18%)
  Pallas kernels  20.1 us (16%)
  local copies, waits for them, and re-layouts  4.46 us (3%)
    all_to_all x1, blocking collectives, on_device(): own = lax.all_to_all(message, 'gz', 0, 0)  21.8 us
    pallas_call x5, Pallas kernels, call(): pl.pallas_call(body, name=name, out_shape=[jax.ShapeDtypeStruct(shape, F3...  20.1 us
    ppermute x5, waiting for transfers between devices, exchange(): lax.ppermute(down_values, axis, down_pairs)  19.9 us
    all_to_all x1, blocking collectives, on_device(): gathered = lax.all_to_all(message, 'gx', 0, 0)  19.2 us
    ppermute x5, starting transfers between devices, exchange(): lax.ppermute(up_values, axis, up_pairs)  16.6 us
    all_to_all x1, blocking collectives, on_device(): gathered = lax.all_to_all(gathered, 'gy', 0, 0)  12.3 us
    ppermute x5, starting transfers between devices, exchange(): lax.ppermute(down_values, axis, down_pairs)  6.31 us
    ppermute x5, waiting for transfers between devices, exchange(): lax.ppermute(up_values, axis, up_pairs)  5.99 us
  transfers between devices with their start and end apart: 10, of which 8 were waited for; matrix products, arithmetic and copies ran while one was open for 2% of the time, Pallas kernels for 0%

profile of v3, /device:TPU:1, one launch (start us, length us, event | category | flops | bytes accessed | tf_op | source)
XLA Modules:
  0.0 127.7 jit_solution(4687920503762798810)
XLA Ops:
  0.7 1.0 slice_bitcast_fusion.2
  1.7 1.0 slice_bitcast_fusion
  2.7 4.8 %collective-permute-start = (f32[3,5,32,128]{3,2,1,0:T(8,128)S(1)}, f32[3,5,32,128]{3,2,1,0:T(8,128)S(1)}, u32[]{:S(2)}, u32[]{:S(2)}) collective-permute-start(f32[3,5,32,128]{3,2,1,0:T(8,128)S(1)} %pad_maximum_fusion), channel_id=1, source_target_pairs={{0,1},{1,2},{2,3},{3,4},{4,5},{5,6},{6,7},{8,9},{9,10},{10,11},{11... | collective-permute-start | bytes 737288 | tf_op jit(solution)/shard_map/ppermute | solution.py:628
  7.6 1.3 %collective-permute-start.1 = (f32[3,5,32,128]{3,2,1,0:T(8,128)S(1)}, f32[3,5,32,128]{3,2,1,0:T(8,128)S(1)}, u32[]{:S(2)}, u32[]{:S(2)}) collective-permute-start(f32[3,5,32,128]{3,2,1,0:T(8,128)S(1)} %pad_maximum_fusion.1), channel_id=1, source_target_pairs={{1,0},{2,1},{3,2},{4,3},{5,4},{6,5},{7,6},{9,8},{10,9},{11,10},{12... | collective-permute-start | bytes 737288 | tf_op jit(solution)/shard_map/ppermute | solution.py:628
  8.9 0.8 fusion
  9.7 0.8 fusion.1
  10.5 0.8 fusion.2
  11.3 3.9 %collective-permute-done.1.za = f32[3,5,32,128]{3,2,1,0:T(8,128)S(1)} collective-permute-done((f32[3,5,32,128]{3,2,1,0:T(8,128)S(1)}, f32[3,5,32,128]{3,2,1,0:T(8,128)S(1)}, u32[]{:S(2)}, u32[]{:S(2)}) %collective-permute-start.1) | collective-permute-done | bytes 245792 | tf_op jit(solution)/shard_map/ppermute | solution.py:628
  15.3 4.5 %collective-permute-start.2 = (f32[3,18,8,128]{3,2,1,0:T(8,128)S(1)}, f32[3,18,8,128]{3,2,1,0:T(8,128)S(1)}, u32[]{:S(2)}, u32[]{:S(2)}) collective-permute-start(f32[3,18,8,128]{3,2,1,0:T(8,128)S(1)} %pad_maximum_fusion.2), channel_id=1, source_target_pairs={{0,32},{32,64},{64,96},{96,128},{128,160},{160,192},{192,224},{224... | collective-permute-start | bytes 663560 | tf_op jit(solution)/shard_map/ppermute | solution.py:628
  19.8 0.0 collective-permute-start.3
  19.9 0.1 pad_add_fusion.pos
  20.0 2.7 %collective-permute-done.2.xb = f32[3,18,8,128]{3,2,1,0:T(8,128)S(1)} collective-permute-done((f32[3,18,8,128]{3,2,1,0:T(8,128)S(1)}, f32[3,18,8,128]{3,2,1,0:T(8,128)S(1)}, u32[]{:S(2)}, u32[]{:S(2)}) %collective-permute-start.2) | collective-permute-done | bytes 221216 | tf_op jit(solution)/shard_map/ppermute | solution.py:628
  22.7 2.7 %collective-permute-done.3.xa = f32[3,18,8,128]{3,2,1,0:T(8,128)S(1)} collective-permute-done((f32[3,18,8,128]{3,2,1,0:T(8,128)S(1)}, f32[3,18,8,128]{3,2,1,0:T(8,128)S(1)}, u32[]{:S(2)}, u32[]{:S(2)}) %collective-permute-start.3) | collective-permute-done | bytes 221216 | tf_op jit(solution)/shard_map/ppermute | solution.py:628
  25.3 1.3 pack0.1
  26.6 3.0 %collective-permute-start.4 = (f32[4,48,128]{2,1,0:T(8,128)S(1)}, f32[4,48,128]{2,1,0:T(8,128)S(1)}, u32[]{:S(2)}, u32[]{:S(2)}) collective-permute-start(f32[4,48,128]{2,1,0:T(8,128)S(1)} %get-tuple-element.21), channel_id=1, source_target_pairs={{0,8},{8,16},{16,24},{1,9},{9,17},{17,25},{2,10},{10,18},{18,26},{... | collective-permute-start | bytes 294920 | tf_op jit(solution)/shard_map/ppermute | solution.py:628
  29.6 1.3 %collective-permute-start.5 = (f32[4,48,128]{2,1,0:T(8,128)S(1)}, f32[4,48,128]{2,1,0:T(8,128)S(1)}, u32[]{:S(2)}, u32[]{:S(2)}) collective-permute-start(f32[4,48,128]{2,1,0:T(8,128)S(1)} %get-tuple-element.22), channel_id=1, source_target_pairs={{8,0},{16,8},{24,16},{9,1},{17,9},{25,17},{10,2},{18,10},{26,18},{... | collective-permute-start | bytes 294920 | tf_op jit(solution)/shard_map/ppermute | solution.py:628
  30.9 0.9 collective-permute-done.4.before
  31.9 3.8 %collective-permute-done.5.after = f32[4,48,128]{2,1,0:T(8,128)S(1)} collective-permute-done((f32[4,48,128]{2,1,0:T(8,128)S(1)}, f32[4,48,128]{2,1,0:T(8,128)S(1)}, u32[]{:S(2)}, u32[]{:S(2)}) %collective-permute-start.5) | collective-permute-done | bytes 98336 | tf_op jit(solution)/shard_map/ppermute | solution.py:628
  35.7 3.2 %down0.1 = (f32[14,48,256]{2,1,0:T(8,128)S(1)}, f32[8,96,128]{2,1,0:T(8,128)S(1)}, f32[6,16,48,256]{3,2,1,0:T(8,128)S(1)}, f32[16,48,256]{2,1,0:T(8,128)S(1)}, f32[16,48,256]{2,1,0:T(8,128)S(1)}) custom-call(f32[3,18,48,128]{3,2,1,0:T(8,128)S(1)} %get-tuple-element.20.whole, f32[4,48,128]{2,1,0:T(8,128)S(1)} %collective-permute-done.4.before, ...), custom_call_target="tpu_custom_call" | custom-call | tf_op jit(solution)/shard_map/down0/pallas_call | solution.py:613
  38.9 21.8 %all_to_all.15.own = f32[8,96,128]{2,1,0:T(8,128)S(1)} all-to-all(f32[8,96,128]{2,1,0:T(8,128)S(1)} %get-tuple-element.23), channel_id=1, replica_groups=mesh['gx'=16,'gy'=4,'gz'=8] {'gz'}, dimensions={0} | all-to-all | bytes 786432 | tf_op jit(solution)/shard_map/all_to_all | solution.py:660
  60.7 2.4 %collective-permute-start.7 = (f32[8,96,128]{2,1,0:T(8,128)S(1)}, f32[8,96,128]{2,1,0:T(8,128)S(1)}, u32[]{:S(2)}, u32[]{:S(2)}) collective-permute-start(f32[8,96,128]{2,1,0:T(8,128)S(1)} %all_to_all.15.own), channel_id=1, source_target_pairs={{32,0},{64,32},{96,64},{128,96},{160,128},{192,160},{224,192},{256... | collective-permute-start | bytes 1179656 | tf_op jit(solution)/shard_map/ppermute | solution.py:628
  63.1 1.1 collective-permute-start.6
  64.2 5.8 %collective-permute-done.7.xa = f32[8,96,128]{2,1,0:T(8,128)S(1)} collective-permute-done((f32[8,96,128]{2,1,0:T(8,128)S(1)}, f32[8,96,128]{2,1,0:T(8,128)S(1)}, u32[]{:S(2)}, u32[]{:S(2)}) %collective-permute-start.7) | collective-permute-done | bytes 393248 | tf_op jit(solution)/shard_map/ppermute | solution.py:628
  69.9 2.6 %pack1.1 = (f32[96,48,128]{2,1,0:T(8,128)S(1)}, f32[12,48,128]{2,1,0:T(8,128)S(1)}, f32[12,48,128]{2,1,0:T(8,128)S(1)}) custom-call(s32[4]{0:T(128)S(1)} %pad_add_fusion.pos, f32[8,96,128]{2,1,0:T(8,128)S(1)} %all_to_all.15.own, f32[8,96,128]{2,1,0:T(8,128)S(1)} %collective-permute-done.6.xb, f32[8,96,128]{2,1,0:T(8,128)S(1)} %collective-permute-done.7.xa), custom_call_target="tpu_custom_call" | custom-call | tf_op jit(solution)/shard_map/pack1/pallas_call | solution.py:613
  72.5 3.1 %collective-permute-start.8 = (f32[12,48,128]{2,1,0:T(8,128)S(1)}, f32[12,48,128]{2,1,0:T(8,128)S(1)}, u32[]{:S(2)}, u32[]{:S(2)}) collective-permute-start(f32[12,48,128]{2,1,0:T(8,128)S(1)} %get-tuple-element.25), channel_id=1, source_target_pairs={{0,8},{8,16},{16,24},{1,9},{9,17},{17,25},{2,10},{10,18},{18,26},{... | collective-permute-start | bytes 884744 | tf_op jit(solution)/shard_map/ppermute | solution.py:628
  75.7 1.3 %collective-permute-start.9 = (f32[12,48,128]{2,1,0:T(8,128)S(1)}, f32[12,48,128]{2,1,0:T(8,128)S(1)}, u32[]{:S(2)}, u32[]{:S(2)}) collective-permute-start(f32[12,48,128]{2,1,0:T(8,128)S(1)} %get-tuple-element.26), channel_id=1, source_target_pairs={{8,0},{16,8},{24,16},{9,1},{17,9},{25,17},{10,2},{18,10},{26,18},{... | collective-permute-start | bytes 884744 | tf_op jit(solution)/shard_map/ppermute | solution.py:628
  77.0 2.3 %collective-permute-done.8.before = f32[12,48,128]{2,1,0:T(8,128)S(1)} collective-permute-done((f32[12,48,128]{2,1,0:T(8,128)S(1)}, f32[12,48,128]{2,1,0:T(8,128)S(1)}, u32[]{:S(2)}, u32[]{:S(2)}) %collective-permute-start.8) | collective-permute-done | bytes 294944 | tf_op jit(solution)/shard_map/ppermute | solution.py:628
  79.3 3.8 %collective-permute-done.9.after = f32[12,48,128]{2,1,0:T(8,128)S(1)} collective-permute-done((f32[12,48,128]{2,1,0:T(8,128)S(1)}, f32[12,48,128]{2,1,0:T(8,128)S(1)}, u32[]{:S(2)}, u32[]{:S(2)}) %collective-permute-start.9) | collective-permute-done | bytes 294944 | tf_op jit(solution)/shard_map/ppermute | solution.py:628
  83.2 6.0 %down1.1 = (f32[16,16,128]{2,1,0:T(8,128)S(1)}, f32[6,40,48,128]{3,2,1,0:T(8,128)S(1)}, f32[40,48,128]{2,1,0:T(8,128)S(1)}, f32[40,48,128]{2,1,0:T(8,128)S(1)}, ...) custom-call(f32[96,48,128]{2,1,0:T(8,128)S(1)} %get-tuple-element.24.whole, ...), custom_call_target="tpu_custom_call" | custom-call | tf_op jit(solution)/shard_map/down1/pallas_call | solution.py:613
  89.2 19.2 %all_to_all.16 = f32[16,16,128]{2,1,0:T(8,128)S(1)} all-to-all(f32[16,16,128]{2,1,0:T(8,128)S(1)} %get-tuple-element.27), channel_id=1, replica_groups=mesh['gx'=16,'gy'=4,'gz'=8] {'gx'}, dimensions={0} | all-to-all | bytes 262144 | tf_op jit(solution)/shard_map/all_to_all | solution.py:683
  108.5 12.3 %all_to_all.17.gathered = f32[4,256,128]{2,1,0:T(8,128)S(1)} all-to-all(f32[4,256,128]{2,1,0:T(8,128)S(1)} %broadcast_in_dim.8), channel_id=1, replica_groups=mesh['gx'=16,'gy'=4,'gz'=8] {'gy'}, dimensions={0} | all-to-all | bytes 1048576 | tf_op jit(solution)/shard_map/all_to_all | solution.py:686
  120.8 6.9 %up.1 = (f32[8,32,128]{2,1,0:T(8,128)}, f32[8,32,128]{2,1,0:T(8,128)}) custom-call(s32[4]{0:T(128)S(1)} %pad_add_fusion.pos, f32[4,256,128]{2,1,0:T(8,128)S(1)} %all_to_all.17.gathered, f32[6,24,24,128]{3,2,1,0:T(8,128)S(1)} %get-tuple-element.28.weights2, f32[24,24,128]{2,1,0:T(8,128)S(1)} %get-tuple-element.29.scaled2, ...), custom_call_target="tpu_custom_call" | custom-call | tf_op jit(solution)/shard_map/up/pallas_call | solution.py:613
  (21 shorter events, 0.2 us)
Async XLA Ops:
  0.6 24.7 %copy-start.2 = (f32[8,32,128]{2,1,0:T(8,128)S(1)}, f32[8,32,128]{2,1,0:T(8,128)}, u32[]{:S(2)}) copy-start(f32[8,32,128]{2,1,0:T(8,128)} %f_ref.1) | copy-start | bytes 393220
  0.6 24.7 %copy-start.1 = (f32[8,32,128]{2,1,0:T(8,128)S(1)}, f32[8,32,128]{2,1,0:T(8,128)}, u32[]{:S(2)}) copy-start(f32[8,32,128]{2,1,0:T(8,128)} %b_ref.1) | copy-start | bytes 393220
  0.7 24.7 %copy-start = (f32[8,32,128]{2,1,0:T(8,128)S(1)}, f32[8,32,128]{2,1,0:T(8,128)}, u32[]{:S(2)}) copy-start(f32[8,32,128]{2,1,0:T(8,128)} %a_ref.1) | copy-start | bytes 393220
  2.7 8.5 %collective-permute-start = (f32[3,5,32,128]{3,2,1,0:T(8,128)S(1)}, f32[3,5,32,128]{3,2,1,0:T(8,128)S(1)}, u32[]{:S(2)}, u32[]{:S(2)}) collective-permute-start(f32[3,5,32,128]{3,2,1,0:T(8,128)S(1)} %pad_maximum_fusion), channel_id=1, source_target_pairs={{0,1},{1,2},{2,3},{3,4},{4,5},{5,6},{6,7},{8,9},{9,10},{10,11},{11... | collective-permute-start | bytes 737288 | tf_op jit(solution)/shard_map/ppermute | solution.py:628
  7.6 7.6 %collective-permute-start.1 = (f32[3,5,32,128]{3,2,1,0:T(8,128)S(1)}, f32[3,5,32,128]{3,2,1,0:T(8,128)S(1)}, u32[]{:S(2)}, u32[]{:S(2)}) collective-permute-start(f32[3,5,32,128]{3,2,1,0:T(8,128)S(1)} %pad_maximum_fusion.1), channel_id=1, source_target_pairs={{1,0},{2,1},{3,2},{4,3},{5,4},{6,5},{7,6},{9,8},{10,9},{11,10},{12... | collective-permute-start | bytes 737288 | tf_op jit(solution)/shard_map/ppermute | solution.py:628
  15.3 7.4 %collective-permute-start.2 = (f32[3,18,8,128]{3,2,1,0:T(8,128)S(1)}, f32[3,18,8,128]{3,2,1,0:T(8,128)S(1)}, u32[]{:S(2)}, u32[]{:S(2)}) collective-permute-start(f32[3,18,8,128]{3,2,1,0:T(8,128)S(1)} %pad_maximum_fusion.2), channel_id=1, source_target_pairs={{0,32},{32,64},{64,96},{96,128},{128,160},{160,192},{192,224},{224... | collective-permute-start | bytes 663560 | tf_op jit(solution)/shard_map/ppermute | solution.py:628
  19.8 5.5 %collective-permute-start.3 = (f32[3,18,8,128]{3,2,1,0:T(8,128)S(1)}, f32[3,18,8,128]{3,2,1,0:T(8,128)S(1)}, u32[]{:S(2)}, u32[]{:S(2)}) collective-permute-start(f32[3,18,8,128]{3,2,1,0:T(8,128)S(1)} %pad_maximum_fusion.3), channel_id=1, source_target_pairs={{32,0},{64,32},{96,64},{128,96},{160,128},{192,160},{224,192},{256... | collective-permute-start | bytes 663560 | tf_op jit(solution)/shard_map/ppermute | solution.py:628
  26.6 5.3 %collective-permute-start.4 = (f32[4,48,128]{2,1,0:T(8,128)S(1)}, f32[4,48,128]{2,1,0:T(8,128)S(1)}, u32[]{:S(2)}, u32[]{:S(2)}) collective-permute-start(f32[4,48,128]{2,1,0:T(8,128)S(1)} %get-tuple-element.21), channel_id=1, source_target_pairs={{0,8},{8,16},{16,24},{1,9},{9,17},{17,25},{2,10},{10,18},{18,26},{... | collective-permute-start | bytes 294920 | tf_op jit(solution)/shard_map/ppermute | solution.py:628
  29.6 6.0 %collective-permute-start.5 = (f32[4,48,128]{2,1,0:T(8,128)S(1)}, f32[4,48,128]{2,1,0:T(8,128)S(1)}, u32[]{:S(2)}, u32[]{:S(2)}) collective-permute-start(f32[4,48,128]{2,1,0:T(8,128)S(1)} %get-tuple-element.22), channel_id=1, source_target_pairs={{8,0},{16,8},{24,16},{9,1},{17,9},{25,17},{10,2},{18,10},{26,18},{... | collective-permute-start | bytes 294920 | tf_op jit(solution)/shard_map/ppermute | solution.py:628
  60.7 9.2 %collective-permute-start.7 = (f32[8,96,128]{2,1,0:T(8,128)S(1)}, f32[8,96,128]{2,1,0:T(8,128)S(1)}, u32[]{:S(2)}, u32[]{:S(2)}) collective-permute-start(f32[8,96,128]{2,1,0:T(8,128)S(1)} %all_to_all.15.own), channel_id=1, source_target_pairs={{32,0},{64,32},{96,64},{128,96},{160,128},{192,160},{224,192},{256... | collective-permute-start | bytes 1179656 | tf_op jit(solution)/shard_map/ppermute | solution.py:628
  63.1 6.8 %collective-permute-start.6 = (f32[8,96,128]{2,1,0:T(8,128)S(1)}, f32[8,96,128]{2,1,0:T(8,128)S(1)}, u32[]{:S(2)}, u32[]{:S(2)}) collective-permute-start(f32[8,96,128]{2,1,0:T(8,128)S(1)} %all_to_all.15.own), channel_id=1, source_target_pairs={{0,32},{32,64},{64,96},{96,128},{128,160},{160,192},{192,224},{224... | collective-permute-start | bytes 1179656 | tf_op jit(solution)/shard_map/ppermute | solution.py:628
  72.5 6.8 %collective-permute-start.8 = (f32[12,48,128]{2,1,0:T(8,128)S(1)}, f32[12,48,128]{2,1,0:T(8,128)S(1)}, u32[]{:S(2)}, u32[]{:S(2)}) collective-permute-start(f32[12,48,128]{2,1,0:T(8,128)S(1)} %get-tuple-element.25), channel_id=1, source_target_pairs={{0,8},{8,16},{16,24},{1,9},{9,17},{17,25},{2,10},{10,18},{18,26},{... | collective-permute-start | bytes 884744 | tf_op jit(solution)/shard_map/ppermute | solution.py:628
  75.7 7.5 %collective-permute-start.9 = (f32[12,48,128]{2,1,0:T(8,128)S(1)}, f32[12,48,128]{2,1,0:T(8,128)S(1)}, u32[]{:S(2)}, u32[]{:S(2)}) collective-permute-start(f32[12,48,128]{2,1,0:T(8,128)S(1)} %get-tuple-element.26), channel_id=1, source_target_pairs={{8,0},{16,8},{24,16},{9,1},{17,9},{25,17},{10,2},{18,10},{26,18},{... | collective-permute-start | bytes 884744 | tf_op jit(solution)/shard_map/ppermute | solution.py:628

commit v4 on v3

--- a/solution.py
+++ b/solution.py
@@ -88,6 +88,27 @@
         ref[index] = value
 
 
+def slices(depth):
+    wide, narrow = [], []
+    for index, reach in enumerate((DEEP - 2, DEEP - 2, DEEP - 3)):
+        for plane in range(depth):
+            (wide if reach <= plane < depth - reach else narrow).append((index, plane))
+    return wide, narrow
+
+
+def slots(depth):
+    wide, narrow = slices(depth)
+    out = [(index, plane, at // 4, 32 * (at % 4), 32) for at, (index, plane) in enumerate(wide)]
+    first = -(-len(wide) // 4)
+    return out + [(index, plane, first + at // 16, 8 * (at % 16), 8) for at, (index, plane) in enumerate(narrow)]
+
+
+def packz(f_ref, a_ref, b_ref, last, first):
+    for index, ref in enumerate((f_ref, a_ref, b_ref)):
+        last[index] = ref[ref.shape[0] - DEEP :]
+        first[index] = ref[:DEEP]
+
+
 def pack0(pos, f_ref, a_ref, b_ref, zb, za, xb, xa, whole, left, right):
     planes = f_ref.shape[0]
     has_before, has_after = pos[0] > 0, pos[0] < pos[3] - 1
@@ -97,28 +118,25 @@
         whole[index, DEEP + planes :, 0:32, :] = za[index]
         whole[index, :, 32:40, :] = jnp.where(has_after, xa[index], 0.0)
         whole[index, :, 40:48, :] = jnp.where(has_before, xb[index], 0.0)
-    depth = planes + 2 * DEEP
-    slot = lane_of((48, 128)) // 8
-    for tile in range(left.shape[0]):
-        low = high = jnp.zeros((48, 128), F32)
-        for place in range(min(16, 3 * depth - 16 * tile)):
-            index, plane = divmod(16 * tile + place, depth)
-            value = whole[index, plane]
-            low = jnp.where(slot == place, roll(value, 8 * place, 1), low)
-            high = jnp.where(slot == place, roll(value, 8 * place + 8, 1), high)
-        left[tile] = low
-        right[tile] = high
+    lane = lane_of((48, 128))
+    low, high = {}, {}
+    for index, plane, tile, to, lanes in slots(planes + 2 * DEEP):
+        value = whole[index, plane]
+        here = (lane >= to) & (lane < to + lanes)
+        zero = jnp.zeros((48, 128), F32)
+        low[tile] = jnp.where(here, roll(value, to, 1), low.get(tile, zero))
+        high[tile] = jnp.where(here, roll(value, to + lanes, 1), high.get(tile, zero))
+    for tile in low:
+        left[tile] = low[tile]
+        right[tile] = high[tile]
 
 
 def unpack0(whole, before, after, ext):
-    depth = whole.shape[1]
     lane = lane_of((48, 128))
-    for index in range(3):
-        for plane in range(depth):
-            tile, place = divmod(index * depth + plane, 16)
-            ahead = jnp.where(lane < 8, roll(after[tile], -8 * place, 1), 0.0)
-            ext[index, plane, :, 0:128] = whole[index, plane]
-            ext[index, plane, :, 128:256] = jnp.where(lane >= 120, roll(before[tile], 120 - 8 * place, 1), ahead)
+    for index, plane, tile, to, lanes in slots(whole.shape[1]):
+        ahead = jnp.where(lane < lanes, roll(after[tile], -to, 1), 0.0)
+        ext[index, plane, :, 0:128] = whole[index, plane]
+        ext[index, plane, :, 128:256] = jnp.where(lane >= 128 - lanes, roll(before[tile], -lanes - to, 1), ahead)
 
 
 def planes_of(count, level, start=0):
@@ -138,12 +156,12 @@
         scaled[plane] = ext[0, plane + 1] * inverse
 
 
-def residual0(weights, diagonal, scaled, value, below, above, at):
-    cut = lambda array: array[0:32, 0:128]
-    result = scaled[at, 0:32, 0:128] - cut(value)
+def residual0(weights, diagonal, scaled, value, below, above, at, lanes):
+    cut = lambda array: array[0:32, 0:lanes]
+    result = scaled[at, 0:32, 0:lanes] - cut(value)
     for index, other in enumerate([below, above] + sides(value)):
-        result = result + weights[index, at, 0:32, 0:128] * cut(other)
-    return diagonal[at, 0:32, 0:128] * result
+        result = result + weights[index, at, 0:32, 0:lanes] * cut(other)
+    return diagonal[at, 0:32, 0:lanes] * result
 
 
 def down0(whole, before, after, iterate, message, weights, diagonal, scaled, ext, start, sums):
@@ -170,60 +188,61 @@
 
     def left_over(plane):
         return residual0(
-            weights, diagonal, scaled, iterate[plane + 3], iterate[plane + 2], iterate[plane + 4], plane + 4
+            weights, diagonal, scaled, iterate[plane + 3], iterate[plane + 2], iterate[plane + 4], plane + 4, 256
         )
 
     half = planes // 2
 
     @planes_of(half, 0)
     def _(plane):
-        sums[plane] = left_over(2 * plane) + left_over(2 * plane + 1)
+        pairs = [left_over(2 * plane) + left_over(2 * plane + 1)]
         for index in (1, 2):
-            low = whole[index, DEEP + 2 * plane, 0:32, :]
-            sums[index * half + plane] = low + whole[index, DEEP + 2 * plane + 1, 0:32, :]
-
-    count = 3 * half
-    tall = [sums[plane, pl.ds(0, 16, stride=2), :] + sums[plane, pl.ds(1, 16, stride=2), :] for plane in range(count)]
-    first = jnp.concatenate([value[0:8] for value in tall], axis=0)
-    second = jnp.concatenate([value[8:16] for value in tall], axis=0)
-    pair = matrix((128, 128), lambda row, lane: lane == row // 2, 0.125)
-    other = matrix((128, 128), lambda row, lane: lane == row // 2 + 64, 0.125)
-    copies(message, dot(first, pair) + dot(second, other))
-
-
-def pack1(pos, own, xb, xa, whole, left, right):
+            low = ext[index, DEEP + 2 * plane, 0:32, :]
+            pairs.append(low + ext[index, DEEP + 2 * plane + 1, 0:32, :])
+        for index, value in enumerate(pairs):
+            sums[0, index * half + plane] = value[:, 0:128]
+            sums[1, index * half + plane] = value[:, 128:256]
+
+    def rows_of(side, places):
+        tall = [
+            sums[side, place, pl.ds(0, 16, stride=2), :] + sums[side, place, pl.ds(1, 16, stride=2), :]
+            for place in places
+        ]
+        return jnp.concatenate(tall, axis=0)
+
+    even = matrix((128, 128), lambda row, lane: lane == row // 2, 0.125)
+    odd = matrix((128, 128), lambda row, lane: lane == row // 2 + 64, 0.125)
+    middle = dot(rows_of(0, range(0, 3 * half, 2)), even) + dot(rows_of(0, range(1, 3 * half, 2)), odd)
+    ends = None
+    for plane in range(half):
+
+        def rule(row, lane, to=32 * plane):
+            ahead = (row < 32) & (lane == to + row // 2)
+            return ahead | ((row >= 96) & (lane == to + 16 + (row - 96) // 2))
+
+        got = dot(rows_of(1, range(plane, 3 * half, half)), matrix((128, 128), rule, 0.125))
+        ends = got if ends is None else ends + got
+    copies(message, jnp.concatenate([middle, ends], axis=0))
+
+
+def unpack1(pos, own, xb, xa, ext):
     has_before, has_after = pos[0] > 0, pos[0] < pos[3] - 1
-    lane = lane_of((8, 128))
-    sources, rows = own.shape[0], own.shape[1]
-    per = rows // 24
-    depth = sources * per
-
-    def spread(value):
-        return jnp.where(lane < 64, value, 0.0), jnp.where(lane < 64, roll(value, 64, 1), 0.0)
-
-    @pl.loop(0, sources, unroll=2)
+    lane = lane_of((16, 128))
+    per = own.shape[1] // 36
+
+    @pl.loop(0, own.shape[0], unroll=2)
     def _(source):
-        for index in range(3):
-            for plane in range(per):
-                at = (index * per + plane) * 8
-                to = index * depth + source * per + plane
-                whole[to, 0:8, :], whole[to, 8:16, :] = spread(own[source, at : at + 8, :])
-                value = jnp.where(has_after, xa[source, at : at + 8, :], 0.0)
-                whole[to, 16:24, :], whole[to, 24:32, :] = spread(value)
-                value = jnp.where(has_before, xb[source, at : at + 8, :], 0.0)
-                whole[to, 32:40, :], whole[to, 40:48, :] = spread(value)
-
-    slot = lane_of((48, 128)) // 16
-
-    @pl.loop(0, left.shape[0], unroll=2)
-    def _(tile):
-        low = high = jnp.zeros((48, 128), F32)
-        for place in range(8):
-            value = whole[8 * tile + place]
-            low = jnp.where(slot == place, roll(value, 16 * place, 1), low)
-            high = jnp.where(slot == place, roll(value, 16 * place - 48, 1), high)
-        left[tile] = low
-        right[tile] = high
+        for block, (ref, there) in enumerate(((own, None), (xa, has_after), (xb, has_before))):
+            for index in range(3):
+                ends = ref[source, 96 + 16 * index : 112 + 16 * index, :]
+                for plane in range(per):
+                    at = (2 * index + plane // 2) * 16
+                    value = roll(ref[source, at : at + 16, :], 64 * (plane % 2), 1)
+                    value = jnp.where(lane < 80, jnp.where(lane < 64, value, roll(ends, 64 - 32 * plane, 1)), 0.0)
+                    value = jnp.where(lane >= 112, roll(ends, 96 - 32 * plane, 1), value)
+                    if there is not None:
+                        value = jnp.where(there, value, 0.0)
+                    ext[index, 4 + source * per + plane, 16 * block : 16 * block + 16, :] = value
 
 
 def pass_all(weights, scaled, value, out, count, combine, level):
@@ -259,26 +278,16 @@
 
 
 def down1(
-    whole, before, after, message, weights1, scaled1, iterate1, weights2, scaled2, iterate2,
+    pos, own, xb, xa, message, weights1, scaled1, iterate1, weights2, scaled2, iterate2,
     ext1, diagonal1, start1, sums1, ext2, diagonal2, start2, sums2, thin, thick,
 ):
-    depth = whole.shape[0] // 3
-    lane = lane_of((48, 128))
+    depth = scaled1.shape[0] - 8
     for index in range(3):
         for end in (0, depth + 4):
             for plane in range(4):
                 ext1[index, end + plane] = jnp.zeros((48, 128), F32)
 
-    @pl.loop(0, before.shape[0], unroll=2)
-    def _(tile):
-        for place in range(8):
-            at = 8 * tile + place
-            index, plane = at // depth, lax.rem(at, depth)
-            value = whole[at]
-            value = jnp.where((lane >= 64) & (lane < 80), roll(after[tile], 64 - 16 * place, 1), value)
-            value = jnp.where(lane >= 112, roll(before[tile], 112 - 16 * place, 1), value)
-            ext1[index, plane + 4] = value
-
+    unpack1(pos, own, xb, xa, ext1)
     prepare(ext1, weights1, diagonal1, scaled1, 1)
     start1[0] = jnp.zeros((48, 128), F32)
     start1[depth + 1] = jnp.zeros((48, 128), F32)
@@ -602,7 +611,7 @@
         value = out0[plane + 1]
         solved[plane] = value[0:32, 0:128]
         left_over[plane] = residual0(
-            weights0, diagonal0, scaled0, value, out0[plane], out0[plane + 2], plane + 4
+            weights0, diagonal0, scaled0, value, out0[plane], out0[plane + 2], plane + 4, 128
         )
 
 
@@ -634,14 +643,14 @@
     planes = right_side.shape[0]
     arrays = (right_side, acoef, beta)
 
-    last = jnp.stack([value[planes - DEEP :] for value in arrays])
-    first = jnp.stack([value[:DEEP] for value in arrays])
+    shape = (3, DEEP) + right_side.shape[1:]
+    last, first = call(packz, "packz", [shape, shape], [], None, arrays)
     zb, za = exchange(last, first, "gz", False)
     last = jnp.stack([jnp.concatenate([zb[i, :, 24:], arrays[i][:, 24:], za[i, :, 24:]]) for i in range(3)])
     first = jnp.stack([jnp.concatenate([zb[i, :, :8], arrays[i][:, :8], za[i, :, :8]]) for i in range(3)])
     xb, xa = exchange(last, first, "gx", True)
     depth = planes + 2 * DEEP
-    tiles = -(-3 * depth // 16)
+    tiles = max(tile for _, _, tile, _, _ in slots(depth)) + 1
     whole0, left, right = call(
         pack0, "pack0", [(3, depth, 48, 128)] + [(tiles, 48, 128)] * 2, [], pos, arrays + (zb, za, xb, xa)
     )
@@ -651,8 +660,8 @@
     iterate0, message, weights0, diagonal0, scaled0 = call(
         down0,
         "down0",
-        [(depth - 4,) + plane0, (files, 3 * half * 8, 128), (6, depth - 2) + plane0] + [(depth - 2,) + plane0] * 2,
-        [(3, depth) + plane0, (depth - 2,) + plane0, (3 * half, 32, 128)],
+        [(depth - 4,) + plane0, (files, 36 * half, 128), (6, depth - 2) + plane0] + [(depth - 2,) + plane0] * 2,
+        [(3, depth) + plane0, (depth - 2,) + plane0, (2, 3 * half, 32, 128)],
         None,
         (whole0, before0, after0),
     )
@@ -660,11 +669,6 @@
     own = lax.all_to_all(message, "gz", 0, 0)
     xb, xa = exchange(own, own, "gx", True)
     depth1 = files * half
-    tiles = 3 * depth1 // 8
-    whole1, left, right = call(
-        pack1, "pack1", [(3 * depth1, 48, 128)] + [(tiles, 48, 128)] * 2, [], pos, (own, xb, xa)
-    )
-    before1, after1 = exchange(right, left, "gy", False)
     plane1, plane2 = (48, 128), (24, 128)
     depth2 = depth1 // 2
     group = depth2 // 4
@@ -676,8 +680,8 @@
         [(3,) + tall1, tall1, (depth1 + 2,) + plane1, (3 * depth2,) + plane1]
         + [(3,) + tall2, tall2, (depth2 + 2,) + plane2, (3 * depth2 // 2, 8, 128)]
         + [(3 * depth2,) + plane2, (6, 4 * group, 128)],
-        None,
-        (whole1, before1, after1),
+        pos,
+        (own, xb, xa),
     )
 
     gathered = lax.all_to_all(message, "gx", 0, 0)

time: 128 us -> 126 us (0.984)
  starting transfers between devices: 22.9 us -> 18.8 us
  Pallas kernels: 20.1 us -> 17.5 us
  waiting for transfers between devices: 25.9 us -> 27.9 us
  blocking collectives: 53.3 us -> 55.2 us
    unnamed x6 -> x12, local copies, waits for them, and re-layouts: 0.02 us -> 5.42 us
    all_to_all x1, blocking collectives: 21.8 us -> 25.7 us  [on_device(): own = lax.all_to_all(message, 'gz', 0, 0)]
    ppermute x5 -> x4, starting transfers between devices: 16.6 us -> 13.4 us  [exchange(): lax.ppermute(up_values, axis, up_pairs)]
    ppermute x5 -> x4, waiting for transfers between devices: 5.99 us -> 9.1 us  [exchange(): lax.ppermute(up_values, axis, up_pairs)]
    all_to_all x1, blocking collectives: 19.2 us -> 16.4 us  [on_device(): gathered = lax.all_to_all(message, 'gx', 0, 0)]
    pallas_call x5, Pallas kernels: 20.1 us -> 17.5 us  [call(): pl.pallas_call(body, name=name, out_shape=[jax.ShapeDtypeStruct(shape, F3...]
    slice x3, local copies, waits for them, and re-layouts: 2.34 us -> 0.02 us  [on_device(): arrays[i][:, :8]]
    another operation x2 -> x0, local copies, waits for them, and re-layouts: 2.05 us -> none  [on_device(): first = jnp.stack([value[:DEEP] for value in arrays])]
  transfers between devices with their start and end apart: 10 -> 8, of which waited for: 8 -> 7; matrix products, arithmetic and copies ran while one was open for 2% -> 0% of each run, Pallas kernels for 0% -> 0%
where the time goes in v4:
time: 126 us
  blocking collectives  55.2 us (44%)
  waiting for transfers between devices  27.9 us (22%)
  starting transfers between devices  18.8 us (15%)
  Pallas kernels  17.5 us (14%)
  local copies, waits for them, and re-layouts  5.49 us (4%)
    all_to_all x1, blocking collectives, on_device(): own = lax.all_to_all(message, 'gz', 0, 0)  25.7 us
    ppermute x4, waiting for transfers between devices, exchange(): lax.ppermute(down_values, axis, down_pairs)  18.8 us
    pallas_call x5, Pallas kernels, call(): pl.pallas_call(body, name=name, out_shape=[jax.ShapeDtypeStruct(shape, F3...  17.5 us
    all_to_all x1, blocking collectives, on_device(): gathered = lax.all_to_all(message, 'gx', 0, 0)  16.4 us
    ppermute x4, starting transfers between devices, exchange(): lax.ppermute(up_values, axis, up_pairs)  13.4 us
    all_to_all x1, blocking collectives, on_device(): gathered = lax.all_to_all(gathered, 'gy', 0, 0)  13.2 us
    ppermute x4, waiting for transfers between devices, exchange(): lax.ppermute(up_values, axis, up_pairs)  9.1 us
    unnamed x12, local copies, waits for them, and re-layouts  5.42 us
  transfers between devices with their start and end apart: 8, of which 7 were waited for; matrix products, arithmetic and copies ran while one was open for 0% of the time, Pallas kernels for 0%

profile of v4, /device:TPU:1, one launch (start us, length us, event | category | flops | bytes accessed | tf_op | source)
XLA Modules:
  0.0 125.9 jit_solution(1060390600767988202)
XLA Ops:
  0.6 0.0 copy-start
  0.6 0.9 copy-done
  1.5 0.0 copy-start.2
  1.5 0.9 copy-done.2
  2.4 0.9 copy-done.4
  3.4 4.8 %collective-permute-start = (f32[3,5,32,128]{3,2,1,0:T(8,128)S(1)}, f32[3,5,32,128]{3,2,1,0:T(8,128)S(1)}, u32[]{:S(2)}, u32[]{:S(2)}) collective-permute-start(f32[3,5,32,128]{3,2,1,0:T(8,128)S(1)} %get-tuple-element.19), channel_id=1, source_target_pairs={{0,1},{1,2},{2,3},{3,4},{4,5},{5,6},{6,7},{8,9},{9,10},{10,11},{11... | collective-permute-start | bytes 737288 | tf_op jit(solution)/shard_map/ppermute | solution.py:637
  8.2 1.3 %collective-permute-start.1 = (f32[3,5,32,128]{3,2,1,0:T(8,128)S(1)}, f32[3,5,32,128]{3,2,1,0:T(8,128)S(1)}, u32[]{:S(2)}, u32[]{:S(2)}) collective-permute-start(f32[3,5,32,128]{3,2,1,0:T(8,128)S(1)} %get-tuple-element.20), channel_id=1, source_target_pairs={{1,0},{2,1},{3,2},{4,3},{5,4},{6,5},{7,6},{9,8},{10,9},{11,10},{12... | collective-permute-start | bytes 737288 | tf_op jit(solution)/shard_map/ppermute | solution.py:637
  9.6 1.8 %collective-permute-done.zb = f32[3,5,32,128]{3,2,1,0:T(8,128)S(1)} collective-permute-done((f32[3,5,32,128]{3,2,1,0:T(8,128)S(1)}, f32[3,5,32,128]{3,2,1,0:T(8,128)S(1)}, u32[]{:S(2)}, u32[]{:S(2)}) %collective-permute-start) | collective-permute-done | bytes 245792 | tf_op jit(solution)/shard_map/ppermute | solution.py:637
  11.4 4.4 %collective-permute-done.1.za = f32[3,5,32,128]{3,2,1,0:T(8,128)S(1)} collective-permute-done((f32[3,5,32,128]{3,2,1,0:T(8,128)S(1)}, f32[3,5,32,128]{3,2,1,0:T(8,128)S(1)}, u32[]{:S(2)}, u32[]{:S(2)}) %collective-permute-start.1) | collective-permute-done | bytes 245792 | tf_op jit(solution)/shard_map/ppermute | solution.py:637
  15.9 4.5 %collective-permute-start.2 = (f32[3,18,8,128]{3,2,1,0:T(8,128)S(1)}, f32[3,18,8,128]{3,2,1,0:T(8,128)S(1)}, u32[]{:S(2)}, u32[]{:S(2)}) collective-permute-start(f32[3,18,8,128]{3,2,1,0:T(8,128)S(1)} %pad_maximum_fusion), channel_id=1, source_target_pairs={{0,32},{32,64},{64,96},{96,128},{128,160},{160,192},{192,224},{224... | collective-permute-start | bytes 663560 | tf_op jit(solution)/shard_map/ppermute | solution.py:637
  20.4 0.0 collective-permute-start.3
  20.5 0.1 pad_add_fusion.pos
  20.5 2.7 %collective-permute-done.2.xb = f32[3,18,8,128]{3,2,1,0:T(8,128)S(1)} collective-permute-done((f32[3,18,8,128]{3,2,1,0:T(8,128)S(1)}, f32[3,18,8,128]{3,2,1,0:T(8,128)S(1)}, u32[]{:S(2)}, u32[]{:S(2)}) %collective-permute-start.2) | collective-permute-done | bytes 221216 | tf_op jit(solution)/shard_map/ppermute | solution.py:637
  23.3 2.7 %collective-permute-done.3.xa = f32[3,18,8,128]{3,2,1,0:T(8,128)S(1)} collective-permute-done((f32[3,18,8,128]{3,2,1,0:T(8,128)S(1)}, f32[3,18,8,128]{3,2,1,0:T(8,128)S(1)}, u32[]{:S(2)}, u32[]{:S(2)}) %collective-permute-start.3) | collective-permute-done | bytes 221216 | tf_op jit(solution)/shard_map/ppermute | solution.py:637
  25.9 0.9 copy-done.1
  26.8 0.9 copy-done.3
  27.7 0.9 copy-done.5
  28.6 1.2 pack0.1
  29.8 3.0 %collective-permute-start.4 = (f32[11,48,128]{2,1,0:T(8,128)S(1)}, f32[11,48,128]{2,1,0:T(8,128)S(1)}, u32[]{:S(2)}, u32[]{:S(2)}) collective-permute-start(f32[11,48,128]{2,1,0:T(8,128)S(1)} %get-tuple-element.22), channel_id=1, source_target_pairs={{0,8},{8,16},{16,24},{1,9},{9,17},{17,25},{2,10},{10,18},{18,26},{... | collective-permute-start | bytes 811016 | tf_op jit(solution)/shard_map/ppermute | solution.py:637
  32.8 1.3 %collective-permute-start.5 = (f32[11,48,128]{2,1,0:T(8,128)S(1)}, f32[11,48,128]{2,1,0:T(8,128)S(1)}, u32[]{:S(2)}, u32[]{:S(2)}) collective-permute-start(f32[11,48,128]{2,1,0:T(8,128)S(1)} %get-tuple-element.23), channel_id=1, source_target_pairs={{8,0},{16,8},{24,16},{9,1},{17,9},{25,17},{10,2},{18,10},{26,18},{... | collective-permute-start | bytes 811016 | tf_op jit(solution)/shard_map/ppermute | solution.py:637
  34.1 4.6 %collective-permute-done.4.before = f32[11,48,128]{2,1,0:T(8,128)S(1)} collective-permute-done((f32[11,48,128]{2,1,0:T(8,128)S(1)}, f32[11,48,128]{2,1,0:T(8,128)S(1)}, u32[]{:S(2)}, u32[]{:S(2)}) %collective-permute-start.4) | collective-permute-done | bytes 270368 | tf_op jit(solution)/shard_map/ppermute | solution.py:637
  38.7 3.8 %collective-permute-done.5.after = f32[11,48,128]{2,1,0:T(8,128)S(1)} collective-permute-done((f32[11,48,128]{2,1,0:T(8,128)S(1)}, f32[11,48,128]{2,1,0:T(8,128)S(1)}, u32[]{:S(2)}, u32[]{:S(2)}) %collective-permute-start.5) | collective-permute-done | bytes 270368 | tf_op jit(solution)/shard_map/ppermute | solution.py:637
  42.5 3.3 %down0.1 = (f32[14,48,256]{2,1,0:T(8,128)S(1)}, f32[8,144,128]{2,1,0:T(8,128)S(1)}, f32[6,16,48,256]{3,2,1,0:T(8,128)S(1)}, f32[16,48,256]{2,1,0:T(8,128)S(1)}, f32[16,48,256]{2,1,0:T(8,128)S(1)}) custom-call(f32[3,18,48,128]{3,2,1,0:T(8,128)S(1)} %get-tuple-element.21.whole, f32[11,48,128]{2,1,0:T(8,128)S(1)} %collective-permute-done.4.before, ...), custom_call_target="tpu_custom_call" | custom-call | tf_op jit(solution)/shard_map/down0/pallas_call | solution.py:622
  45.9 25.7 %all_to_all.15.own = f32[8,144,128]{2,1,0:T(8,128)S(1)} all-to-all(f32[8,144,128]{2,1,0:T(8,128)S(1)} %get-tuple-element.24), channel_id=1, replica_groups=mesh['gx'=16,'gy'=4,'gz'=8] {'gz'}, dimensions={0} | all-to-all | bytes 1179648 | tf_op jit(solution)/shard_map/all_to_all | solution.py:669
  71.5 2.8 %collective-permute-start.7 = (f32[8,144,128]{2,1,0:T(8,128)S(1)}, f32[8,144,128]{2,1,0:T(8,128)S(1)}, u32[]{:S(2)}, u32[]{:S(2)}) collective-permute-start(f32[8,144,128]{2,1,0:T(8,128)S(1)} %all_to_all.15.own), channel_id=1, source_target_pairs={{32,0},{64,32},{96,64},{128,96},{160,128},{192,160},{224,192},{256... | collective-permute-start | bytes 1769480 | tf_op jit(solution)/shard_map/ppermute | solution.py:637
  74.3 1.1 collective-permute-start.6
  75.4 7.9 %collective-permute-done.7.xa = f32[8,144,128]{2,1,0:T(8,128)S(1)} collective-permute-done((f32[8,144,128]{2,1,0:T(8,128)S(1)}, f32[8,144,128]{2,1,0:T(8,128)S(1)}, u32[]{:S(2)}, u32[]{:S(2)}) %collective-permute-start.7) | collective-permute-done | bytes 589856 | tf_op jit(solution)/shard_map/ppermute | solution.py:637
  83.2 0.0 collective-permute-done.6.xb
  83.2 6.1 %down1.1 = (f32[16,16,128]{2,1,0:T(8,128)S(1)}, f32[6,40,48,128]{3,2,1,0:T(8,128)S(1)}, f32[40,48,128]{2,1,0:T(8,128)S(1)}, f32[40,48,128]{2,1,0:T(8,128)S(1)}, ...) custom-call(s32[4]{0:T(128)S(1)} %pad_add_fusion.pos, ...), custom_call_target="tpu_custom_call" | custom-call | tf_op jit(solution)/shard_map/down1/pallas_call | solution.py:622
  89.3 16.4 %all_to_all.16 = f32[16,16,128]{2,1,0:T(8,128)S(1)} all-to-all(f32[16,16,128]{2,1,0:T(8,128)S(1)} %get-tuple-element.25), channel_id=1, replica_groups=mesh['gx'=16,'gy'=4,'gz'=8] {'gx'}, dimensions={0} | all-to-all | bytes 262144 | tf_op jit(solution)/shard_map/all_to_all | solution.py:687
  105.7 13.2 %all_to_all.17.gathered = f32[4,256,128]{2,1,0:T(8,128)S(1)} all-to-all(f32[4,256,128]{2,1,0:T(8,128)S(1)} %broadcast_in_dim.8), channel_id=1, replica_groups=mesh['gx'=16,'gy'=4,'gz'=8] {'gy'}, dimensions={0} | all-to-all | bytes 1048576 | tf_op jit(solution)/shard_map/all_to_all | solution.py:690
  119.0 6.9 %up.1 = (f32[8,32,128]{2,1,0:T(8,128)}, f32[8,32,128]{2,1,0:T(8,128)}) custom-call(s32[4]{0:T(128)S(1)} %pad_add_fusion.pos, f32[4,256,128]{2,1,0:T(8,128)S(1)} %all_to_all.17.gathered, f32[6,24,24,128]{3,2,1,0:T(8,128)S(1)} %get-tuple-element.26.weights2, f32[24,24,128]{2,1,0:T(8,128)S(1)} %get-tuple-element.27.scaled2, ...), custom_call_target="tpu_custom_call" | custom-call | tf_op jit(solution)/shard_map/up/pallas_call | solution.py:622
  (17 shorter events, 0.2 us)
Async XLA Ops:
  0.6 0.9 copy-start
  1.5 0.9 copy-start.2
  2.4 0.9 copy-start.4
  3.4 8.0 %collective-permute-start = (f32[3,5,32,128]{3,2,1,0:T(8,128)S(1)}, f32[3,5,32,128]{3,2,1,0:T(8,128)S(1)}, u32[]{:S(2)}, u32[]{:S(2)}) collective-permute-start(f32[3,5,32,128]{3,2,1,0:T(8,128)S(1)} %get-tuple-element.19), channel_id=1, source_target_pairs={{0,1},{1,2},{2,3},{3,4},{4,5},{5,6},{6,7},{8,9},{9,10},{10,11},{11... | collective-permute-start | bytes 737288 | tf_op jit(solution)/shard_map/ppermute | solution.py:637
  8.2 7.6 %collective-permute-start.1 = (f32[3,5,32,128]{3,2,1,0:T(8,128)S(1)}, f32[3,5,32,128]{3,2,1,0:T(8,128)S(1)}, u32[]{:S(2)}, u32[]{:S(2)}) collective-permute-start(f32[3,5,32,128]{3,2,1,0:T(8,128)S(1)} %get-tuple-element.20), channel_id=1, source_target_pairs={{1,0},{2,1},{3,2},{4,3},{5,4},{6,5},{7,6},{9,8},{10,9},{11,10},{12... | collective-permute-start | bytes 737288 | tf_op jit(solution)/shard_map/ppermute | solution.py:637
  15.9 7.4 %collective-permute-start.2 = (f32[3,18,8,128]{3,2,1,0:T(8,128)S(1)}, f32[3,18,8,128]{3,2,1,0:T(8,128)S(1)}, u32[]{:S(2)}, u32[]{:S(2)}) collective-permute-start(f32[3,18,8,128]{3,2,1,0:T(8,128)S(1)} %pad_maximum_fusion), channel_id=1, source_target_pairs={{0,32},{32,64},{64,96},{96,128},{128,160},{160,192},{192,224},{224... | collective-permute-start | bytes 663560 | tf_op jit(solution)/shard_map/ppermute | solution.py:637
  20.4 5.5 %collective-permute-start.3 = (f32[3,18,8,128]{3,2,1,0:T(8,128)S(1)}, f32[3,18,8,128]{3,2,1,0:T(8,128)S(1)}, u32[]{:S(2)}, u32[]{:S(2)}) collective-permute-start(f32[3,18,8,128]{3,2,1,0:T(8,128)S(1)} %pad_maximum_fusion.1), channel_id=1, source_target_pairs={{32,0},{64,32},{96,64},{128,96},{160,128},{192,160},{224,192},{256... | collective-permute-start | bytes 663560 | tf_op jit(solution)/shard_map/ppermute | solution.py:637
  25.9 0.9 copy-start.1
  26.8 0.9 copy-start.3
  27.7 0.9 copy-start.5
  29.8 8.9 %collective-permute-start.4 = (f32[11,48,128]{2,1,0:T(8,128)S(1)}, f32[11,48,128]{2,1,0:T(8,128)S(1)}, u32[]{:S(2)}, u32[]{:S(2)}) collective-permute-start(f32[11,48,128]{2,1,0:T(8,128)S(1)} %get-tuple-element.22), channel_id=1, source_target_pairs={{0,8},{8,16},{16,24},{1,9},{9,17},{17,25},{2,10},{10,18},{18,26},{... | collective-permute-start | bytes 811016 | tf_op jit(solution)/shard_map/ppermute | solution.py:637
  32.8 9.7 %collective-permute-start.5 = (f32[11,48,128]{2,1,0:T(8,128)S(1)}, f32[11,48,128]{2,1,0:T(8,128)S(1)}, u32[]{:S(2)}, u32[]{:S(2)}) collective-permute-start(f32[11,48,128]{2,1,0:T(8,128)S(1)} %get-tuple-element.23), channel_id=1, source_target_pairs={{8,0},{16,8},{24,16},{9,1},{17,9},{25,17},{10,2},{18,10},{26,18},{... | collective-permute-start | bytes 811016 | tf_op jit(solution)/shard_map/ppermute | solution.py:637
  71.5 11.7 %collective-permute-start.7 = (f32[8,144,128]{2,1,0:T(8,128)S(1)}, f32[8,144,128]{2,1,0:T(8,128)S(1)}, u32[]{:S(2)}, u32[]{:S(2)}) collective-permute-start(f32[8,144,128]{2,1,0:T(8,128)S(1)} %all_to_all.15.own), channel_id=1, source_target_pairs={{32,0},{64,32},{96,64},{128,96},{160,128},{192,160},{224,192},{256... | collective-permute-start | bytes 1769480 | tf_op jit(solution)/shard_map/ppermute | solution.py:637
  74.3 8.9 %collective-permute-start.6 = (f32[8,144,128]{2,1,0:T(8,128)S(1)}, f32[8,144,128]{2,1,0:T(8,128)S(1)}, u32[]{:S(2)}, u32[]{:S(2)}) collective-permute-start(f32[8,144,128]{2,1,0:T(8,128)S(1)} %all_to_all.15.own), channel_id=1, source_target_pairs={{0,32},{32,64},{64,96},{96,128},{128,160},{160,192},{192,224},{224... | collective-permute-start | bytes 1769480 | tf_op jit(solution)/shard_map/ppermute | solution.py:637

commit v5 on v4

--- a/solution.py
+++ b/solution.py
@@ -18,6 +18,7 @@
 
 F32 = jnp.float32
 AXES = ("gx", "gy", "gz")
+REACH = (4, 4, 5)
 DEEP = 5
 
 
@@ -88,42 +89,56 @@
         ref[index] = value
 
 
-def slices(depth):
+def away(plane, depth):
+    return max(DEEP - plane, plane - (depth - 1 - DEEP), 0)
+
+
+def slots(depth):
     wide, narrow = [], []
-    for index, reach in enumerate((DEEP - 2, DEEP - 2, DEEP - 3)):
+    for index, reach in enumerate(REACH):
         for plane in range(depth):
-            (wide if reach <= plane < depth - reach else narrow).append((index, plane))
-    return wide, narrow
-
-
-def slots(depth):
-    wide, narrow = slices(depth)
+            if away(plane, depth) < reach:
+                (wide if away(plane, depth) <= reach - 2 else narrow).append((index, plane))
     out = [(index, plane, at // 4, 32 * (at % 4), 32) for at, (index, plane) in enumerate(wide)]
     first = -(-len(wide) // 4)
     return out + [(index, plane, first + at // 16, 8 * (at % 16), 8) for at, (index, plane) in enumerate(narrow)]
 
 
-def packz(f_ref, a_ref, b_ref, last, first):
-    for index, ref in enumerate((f_ref, a_ref, b_ref)):
-        last[index] = ref[ref.shape[0] - DEEP :]
-        first[index] = ref[:DEEP]
-
-
-def pack0(pos, f_ref, a_ref, b_ref, zb, za, xb, xa, whole, left, right):
-    planes = f_ref.shape[0]
+def packx(own, zb, za, last, first):
+    planes, at = own.shape[1], 0
+    for index, reach in enumerate(REACH):
+        for value in (zb[index, DEEP - reach + 1 :], own[index], za[index, : reach - 1]):
+            last[at : at + value.shape[0]] = value[:, 24:]
+            first[at : at + value.shape[0]] = value[:, :8]
+            at += value.shape[0]
+
+
+def pack0(pos, own, zb, za, xb, xa, whole, left, right):
+    planes = own.shape[1]
+    depth = planes + 2 * DEEP
     has_before, has_after = pos[0] > 0, pos[0] < pos[3] - 1
-    for index, ref in enumerate((f_ref, a_ref, b_ref)):
-        whole[index, 0:DEEP, 0:32, :] = zb[index]
-        whole[index, DEEP : DEEP + planes, 0:32, :] = ref[...]
-        whole[index, DEEP + planes :, 0:32, :] = za[index]
-        whole[index, :, 32:40, :] = jnp.where(has_after, xa[index], 0.0)
-        whole[index, :, 40:48, :] = jnp.where(has_before, xb[index], 0.0)
-    lane = lane_of((48, 128))
+    at_x = 0
+    for index, reach in enumerate(REACH):
+        for plane in range(DEEP - reach):
+            for end in (plane, depth - 1 - plane):
+                whole[index, end] = jnp.zeros((48, 128), F32)
+        whole[index, DEEP - reach : DEEP, 0:32, :] = zb[index, DEEP - reach :]
+        whole[index, DEEP : DEEP + planes, 0:32, :] = own[index]
+        whole[index, DEEP + planes : DEEP + planes + reach, 0:32, :] = za[index, :reach]
+        for plane in (DEEP - reach, DEEP + planes + reach - 1):
+            whole[index, plane, 32:48, :] = jnp.zeros((16, 128), F32)
+        inner, count = DEEP - reach + 1, planes + 2 * reach - 2
+        whole[index, inner : inner + count, 32:40, :] = jnp.where(has_after, xa[at_x : at_x + count], 0.0)
+        whole[index, inner : inner + count, 40:48, :] = jnp.where(has_before, xb[at_x : at_x + count], 0.0)
+        at_x += count
+    lane = lane_of((40, 128))
+    four = row_of((8, 128)) < 4
     low, high = {}, {}
-    for index, plane, tile, to, lanes in slots(planes + 2 * DEEP):
-        value = whole[index, plane]
+    for index, plane, tile, to, lanes in slots(depth):
+        ends = jnp.where(four, whole[index, plane, 32:40, :], whole[index, plane, 40:48, :])
+        value = jnp.concatenate([whole[index, plane, 0:32, :], ends], axis=0)
         here = (lane >= to) & (lane < to + lanes)
-        zero = jnp.zeros((48, 128), F32)
+        zero = jnp.zeros((40, 128), F32)
         low[tile] = jnp.where(here, roll(value, to, 1), low.get(tile, zero))
         high[tile] = jnp.where(here, roll(value, to + lanes, 1), high.get(tile, zero))
     for tile in low:
@@ -132,11 +147,20 @@
 
 
 def unpack0(whole, before, after, ext):
-    lane = lane_of((48, 128))
-    for index, plane, tile, to, lanes in slots(whole.shape[1]):
-        ahead = jnp.where(lane < lanes, roll(after[tile], -to, 1), 0.0)
-        ext[index, plane, :, 0:128] = whole[index, plane]
-        ext[index, plane, :, 128:256] = jnp.where(lane >= 128 - lanes, roll(before[tile], -lanes - to, 1), ahead)
+    depth = whole.shape[1]
+    ext[:, :, :, 0:128] = whole[...]
+    lane = lane_of((40, 128))
+    there = {(index, plane): rest for index, plane, *rest in slots(depth)}
+    for index in range(3):
+        for plane in range(depth):
+            if (index, plane) not in there:
+                ext[index, plane, :, 128:256] = jnp.zeros((48, 128), F32)
+                continue
+            tile, to, lanes = there[index, plane]
+            ahead = jnp.where(lane < lanes, roll(after[tile], -to, 1), 0.0)
+            value = jnp.where(lane >= 128 - lanes, roll(before[tile], -lanes - to, 1), ahead)
+            ext[index, plane, 0:40, 128:256] = value
+            ext[index, plane, 40:48, 128:256] = value[32:40]
 
 
 def planes_of(count, level, start=0):
@@ -643,16 +667,17 @@
     planes = right_side.shape[0]
     arrays = (right_side, acoef, beta)
 
-    shape = (3, DEEP) + right_side.shape[1:]
-    last, first = call(packz, "packz", [shape, shape], [], None, arrays)
+    last = jnp.stack([value[planes - DEEP :] for value in arrays])
+    first = jnp.stack([value[:DEEP] for value in arrays])
     zb, za = exchange(last, first, "gz", False)
-    last = jnp.stack([jnp.concatenate([zb[i, :, 24:], arrays[i][:, 24:], za[i, :, 24:]]) for i in range(3)])
-    first = jnp.stack([jnp.concatenate([zb[i, :, :8], arrays[i][:, :8], za[i, :, :8]]) for i in range(3)])
+    own = jnp.stack(arrays)
+    shape = (sum(planes + 2 * reach - 2 for reach in REACH), 8, 128)
+    last, first = call(packx, "packx", [shape, shape], [], None, (own, zb, za))
     xb, xa = exchange(last, first, "gx", True)
     depth = planes + 2 * DEEP
     tiles = max(tile for _, _, tile, _, _ in slots(depth)) + 1
     whole0, left, right = call(
-        pack0, "pack0", [(3, depth, 48, 128)] + [(tiles, 48, 128)] * 2, [], pos, arrays + (zb, za, xb, xa)
+        pack0, "pack0", [(3, depth, 48, 128)] + [(tiles, 40, 128)] * 2, [], pos, (own, zb, za, xb, xa)
     )
     before0, after0 = exchange(right, left, "gy", False)
     plane0 = (48, 256)
@@ -666,8 +691,8 @@
         (whole0, before0, after0),
     )
 
-    own = lax.all_to_all(message, "gz", 0, 0)
-    xb, xa = exchange(own, own, "gx", True)
+    whole1 = lax.all_to_all(message, "gz", 0, 0)
+    xb, xa = exchange(whole1, whole1, "gx", True)
     depth1 = files * half
     plane1, plane2 = (48, 128), (24, 128)
     depth2 = depth1 // 2
@@ -681,7 +706,7 @@
         + [(3,) + tall2, tall2, (depth2 + 2,) + plane2, (3 * depth2 // 2, 8, 128)]
         + [(3 * depth2,) + plane2, (6, 4 * group, 128)],
         pos,
-        (own, xb, xa),
+        (whole1, xb, xa),
     )
 
     gathered = lax.all_to_all(message, "gx", 0, 0)

time: 126 us -> 121 us (0.960)
  local copies, waits for them, and re-layouts: 5.49 us -> 2.04 us
  waiting for transfers between devices: 27.9 us -> 25.5 us
    unnamed x12 -> x0, local copies, waits for them, and re-layouts: 5.42 us -> none
    ppermute x4, waiting for transfers between devices: 9.1 us -> 6.66 us  [exchange(): lax.ppermute(up_values, axis, up_pairs)]
    another operation x0 -> x2, local copies, waits for them, and re-layouts: none -> 2.01 us  [on_device(): first = jnp.stack([value[:DEEP] for value in arrays])]
  transfers between devices with their start and end apart: 8 -> 8, of which waited for: 7 -> 7; matrix products, arithmetic and copies ran while one was open for 0% -> 1% of each run, Pallas kernels for 0% -> 0%
where the time goes in v5:
time: 121 us
  blocking collectives  55.3 us (46%)
  waiting for transfers between devices  25.5 us (21%)
  starting transfers between devices  18.9 us (16%)
  Pallas kernels  17.2 us (14%)
  local copies, waits for them, and re-layouts  2.04 us (2%)
    all_to_all x1, blocking collectives, on_device(): whole1 = lax.all_to_all(message, 'gz', 0, 0)  25.6 us
    ppermute x4, waiting for transfers between devices, exchange(): lax.ppermute(down_values, axis, down_pairs)  18.8 us
    pallas_call x5, Pallas kernels, call(): pl.pallas_call(body, name=name, out_shape=[jax.ShapeDtypeStruct(shape, F3...  17.2 us
    all_to_all x1, blocking collectives, on_device(): gathered = lax.all_to_all(message, 'gx', 0, 0)  16.4 us
    ppermute x4, starting transfers between devices, exchange(): lax.ppermute(up_values, axis, up_pairs)  13.5 us
    all_to_all x1, blocking collectives, on_device(): gathered = lax.all_to_all(gathered, 'gy', 0, 0)  13.2 us
    ppermute x4, waiting for transfers between devices, exchange(): lax.ppermute(up_values, axis, up_pairs)  6.66 us
    ppermute x4, starting transfers between devices, exchange(): lax.ppermute(down_values, axis, down_pairs)  5.37 us
  transfers between devices with their start and end apart: 8, of which 7 were waited for; matrix products, arithmetic and copies ran while one was open for 1% of the time, Pallas kernels for 0%

profile of v5, /device:TPU:1, one launch (start us, length us, event | category | flops | bytes accessed | tf_op | source)
XLA Modules:
  0.0 120.7 jit_solution(6496395952116946827)
XLA Ops:
  0.6 1.0 slice_bitcast_fusion.2
  1.6 1.0 slice_bitcast_fusion
  2.7 4.8 %collective-permute-start = (f32[3,5,32,128]{3,2,1,0:T(8,128)S(1)}, f32[3,5,32,128]{3,2,1,0:T(8,128)S(1)}, u32[]{:S(2)}, u32[]{:S(2)}) collective-permute-start(f32[3,5,32,128]{3,2,1,0:T(8,128)S(1)} %pad_maximum_fusion.1), channel_id=1, source_target_pairs={{0,1},{1,2},{2,3},{3,4},{4,5},{5,6},{6,7},{8,9},{9,10},{10,11},{11... | collective-permute-start | bytes 737288 | tf_op jit(solution)/shard_map/ppermute | solution.py:661
  7.5 1.3 %collective-permute-start.1 = (f32[3,5,32,128]{3,2,1,0:T(8,128)S(1)}, f32[3,5,32,128]{3,2,1,0:T(8,128)S(1)}, u32[]{:S(2)}, u32[]{:S(2)}) collective-permute-start(f32[3,5,32,128]{3,2,1,0:T(8,128)S(1)} %pad_maximum_fusion.2), channel_id=1, source_target_pairs={{1,0},{2,1},{3,2},{4,3},{5,4},{6,5},{7,6},{9,8},{10,9},{11,10},{12... | collective-permute-start | bytes 737288 | tf_op jit(solution)/shard_map/ppermute | solution.py:661
  8.8 1.1 pad_maximum_fusion.own
  9.9 0.7 collective-permute-done.zb
  10.6 4.5 %collective-permute-done.1.za = f32[3,5,32,128]{3,2,1,0:T(8,128)S(1)} collective-permute-done((f32[3,5,32,128]{3,2,1,0:T(8,128)S(1)}, f32[3,5,32,128]{3,2,1,0:T(8,128)S(1)}, u32[]{:S(2)}, u32[]{:S(2)}) %collective-permute-start.1) | collective-permute-done | bytes 245792 | tf_op jit(solution)/shard_map/ppermute | solution.py:661
  15.1 4.5 %collective-permute-start.2 = (f32[44,8,128]{2,1,0:T(8,128)S(1)}, f32[44,8,128]{2,1,0:T(8,128)S(1)}, u32[]{:S(2)}, u32[]{:S(2)}) collective-permute-start(f32[44,8,128]{2,1,0:T(8,128)S(1)} %get-tuple-element.19), channel_id=1, source_target_pairs={{0,32},{32,64},{64,96},{96,128},{128,160},{160,192},{192,224},{224... | collective-permute-start | bytes 540680 | tf_op jit(solution)/shard_map/ppermute | solution.py:661
  19.7 0.0 collective-permute-start.3
  19.7 0.1 pad_add_fusion.pos
  19.7 2.4 %collective-permute-done.2.xb = f32[44,8,128]{2,1,0:T(8,128)S(1)} collective-permute-done((f32[44,8,128]{2,1,0:T(8,128)S(1)}, f32[44,8,128]{2,1,0:T(8,128)S(1)}, u32[]{:S(2)}, u32[]{:S(2)}) %collective-permute-start.2) | collective-permute-done | bytes 180256 | tf_op jit(solution)/shard_map/ppermute | solution.py:661
  22.1 2.7 %collective-permute-done.3.xa = f32[44,8,128]{2,1,0:T(8,128)S(1)} collective-permute-done((f32[44,8,128]{2,1,0:T(8,128)S(1)}, f32[44,8,128]{2,1,0:T(8,128)S(1)}, u32[]{:S(2)}, u32[]{:S(2)}) %collective-permute-start.3) | collective-permute-done | bytes 180256 | tf_op jit(solution)/shard_map/ppermute | solution.py:661
  24.8 1.0 pack0.1
  25.7 3.0 %collective-permute-start.4 = (f32[11,40,128]{2,1,0:T(8,128)S(1)}, f32[11,40,128]{2,1,0:T(8,128)S(1)}, u32[]{:S(2)}, u32[]{:S(2)}) collective-permute-start(f32[11,40,128]{2,1,0:T(8,128)S(1)} %get-tuple-element.22), channel_id=1, source_target_pairs={{0,8},{8,16},{16,24},{1,9},{9,17},{17,25},{2,10},{10,18},{18,26},{... | collective-permute-start | bytes 675848 | tf_op jit(solution)/shard_map/ppermute | solution.py:661
  28.7 1.3 %collective-permute-start.5 = (f32[11,40,128]{2,1,0:T(8,128)S(1)}, f32[11,40,128]{2,1,0:T(8,128)S(1)}, u32[]{:S(2)}, u32[]{:S(2)}) collective-permute-start(f32[11,40,128]{2,1,0:T(8,128)S(1)} %get-tuple-element.23), channel_id=1, source_target_pairs={{8,0},{16,8},{24,16},{9,1},{17,9},{25,17},{10,2},{18,10},{26,18},{... | collective-permute-start | bytes 675848 | tf_op jit(solution)/shard_map/ppermute | solution.py:661
  30.0 3.6 %collective-permute-done.4.before = f32[11,40,128]{2,1,0:T(8,128)S(1)} collective-permute-done((f32[11,40,128]{2,1,0:T(8,128)S(1)}, f32[11,40,128]{2,1,0:T(8,128)S(1)}, u32[]{:S(2)}, u32[]{:S(2)}) %collective-permute-start.4) | collective-permute-done | bytes 225312 | tf_op jit(solution)/shard_map/ppermute | solution.py:661
  33.6 3.8 %collective-permute-done.5.after = f32[11,40,128]{2,1,0:T(8,128)S(1)} collective-permute-done((f32[11,40,128]{2,1,0:T(8,128)S(1)}, f32[11,40,128]{2,1,0:T(8,128)S(1)}, u32[]{:S(2)}, u32[]{:S(2)}) %collective-permute-start.5) | collective-permute-done | bytes 225312 | tf_op jit(solution)/shard_map/ppermute | solution.py:661
  37.4 3.2 %down0.1 = (f32[14,48,256]{2,1,0:T(8,128)S(1)}, f32[8,144,128]{2,1,0:T(8,128)S(1)}, f32[6,16,48,256]{3,2,1,0:T(8,128)S(1)}, f32[16,48,256]{2,1,0:T(8,128)S(1)}, f32[16,48,256]{2,1,0:T(8,128)S(1)}) custom-call(f32[3,18,48,128]{3,2,1,0:T(8,128)S(1)} %get-tuple-element.21.whole, f32[11,40,128]{2,1,0:T(8,128)S(1)} %collective-permute-done.4.before, ...), custom_call_target="tpu_custom_call" | custom-call | tf_op jit(solution)/shard_map/down0/pallas_call | solution.py:646
  40.6 25.6 %all_to_all.15.own = f32[8,144,128]{2,1,0:T(8,128)S(1)} all-to-all(f32[8,144,128]{2,1,0:T(8,128)S(1)} %get-tuple-element.24), channel_id=1, replica_groups=mesh['gx'=16,'gy'=4,'gz'=8] {'gz'}, dimensions={0} | all-to-all | bytes 1179648 | tf_op jit(solution)/shard_map/all_to_all | solution.py:694
  66.2 2.8 %collective-permute-start.7 = (f32[8,144,128]{2,1,0:T(8,128)S(1)}, f32[8,144,128]{2,1,0:T(8,128)S(1)}, u32[]{:S(2)}, u32[]{:S(2)}) collective-permute-start(f32[8,144,128]{2,1,0:T(8,128)S(1)} %all_to_all.15.own), channel_id=1, source_target_pairs={{32,0},{64,32},{96,64},{128,96},{160,128},{192,160},{224,192},{256... | collective-permute-start | bytes 1769480 | tf_op jit(solution)/shard_map/ppermute | solution.py:661
  69.0 1.2 collective-permute-start.6
  70.2 7.9 %collective-permute-done.7.xa = f32[8,144,128]{2,1,0:T(8,128)S(1)} collective-permute-done((f32[8,144,128]{2,1,0:T(8,128)S(1)}, f32[8,144,128]{2,1,0:T(8,128)S(1)}, u32[]{:S(2)}, u32[]{:S(2)}) %collective-permute-start.7) | collective-permute-done | bytes 589856 | tf_op jit(solution)/shard_map/ppermute | solution.py:661
  78.0 0.0 collective-permute-done.6.xb
  78.0 6.1 %down1.1 = (f32[16,16,128]{2,1,0:T(8,128)S(1)}, f32[6,40,48,128]{3,2,1,0:T(8,128)S(1)}, f32[40,48,128]{2,1,0:T(8,128)S(1)}, f32[40,48,128]{2,1,0:T(8,128)S(1)}, ...) custom-call(s32[4]{0:T(128)S(1)} %pad_add_fusion.pos, ...), custom_call_target="tpu_custom_call" | custom-call | tf_op jit(solution)/shard_map/down1/pallas_call | solution.py:646
  84.1 16.4 %all_to_all.16 = f32[16,16,128]{2,1,0:T(8,128)S(1)} all-to-all(f32[16,16,128]{2,1,0:T(8,128)S(1)} %get-tuple-element.25), channel_id=1, replica_groups=mesh['gx'=16,'gy'=4,'gz'=8] {'gx'}, dimensions={0} | all-to-all | bytes 262144 | tf_op jit(solution)/shard_map/all_to_all | solution.py:712
  100.6 13.2 %all_to_all.17.gathered = f32[4,256,128]{2,1,0:T(8,128)S(1)} all-to-all(f32[4,256,128]{2,1,0:T(8,128)S(1)} %broadcast_in_dim.8), channel_id=1, replica_groups=mesh['gx'=16,'gy'=4,'gz'=8] {'gy'}, dimensions={0} | all-to-all | bytes 1048576 | tf_op jit(solution)/shard_map/all_to_all | solution.py:715
  113.8 6.9 %up.1 = (f32[8,32,128]{2,1,0:T(8,128)}, f32[8,32,128]{2,1,0:T(8,128)}) custom-call(s32[4]{0:T(128)S(1)} %pad_add_fusion.pos, f32[4,256,128]{2,1,0:T(8,128)S(1)} %all_to_all.17.gathered, f32[6,24,24,128]{3,2,1,0:T(8,128)S(1)} %get-tuple-element.26.weights2, f32[24,24,128]{2,1,0:T(8,128)S(1)} %get-tuple-element.27.scaled2, ...), custom_call_target="tpu_custom_call" | custom-call | tf_op jit(solution)/shard_map/up/pallas_call | solution.py:646
  (4 shorter events, 0.1 us)
Async XLA Ops:
  2.7 8.0 %collective-permute-start = (f32[3,5,32,128]{3,2,1,0:T(8,128)S(1)}, f32[3,5,32,128]{3,2,1,0:T(8,128)S(1)}, u32[]{:S(2)}, u32[]{:S(2)}) collective-permute-start(f32[3,5,32,128]{3,2,1,0:T(8,128)S(1)} %pad_maximum_fusion.1), channel_id=1, source_target_pairs={{0,1},{1,2},{2,3},{3,4},{4,5},{5,6},{6,7},{8,9},{9,10},{10,11},{11... | collective-permute-start | bytes 737288 | tf_op jit(solution)/shard_map/ppermute | solution.py:661
  7.5 7.6 %collective-permute-start.1 = (f32[3,5,32,128]{3,2,1,0:T(8,128)S(1)}, f32[3,5,32,128]{3,2,1,0:T(8,128)S(1)}, u32[]{:S(2)}, u32[]{:S(2)}) collective-permute-start(f32[3,5,32,128]{3,2,1,0:T(8,128)S(1)} %pad_maximum_fusion.2), channel_id=1, source_target_pairs={{1,0},{2,1},{3,2},{4,3},{5,4},{6,5},{7,6},{9,8},{10,9},{11,10},{12... | collective-permute-start | bytes 737288 | tf_op jit(solution)/shard_map/ppermute | solution.py:661
  15.1 7.0 %collective-permute-start.2 = (f32[44,8,128]{2,1,0:T(8,128)S(1)}, f32[44,8,128]{2,1,0:T(8,128)S(1)}, u32[]{:S(2)}, u32[]{:S(2)}) collective-permute-start(f32[44,8,128]{2,1,0:T(8,128)S(1)} %get-tuple-element.19), channel_id=1, source_target_pairs={{0,32},{32,64},{64,96},{96,128},{128,160},{160,192},{192,224},{224... | collective-permute-start | bytes 540680 | tf_op jit(solution)/shard_map/ppermute | solution.py:661
  19.7 5.1 %collective-permute-start.3 = (f32[44,8,128]{2,1,0:T(8,128)S(1)}, f32[44,8,128]{2,1,0:T(8,128)S(1)}, u32[]{:S(2)}, u32[]{:S(2)}) collective-permute-start(f32[44,8,128]{2,1,0:T(8,128)S(1)} %get-tuple-element.20), channel_id=1, source_target_pairs={{32,0},{64,32},{96,64},{128,96},{160,128},{192,160},{224,192},{256... | collective-permute-start | bytes 540680 | tf_op jit(solution)/shard_map/ppermute | solution.py:661
  25.7 7.8 %collective-permute-start.4 = (f32[11,40,128]{2,1,0:T(8,128)S(1)}, f32[11,40,128]{2,1,0:T(8,128)S(1)}, u32[]{:S(2)}, u32[]{:S(2)}) collective-permute-start(f32[11,40,128]{2,1,0:T(8,128)S(1)} %get-tuple-element.22), channel_id=1, source_target_pairs={{0,8},{8,16},{16,24},{1,9},{9,17},{17,25},{2,10},{10,18},{18,26},{... | collective-permute-start | bytes 675848 | tf_op jit(solution)/shard_map/ppermute | solution.py:661
  28.7 8.7 %collective-permute-start.5 = (f32[11,40,128]{2,1,0:T(8,128)S(1)}, f32[11,40,128]{2,1,0:T(8,128)S(1)}, u32[]{:S(2)}, u32[]{:S(2)}) collective-permute-start(f32[11,40,128]{2,1,0:T(8,128)S(1)} %get-tuple-element.23), channel_id=1, source_target_pairs={{8,0},{16,8},{24,16},{9,1},{17,9},{25,17},{10,2},{18,10},{26,18},{... | collective-permute-start | bytes 675848 | tf_op jit(solution)/shard_map/ppermute | solution.py:661
  66.2 11.8 %collective-permute-start.7 = (f32[8,144,128]{2,1,0:T(8,128)S(1)}, f32[8,144,128]{2,1,0:T(8,128)S(1)}, u32[]{:S(2)}, u32[]{:S(2)}) collective-permute-start(f32[8,144,128]{2,1,0:T(8,128)S(1)} %all_to_all.15.own), channel_id=1, source_target_pairs={{32,0},{64,32},{96,64},{128,96},{160,128},{192,160},{224,192},{256... | collective-permute-start | bytes 1769480 | tf_op jit(solution)/shard_map/ppermute | solution.py:661
  69.0 9.1 %collective-permute-start.6 = (f32[8,144,128]{2,1,0:T(8,128)S(1)}, f32[8,144,128]{2,1,0:T(8,128)S(1)}, u32[]{:S(2)}, u32[]{:S(2)}) collective-permute-start(f32[8,144,128]{2,1,0:T(8,128)S(1)} %all_to_all.15.own), channel_id=1, source_target_pairs={{0,32},{32,64},{64,96},{96,128},{128,160},{160,192},{192,224},{224... | collective-permute-start | bytes 1769480 | tf_op jit(solution)/shard_map/ppermute | solution.py:661

commit v6 on v5

--- a/solution.py
+++ b/solution.py
@@ -104,33 +104,40 @@
     return out + [(index, plane, first + at // 16, 8 * (at % 16), 8) for at, (index, plane) in enumerate(narrow)]
 
 
-def packx(own, zb, za, last, first):
+def masked(pos, xb, xa, index):
+    before = jnp.where(pos[0] > 0, xb[index], 0.0)
+    return before, jnp.where(pos[0] < pos[3] - 1, xa[index], 0.0)
+
+
+def packz(pos, own, xb, xa, last, first):
     planes, at = own.shape[1], 0
+    four = lax.broadcasted_iota(jnp.int32, xb.shape[1:], 1) < 4
     for index, reach in enumerate(REACH):
-        for value in (zb[index, DEEP - reach + 1 :], own[index], za[index, : reach - 1]):
-            last[at : at + value.shape[0]] = value[:, 24:]
-            first[at : at + value.shape[0]] = value[:, :8]
-            at += value.shape[0]
-
-
-def pack0(pos, own, zb, za, xb, xa, whole, left, right):
+        before, after = masked(pos, xb, xa, index)
+        ends = jnp.where(four, after, before)
+        last[at : at + reach, 0:32, :] = own[index, planes - reach :]
+        last[at : at + reach, 32:40, :] = ends[planes - reach :]
+        first[at : at + reach, 0:32, :] = own[index, :reach]
+        first[at : at + reach, 32:40, :] = ends[:reach]
+        at += reach
+
+
+def pack0(pos, own, xb, xa, zb, za, whole, left, right):
     planes = own.shape[1]
     depth = planes + 2 * DEEP
-    has_before, has_after = pos[0] > 0, pos[0] < pos[3] - 1
-    at_x = 0
+    at = 0
     for index, reach in enumerate(REACH):
         for plane in range(DEEP - reach):
             for end in (plane, depth - 1 - plane):
                 whole[index, end] = jnp.zeros((48, 128), F32)
-        whole[index, DEEP - reach : DEEP, 0:32, :] = zb[index, DEEP - reach :]
+        for ref, start in ((zb, DEEP - reach), (za, DEEP + planes)):
+            whole[index, start : start + reach, 0:40, :] = ref[at : at + reach]
+            whole[index, start : start + reach, 40:48, :] = ref[at : at + reach, 32:40, :]
+        before, after = masked(pos, xb, xa, index)
         whole[index, DEEP : DEEP + planes, 0:32, :] = own[index]
-        whole[index, DEEP + planes : DEEP + planes + reach, 0:32, :] = za[index, :reach]
-        for plane in (DEEP - reach, DEEP + planes + reach - 1):
-            whole[index, plane, 32:48, :] = jnp.zeros((16, 128), F32)
-        inner, count = DEEP - reach + 1, planes + 2 * reach - 2
-        whole[index, inner : inner + count, 32:40, :] = jnp.where(has_after, xa[at_x : at_x + count], 0.0)
-        whole[index, inner : inner + count, 40:48, :] = jnp.where(has_before, xb[at_x : at_x + count], 0.0)
-        at_x += count
+        whole[index, DEEP : DEEP + planes, 32:40, :] = after
+        whole[index, DEEP : DEEP + planes, 40:48, :] = before
+        at += reach
     lane = lane_of((40, 128))
     four = row_of((8, 128)) < 4
     low, high = {}, {}
@@ -383,10 +390,10 @@
 
     quarter = half // 2
     group = quarter // 2
-    place2 = [
-        matrix((128, 128), lambda row, lane, at=at: (row < 32) & (lane == row // 2 + 16 * at), 0.125)
-        for at in range(6)
-    ]
+    place2 = []
+    for at in range(6):
+        to = 64 * (at % 2) + 16 * lax.rem(pos[1] + at // 2, 4)
+        place2.append(matrix((128, 128), lambda row, lane, to=to: (row < 32) & (lane == row // 2 + to), 0.125))
     for index in range(3):
         for plane in range(quarter):
             if index == 0:
@@ -418,16 +425,13 @@
 def bottom(gathered, whole, weights, scaled, update, values):
     group = weights.shape[1]
     rows = weights.shape[2]
+    place = lax.rem(lane_of(gathered.shape[1:]) // 16, 4)
     for index in range(3):
-        total = None
-        lane = lane_of(gathered.shape[1:])
-        for source in range(4):
-            value = gathered[source]
-            for side in range(2):
-                to = 64 * side + 16 * source
-                moved = roll(value, to - 16 * (2 * index + side), 1)
-                moved = jnp.where((lane >= to) & (lane < to + 16), moved, 0.0)
-                total = moved if total is None else total + moved
+        total = gathered[0]
+        for source in range(1, 4):
+            total = jnp.where(place == (source + index) % 4, gathered[source], total)
+        if index:
+            total = jnp.where(place + index < 4, roll(total, -16 * index, 1), roll(total, 64 - 16 * index, 1))
         whole[index] = total
     shape = (rows, 128)
     row, lane = row_of(shape), lane_of(shape)
@@ -667,17 +671,16 @@
     planes = right_side.shape[0]
     arrays = (right_side, acoef, beta)
 
-    last = jnp.stack([value[planes - DEEP :] for value in arrays])
-    first = jnp.stack([value[:DEEP] for value in arrays])
+    last = jnp.stack([value[:, 24:] for value in arrays])
+    first = jnp.stack([value[:, :8] for value in arrays])
+    xb, xa = exchange(last, first, "gx", True)
+    own = jnp.stack(arrays)
+    last, first = call(packz, "packz", [(sum(REACH), 40, 128)] * 2, [], pos, (own, xb, xa))
     zb, za = exchange(last, first, "gz", False)
-    own = jnp.stack(arrays)
-    shape = (sum(planes + 2 * reach - 2 for reach in REACH), 8, 128)
-    last, first = call(packx, "packx", [shape, shape], [], None, (own, zb, za))
-    xb, xa = exchange(last, first, "gx", True)
     depth = planes + 2 * DEEP
     tiles = max(tile for _, _, tile, _, _ in slots(depth)) + 1
     whole0, left, right = call(
-        pack0, "pack0", [(3, depth, 48, 128)] + [(tiles, 40, 128)] * 2, [], pos, (own, zb, za, xb, xa)
+        pack0, "pack0", [(3, depth, 48, 128)] + [(tiles, 40, 128)] * 2, [], pos, (own, xb, xa, zb, za)
     )
     before0, after0 = exchange(right, left, "gy", False)
     plane0 = (48, 256)

time: 121 us -> 120 us (level)
  starting transfers between devices: 18.9 us -> 23.7 us
  waiting for transfers between devices: 25.5 us -> 21.4 us
  blocking collectives: 55.3 us -> 53.8 us
    ppermute x4, starting transfers between devices: 5.37 us -> 10.9 us  [exchange(): lax.ppermute(down_values, axis, down_pairs)]
    ppermute x4, waiting for transfers between devices: 18.8 us -> 16.7 us  [exchange(): lax.ppermute(down_values, axis, down_pairs)]
    all_to_all x1, blocking collectives: 25.6 us -> 23.7 us  [on_device(): whole1 = lax.all_to_all(message, 'gz', 0, 0)]
    ppermute x4, waiting for transfers between devices: 6.66 us -> 4.74 us  [exchange(): lax.ppermute(up_values, axis, up_pairs)]
  transfers between devices with their start and end apart: 8 -> 8, of which waited for: 7 -> 5; matrix products, arithmetic and copies ran while one was open for 1% -> 1% of each run, Pallas kernels for 0% -> 0%
where the time goes in v6:
time: 120 us
  blocking collectives  53.8 us (45%)
  starting transfers between devices  23.7 us (20%)
  waiting for transfers between devices  21.4 us (18%)
  Pallas kernels  17.1 us (14%)
  local copies, waits for them, and re-layouts  1.63 us (1%)
    all_to_all x1, blocking collectives, on_device(): whole1 = lax.all_to_all(message, 'gz', 0, 0)  23.7 us
    pallas_call x5, Pallas kernels, call(): pl.pallas_call(body, name=name, out_shape=[jax.ShapeDtypeStruct(shape, F3...  17.1 us
    all_to_all x1, blocking collectives, on_device(): gathered = lax.all_to_all(message, 'gx', 0, 0)  17 us
    ppermute x4, waiting for transfers between devices, exchange(): lax.ppermute(down_values, axis, down_pairs)  16.7 us
    all_to_all x1, blocking collectives, on_device(): gathered = lax.all_to_all(gathered, 'gy', 0, 0)  13.2 us
    ppermute x4, starting transfers between devices, exchange(): lax.ppermute(up_values, axis, up_pairs)  12.7 us
    ppermute x4, starting transfers between devices, exchange(): lax.ppermute(down_values, axis, down_pairs)  10.9 us
    ppermute x4, waiting for transfers between devices, exchange(): lax.ppermute(up_values, axis, up_pairs)  4.74 us
  transfers between devices with their start and end apart: 8, of which 5 were waited for; matrix products, arithmetic and copies ran while one was open for 1% of the time, Pallas kernels for 0%

profile of v6, /device:TPU:1, one launch (start us, length us, event | category | flops | bytes accessed | tf_op | source)
XLA Modules:
  0.0 119.6 jit_solution(10292599554586823214)
XLA Ops:
  0.6 0.8 slice_bitcast_fusion.2
  1.4 0.8 slice_bitcast_fusion
  2.2 2.7 %collective-permute-start = (f32[3,8,8,128]{3,2,1,0:T(8,128)S(1)}, f32[3,8,8,128]{3,2,1,0:T(8,128)S(1)}, u32[]{:S(2)}, u32[]{:S(2)}) collective-permute-start(f32[3,8,8,128]{3,2,1,0:T(8,128)S(1)} %pad_maximum_fusion.1), channel_id=1, source_target_pairs={{0,32},{32,64},{64,96},{96,128},{128,160},{160,192},{192,224},{224... | collective-permute-start | bytes 294920 | tf_op jit(solution)/shard_map/ppermute | solution.py:665
  5.0 4.2 %collective-permute-start.1 = (f32[3,8,8,128]{3,2,1,0:T(8,128)S(1)}, f32[3,8,8,128]{3,2,1,0:T(8,128)S(1)}, u32[]{:S(2)}, u32[]{:S(2)}) collective-permute-start(f32[3,8,8,128]{3,2,1,0:T(8,128)S(1)} %pad_maximum_fusion.2), channel_id=1, source_target_pairs={{32,0},{64,32},{96,64},{128,96},{160,128},{192,160},{224,192},{256... | collective-permute-start | bytes 294920 | tf_op jit(solution)/shard_map/ppermute | solution.py:665
  9.2 1.1 pad_maximum_fusion.own
  10.2 0.1 pad_add_fusion.pos
  10.3 0.0 collective-permute-done.xb
  10.3 0.0 collective-permute-done.1.xa
  10.3 0.6 packz.1
  10.9 2.7 %collective-permute-start.2 = (f32[13,40,128]{2,1,0:T(8,128)S(1)}, f32[13,40,128]{2,1,0:T(8,128)S(1)}, u32[]{:S(2)}, u32[]{:S(2)}) collective-permute-start(f32[13,40,128]{2,1,0:T(8,128)S(1)} %get-tuple-element.19), channel_id=1, source_target_pairs={{0,1},{1,2},{2,3},{3,4},{4,5},{5,6},{6,7},{8,9},{9,10},{10,11},{11... | collective-permute-start | bytes 798728 | tf_op jit(solution)/shard_map/ppermute | solution.py:665
  13.6 1.3 %collective-permute-start.3 = (f32[13,40,128]{2,1,0:T(8,128)S(1)}, f32[13,40,128]{2,1,0:T(8,128)S(1)}, u32[]{:S(2)}, u32[]{:S(2)}) collective-permute-start(f32[13,40,128]{2,1,0:T(8,128)S(1)} %get-tuple-element.20), channel_id=1, source_target_pairs={{1,0},{2,1},{3,2},{4,3},{5,4},{6,5},{7,6},{9,8},{10,9},{11,10},{12... | collective-permute-start | bytes 798728 | tf_op jit(solution)/shard_map/ppermute | solution.py:665
  14.9 2.0 %collective-permute-done.2.zb = f32[13,40,128]{2,1,0:T(8,128)S(1)} collective-permute-done((f32[13,40,128]{2,1,0:T(8,128)S(1)}, f32[13,40,128]{2,1,0:T(8,128)S(1)}, u32[]{:S(2)}, u32[]{:S(2)}) %collective-permute-start.2) | collective-permute-done | bytes 266272 | tf_op jit(solution)/shard_map/ppermute | solution.py:665
  16.9 5.0 %collective-permute-done.3.za = f32[13,40,128]{2,1,0:T(8,128)S(1)} collective-permute-done((f32[13,40,128]{2,1,0:T(8,128)S(1)}, f32[13,40,128]{2,1,0:T(8,128)S(1)}, u32[]{:S(2)}, u32[]{:S(2)}) %collective-permute-start.3) | collective-permute-done | bytes 266272 | tf_op jit(solution)/shard_map/ppermute | solution.py:665
  22.0 1.0 pack0.1
  22.9 5.3 %collective-permute-start.4 = (f32[11,40,128]{2,1,0:T(8,128)S(1)}, f32[11,40,128]{2,1,0:T(8,128)S(1)}, u32[]{:S(2)}, u32[]{:S(2)}) collective-permute-start(f32[11,40,128]{2,1,0:T(8,128)S(1)} %get-tuple-element.22), channel_id=1, source_target_pairs={{0,8},{8,16},{16,24},{1,9},{9,17},{17,25},{2,10},{10,18},{18,26},{... | collective-permute-start | bytes 675848 | tf_op jit(solution)/shard_map/ppermute | solution.py:665
  28.3 1.3 %collective-permute-start.5 = (f32[11,40,128]{2,1,0:T(8,128)S(1)}, f32[11,40,128]{2,1,0:T(8,128)S(1)}, u32[]{:S(2)}, u32[]{:S(2)}) collective-permute-start(f32[11,40,128]{2,1,0:T(8,128)S(1)} %get-tuple-element.23), channel_id=1, source_target_pairs={{8,0},{16,8},{24,16},{9,1},{17,9},{25,17},{10,2},{18,10},{26,18},{... | collective-permute-start | bytes 675848 | tf_op jit(solution)/shard_map/ppermute | solution.py:665
  29.6 2.7 %collective-permute-done.4.before = f32[11,40,128]{2,1,0:T(8,128)S(1)} collective-permute-done((f32[11,40,128]{2,1,0:T(8,128)S(1)}, f32[11,40,128]{2,1,0:T(8,128)S(1)}, u32[]{:S(2)}, u32[]{:S(2)}) %collective-permute-start.4) | collective-permute-done | bytes 225312 | tf_op jit(solution)/shard_map/ppermute | solution.py:665
  32.3 3.8 %collective-permute-done.5.after = f32[11,40,128]{2,1,0:T(8,128)S(1)} collective-permute-done((f32[11,40,128]{2,1,0:T(8,128)S(1)}, f32[11,40,128]{2,1,0:T(8,128)S(1)}, u32[]{:S(2)}, u32[]{:S(2)}) %collective-permute-start.5) | collective-permute-done | bytes 225312 | tf_op jit(solution)/shard_map/ppermute | solution.py:665
  36.1 3.2 %down0.1 = (f32[14,48,256]{2,1,0:T(8,128)S(1)}, f32[8,144,128]{2,1,0:T(8,128)S(1)}, f32[6,16,48,256]{3,2,1,0:T(8,128)S(1)}, f32[16,48,256]{2,1,0:T(8,128)S(1)}, f32[16,48,256]{2,1,0:T(8,128)S(1)}) custom-call(f32[3,18,48,128]{3,2,1,0:T(8,128)S(1)} %get-tuple-element.21.whole, f32[11,40,128]{2,1,0:T(8,128)S(1)} %collective-permute-done.4.before, ...), custom_call_target="tpu_custom_call" | custom-call | tf_op jit(solution)/shard_map/down0/pallas_call | solution.py:650
  39.3 23.7 %all_to_all.15.own = f32[8,144,128]{2,1,0:T(8,128)S(1)} all-to-all(f32[8,144,128]{2,1,0:T(8,128)S(1)} %get-tuple-element.24), channel_id=1, replica_groups=mesh['gx'=16,'gy'=4,'gz'=8] {'gz'}, dimensions={0} | all-to-all | bytes 1179648 | tf_op jit(solution)/shard_map/all_to_all | solution.py:697
  62.9 4.1 %collective-permute-start.7 = (f32[8,144,128]{2,1,0:T(8,128)S(1)}, f32[8,144,128]{2,1,0:T(8,128)S(1)}, u32[]{:S(2)}, u32[]{:S(2)}) collective-permute-start(f32[8,144,128]{2,1,0:T(8,128)S(1)} %all_to_all.15.own), channel_id=1, source_target_pairs={{32,0},{64,32},{96,64},{128,96},{160,128},{192,160},{224,192},{256... | collective-permute-start | bytes 1769480 | tf_op jit(solution)/shard_map/ppermute | solution.py:665
  67.0 2.0 %collective-permute-start.6 = (f32[8,144,128]{2,1,0:T(8,128)S(1)}, f32[8,144,128]{2,1,0:T(8,128)S(1)}, u32[]{:S(2)}, u32[]{:S(2)}) collective-permute-start(f32[8,144,128]{2,1,0:T(8,128)S(1)} %all_to_all.15.own), channel_id=1, source_target_pairs={{0,32},{32,64},{64,96},{96,128},{128,160},{160,192},{192,224},{224... | collective-permute-start | bytes 1769480 | tf_op jit(solution)/shard_map/ppermute | solution.py:665
  69.1 7.9 %collective-permute-done.7.xa = f32[8,144,128]{2,1,0:T(8,128)S(1)} collective-permute-done((f32[8,144,128]{2,1,0:T(8,128)S(1)}, f32[8,144,128]{2,1,0:T(8,128)S(1)}, u32[]{:S(2)}, u32[]{:S(2)}) %collective-permute-start.7) | collective-permute-done | bytes 589856 | tf_op jit(solution)/shard_map/ppermute | solution.py:665
  76.9 0.0 collective-permute-done.6.xb
  76.9 6.1 %down1.1 = (f32[16,16,128]{2,1,0:T(8,128)S(1)}, f32[6,40,48,128]{3,2,1,0:T(8,128)S(1)}, f32[40,48,128]{2,1,0:T(8,128)S(1)}, f32[40,48,128]{2,1,0:T(8,128)S(1)}, ...) custom-call(s32[4]{0:T(128)S(1)} %pad_add_fusion.pos, ...), custom_call_target="tpu_custom_call" | custom-call | tf_op jit(solution)/shard_map/down1/pallas_call | solution.py:650
  83.0 17.0 %all_to_all.16 = f32[16,16,128]{2,1,0:T(8,128)S(1)} all-to-all(f32[16,16,128]{2,1,0:T(8,128)S(1)} %get-tuple-element.25), channel_id=1, replica_groups=mesh['gx'=16,'gy'=4,'gz'=8] {'gx'}, dimensions={0} | all-to-all | bytes 262144 | tf_op jit(solution)/shard_map/all_to_all | solution.py:715
  100.0 13.2 %all_to_all.17.gathered = f32[4,256,128]{2,1,0:T(8,128)S(1)} all-to-all(f32[4,256,128]{2,1,0:T(8,128)S(1)} %broadcast_in_dim.8), channel_id=1, replica_groups=mesh['gx'=16,'gy'=4,'gz'=8] {'gy'}, dimensions={0} | all-to-all | bytes 1048576 | tf_op jit(solution)/shard_map/all_to_all | solution.py:718
  113.3 6.3 %up.1 = (f32[8,32,128]{2,1,0:T(8,128)}, f32[8,32,128]{2,1,0:T(8,128)}) custom-call(s32[4]{0:T(128)S(1)} %pad_add_fusion.pos, f32[4,256,128]{2,1,0:T(8,128)S(1)} %all_to_all.17.gathered, f32[6,24,24,128]{3,2,1,0:T(8,128)S(1)} %get-tuple-element.26.weights2, f32[24,24,128]{2,1,0:T(8,128)S(1)} %get-tuple-element.27.scaled2, ...), custom_call_target="tpu_custom_call" | custom-call | tf_op jit(solution)/shard_map/up/pallas_call | solution.py:650
  (3 shorter events, 0.1 us)
Async XLA Ops:
  2.2 8.1 %collective-permute-start = (f32[3,8,8,128]{3,2,1,0:T(8,128)S(1)}, f32[3,8,8,128]{3,2,1,0:T(8,128)S(1)}, u32[]{:S(2)}, u32[]{:S(2)}) collective-permute-start(f32[3,8,8,128]{3,2,1,0:T(8,128)S(1)} %pad_maximum_fusion.1), channel_id=1, source_target_pairs={{0,32},{32,64},{64,96},{96,128},{128,160},{160,192},{192,224},{224... | collective-permute-start | bytes 294920 | tf_op jit(solution)/shard_map/ppermute | solution.py:665
  5.0 5.4 %collective-permute-start.1 = (f32[3,8,8,128]{3,2,1,0:T(8,128)S(1)}, f32[3,8,8,128]{3,2,1,0:T(8,128)S(1)}, u32[]{:S(2)}, u32[]{:S(2)}) collective-permute-start(f32[3,8,8,128]{3,2,1,0:T(8,128)S(1)} %pad_maximum_fusion.2), channel_id=1, source_target_pairs={{32,0},{64,32},{96,64},{128,96},{160,128},{192,160},{224,192},{256... | collective-permute-start | bytes 294920 | tf_op jit(solution)/shard_map/ppermute | solution.py:665
  10.9 6.0 %collective-permute-start.2 = (f32[13,40,128]{2,1,0:T(8,128)S(1)}, f32[13,40,128]{2,1,0:T(8,128)S(1)}, u32[]{:S(2)}, u32[]{:S(2)}) collective-permute-start(f32[13,40,128]{2,1,0:T(8,128)S(1)} %get-tuple-element.19), channel_id=1, source_target_pairs={{0,1},{1,2},{2,3},{3,4},{4,5},{5,6},{6,7},{8,9},{9,10},{10,11},{11... | collective-permute-start | bytes 798728 | tf_op jit(solution)/shard_map/ppermute | solution.py:665
  13.6 8.3 %collective-permute-start.3 = (f32[13,40,128]{2,1,0:T(8,128)S(1)}, f32[13,40,128]{2,1,0:T(8,128)S(1)}, u32[]{:S(2)}, u32[]{:S(2)}) collective-permute-start(f32[13,40,128]{2,1,0:T(8,128)S(1)} %get-tuple-element.20), channel_id=1, source_target_pairs={{1,0},{2,1},{3,2},{4,3},{5,4},{6,5},{7,6},{9,8},{10,9},{11,10},{12... | collective-permute-start | bytes 798728 | tf_op jit(solution)/shard_map/ppermute | solution.py:665
  22.9 9.3 %collective-permute-start.4 = (f32[11,40,128]{2,1,0:T(8,128)S(1)}, f32[11,40,128]{2,1,0:T(8,128)S(1)}, u32[]{:S(2)}, u32[]{:S(2)}) collective-permute-start(f32[11,40,128]{2,1,0:T(8,128)S(1)} %get-tuple-element.22), channel_id=1, source_target_pairs={{0,8},{8,16},{16,24},{1,9},{9,17},{17,25},{2,10},{10,18},{18,26},{... | collective-permute-start | bytes 675848 | tf_op jit(solution)/shard_map/ppermute | solution.py:665
  28.3 7.8 %collective-permute-start.5 = (f32[11,40,128]{2,1,0:T(8,128)S(1)}, f32[11,40,128]{2,1,0:T(8,128)S(1)}, u32[]{:S(2)}, u32[]{:S(2)}) collective-permute-start(f32[11,40,128]{2,1,0:T(8,128)S(1)} %get-tuple-element.23), channel_id=1, source_target_pairs={{8,0},{16,8},{24,16},{9,1},{17,9},{25,17},{10,2},{18,10},{26,18},{... | collective-permute-start | bytes 675848 | tf_op jit(solution)/shard_map/ppermute | solution.py:665
  62.9 14.0 %collective-permute-start.7 = (f32[8,144,128]{2,1,0:T(8,128)S(1)}, f32[8,144,128]{2,1,0:T(8,128)S(1)}, u32[]{:S(2)}, u32[]{:S(2)}) collective-permute-start(f32[8,144,128]{2,1,0:T(8,128)S(1)} %all_to_all.15.own), channel_id=1, source_target_pairs={{32,0},{64,32},{96,64},{128,96},{160,128},{192,160},{224,192},{256... | collective-permute-start | bytes 1769480 | tf_op jit(solution)/shard_map/ppermute | solution.py:665
  67.0 9.9 %collective-permute-start.6 = (f32[8,144,128]{2,1,0:T(8,128)S(1)}, f32[8,144,128]{2,1,0:T(8,128)S(1)}, u32[]{:S(2)}, u32[]{:S(2)}) collective-permute-start(f32[8,144,128]{2,1,0:T(8,128)S(1)} %all_to_all.15.own), channel_id=1, source_target_pairs={{0,32},{32,64},{64,96},{96,128},{128,160},{160,192},{192,224},{224... | collective-permute-start | bytes 1769480 | tf_op jit(solution)/shard_map/ppermute | solution.py:665

commit v7 on v6

--- a/solution.py
+++ b/solution.py
@@ -77,7 +77,14 @@
 
 
 def dot(left, right):
-    return jnp.dot(left, right, precision=lax.Precision.HIGHEST, preferred_element_type=F32)
+    right = right.astype(jnp.bfloat16)
+    high = left.astype(jnp.bfloat16)
+    rest = left - high.astype(F32)
+    middle = rest.astype(jnp.bfloat16)
+    low = (rest - middle.astype(F32)).astype(jnp.bfloat16)
+    total = jnp.dot(low, right, preferred_element_type=F32)
+    total = total + jnp.dot(middle, right, preferred_element_type=F32)
+    return total + jnp.dot(high, right, preferred_element_type=F32)
 
 
 def matrix(shape, rule, value=1.0):
@@ -153,38 +160,34 @@
         right[tile] = high[tile]
 
 
-def unpack0(whole, before, after, ext):
-    depth = whole.shape[1]
-    ext[:, :, :, 0:128] = whole[...]
+def unpack0(whole, before, after, ext, wanted):
     lane = lane_of((40, 128))
-    there = {(index, plane): rest for index, plane, *rest in slots(depth)}
-    for index in range(3):
-        for plane in range(depth):
-            if (index, plane) not in there:
-                ext[index, plane, :, 128:256] = jnp.zeros((48, 128), F32)
-                continue
-            tile, to, lanes = there[index, plane]
-            ahead = jnp.where(lane < lanes, roll(after[tile], -to, 1), 0.0)
-            value = jnp.where(lane >= 128 - lanes, roll(before[tile], -lanes - to, 1), ahead)
-            ext[index, plane, 0:40, 128:256] = value
-            ext[index, plane, 40:48, 128:256] = value[32:40]
+    there = {(index, plane): rest for index, plane, *rest in slots(whole.shape[1])}
+    for index, plane in wanted:
+        ext[index, plane, :, 0:128] = whole[index, plane]
+        if (index, plane) not in there:
+            ext[index, plane, :, 128:256] = jnp.zeros((48, 128), F32)
+            continue
+        tile, to, lanes = there[index, plane]
+        ahead = jnp.where(lane < lanes, roll(after[tile], -to, 1), 0.0)
+        value = jnp.where(lane >= 128 - lanes, roll(before[tile], -lanes - to, 1), ahead)
+        ext[index, plane, 0:40, 128:256] = value
+        ext[index, plane, 40:48, 128:256] = value[32:40]
 
 
 def planes_of(count, level, start=0):
-    most = (7, 10, 16)[level]
+    most = (12, 32, 16)[level]
     return pl.loop(start, start + count, unroll=max(n for n in range(1, most + 1) if count % n == 0))
 
 
-def prepare0(ext, weights, diagonal, scaled):
-    @planes_of(diagonal.shape[0], 0)
-    def _(plane):
-        got, middle, inverse = coefficients(
-            ext[2, plane + 1], ext[2, plane], ext[2, plane + 2], ext[1, plane + 1], 0
-        )
-        for index in range(6):
-            weights[index, plane] = got[index]
-        diagonal[plane] = middle
-        scaled[plane] = ext[0, plane + 1] * inverse
+def coefficients0(ext, plane):
+    got, middle, inverse = coefficients(ext[2, plane], ext[2, plane - 1], ext[2, plane + 1], ext[1, plane], 0)
+    return got, middle, ext[0, plane] * inverse
+
+
+def first_sweeps(weights, scaled, below, middle, above):
+    value = FIRST * middle
+    return value + (CARRY * value + GAIN * defect(scaled, weights, value, FIRST * below, FIRST * above))
 
 
 def residual0(weights, diagonal, scaled, value, below, above, at, lanes):
@@ -195,31 +198,27 @@
     return diagonal[at, 0:32, 0:lanes] * result
 
 
-def down0(whole, before, after, iterate, message, weights, diagonal, scaled, ext, start, sums):
-    unpack0(whole, before, after, ext)
-    prepare0(ext, weights, diagonal, scaled)
-
-    @planes_of(start.shape[0], 0)
-    def _(plane):
-        start[plane] = FIRST * scaled[plane]
+def down0(whole, before, after, iterate, message, weights, diagonal, scaled, ext, sums):
+    depth = whole.shape[1]
+    wanted = [(index, plane) for index in range(2) for plane in range(3, depth - 3)]
+    unpack0(whole, before, after, ext, wanted + [(2, plane) for plane in range(2, depth - 2)])
+
+    @planes_of(diagonal.shape[0], 0)
+    def _(plane):
+        got, diagonal[plane], scaled[plane] = coefficients0(ext, plane + 3)
+        for index in range(6):
+            weights[index, plane] = got[index]
 
     @planes_of(iterate.shape[0], 0)
     def _(plane):
-        value = start[plane + 1]
-        got = defect(
-            scaled[plane + 1],
-            [weights[index, plane + 1] for index in range(6)],
-            value,
-            start[plane],
-            start[plane + 2],
-        )
-        iterate[plane] = value + (CARRY * value + GAIN * got)
+        faces = [weights[index, plane + 1] for index in range(6)]
+        iterate[plane] = first_sweeps(faces, scaled[plane + 1], scaled[plane], scaled[plane + 1], scaled[plane + 2])
 
     planes = whole.shape[1] - 2 * DEEP
 
     def left_over(plane):
         return residual0(
-            weights, diagonal, scaled, iterate[plane + 3], iterate[plane + 2], iterate[plane + 4], plane + 4, 256
+            weights, diagonal, scaled, iterate[plane + 1], iterate[plane], iterate[plane + 2], plane + 2, 256
         )
 
     half = planes // 2
@@ -256,24 +255,39 @@
     copies(message, jnp.concatenate([middle, ends], axis=0))
 
 
-def unpack1(pos, own, xb, xa, ext):
-    has_before, has_after = pos[0] > 0, pos[0] < pos[3] - 1
+def rest0(whole, before, after, weights, scaled, later, outer, ext):
+    depth = whole.shape[1]
+    ends = ((1, 2), (depth - 2, depth - 3))
+    wanted = [(index, plane) for index in range(2) for end in ends for plane in end]
+    unpack0(whole, before, after, ext, wanted + [(2, p) for p in (0, 1, 2, 3, depth - 4, depth - 3, depth - 2, depth - 1)])
+    count = scaled.shape[0]
+    for side, (far, near) in enumerate(ends):
+        at, beside = (0, 1) if side == 0 else (count - 1, count - 2)
+        farthest = coefficients0(ext, far)[2]
+        faces, _, middle = coefficients0(ext, near)
+        around = (farthest, scaled[at]) if side == 0 else (scaled[at], farthest)
+        outer[3 * side] = first_sweeps(faces, middle, around[0], middle, around[1])
+        faces = [weights[index, at] for index in range(6)]
+        around = (middle, scaled[beside]) if side == 0 else (scaled[beside], middle)
+        outer[1 + side] = first_sweeps(faces, scaled[at], around[0], scaled[at], around[1])
+
+
+def unpack1(ref, there, put):
     lane = lane_of((16, 128))
-    per = own.shape[1] // 36
-
-    @pl.loop(0, own.shape[0], unroll=2)
+    per = ref.shape[1] // 36
+
+    @pl.loop(0, ref.shape[0], unroll=ref.shape[0])
     def _(source):
-        for block, (ref, there) in enumerate(((own, None), (xa, has_after), (xb, has_before))):
-            for index in range(3):
-                ends = ref[source, 96 + 16 * index : 112 + 16 * index, :]
-                for plane in range(per):
-                    at = (2 * index + plane // 2) * 16
-                    value = roll(ref[source, at : at + 16, :], 64 * (plane % 2), 1)
-                    value = jnp.where(lane < 80, jnp.where(lane < 64, value, roll(ends, 64 - 32 * plane, 1)), 0.0)
-                    value = jnp.where(lane >= 112, roll(ends, 96 - 32 * plane, 1), value)
-                    if there is not None:
-                        value = jnp.where(there, value, 0.0)
-                    ext[index, 4 + source * per + plane, 16 * block : 16 * block + 16, :] = value
+        for index in range(3):
+            ends = ref[source, 96 + 16 * index : 112 + 16 * index, :]
+            for plane in range(per):
+                at = (2 * index + plane // 2) * 16
+                value = roll(ref[source, at : at + 16, :], 64 * (plane % 2), 1)
+                value = jnp.where(lane < 80, jnp.where(lane < 64, value, roll(ends, 64 - 32 * plane, 1)), 0.0)
+                value = jnp.where(lane >= 112, roll(ends, 96 - 32 * plane, 1), value)
+                if there is not None:
+                    value = jnp.where(there, value, 0.0)
+                put(index, source * per + plane, value)
 
 
 def pass_all(weights, scaled, value, out, count, combine, level):
@@ -318,7 +332,12 @@
             for plane in range(4):
                 ext1[index, end + plane] = jnp.zeros((48, 128), F32)
 
-    unpack1(pos, own, xb, xa, ext1)
+    for start, ref, there in ((0, own, None), (16, xa, pos[0] < pos[3] - 1), (32, xb, pos[0] > 0)):
+
+        def put(index, plane, value, start=start):
+            ext1[index, plane + 4, start : start + 16, :] = value
+
+        unpack1(ref, there, put)
     prepare(ext1, weights1, diagonal1, scaled1, 1)
     start1[0] = jnp.zeros((48, 128), F32)
     start1[depth + 1] = jnp.zeros((48, 128), F32)
@@ -516,7 +535,7 @@
 
 def up(
     pos, gathered, weights2, scaled2, iterate2, weights1, scaled1, iterate1,
-    weights0, diagonal0, scaled0, iterate0, solved, left_over,
+    weights0, diagonal0, scaled0, iterate0, outer0, solved, left_over,
     whole3, weights3, scaled3, update3, values3,
     thin3, error2, value2, update2, middle2, out2,
     tall1, value1, update1, middle1, out1,
@@ -605,16 +624,19 @@
 
     @planes_of(iterate0.shape[0], 0)
     def _(plane):
-        value0[plane] = iterate0[plane] + out0[plane + 1]
-
-    count = iterate0.shape[0]
+        value0[plane + 2] = iterate0[plane] + out0[plane + 3]
+
+    count = value0.shape[0]
+    for at, plane in enumerate((0, 1, count - 2, count - 1)):
+        value0[plane] = outer0[at] + out0[plane + 1]
+
 
     @planes_of(count - 2, 0)
     def _(plane):
         value = value0[plane + 1]
         got = FIRST * defect(
-            scaled0[plane + 2],
-            [weights0[index, plane + 2] for index in range(6)],
+            scaled0[plane],
+            [weights0[index, plane] for index in range(6)],
             value,
             value0[plane],
             value0[plane + 2],
@@ -626,8 +648,8 @@
     def _(plane):
         value = middle0[plane + 1]
         got = defect(
-            scaled0[plane + 3],
-            [weights0[index, plane + 3] for index in range(6)],
+            scaled0[plane + 1],
+            [weights0[index, plane + 1] for index in range(6)],
             value,
             middle0[plane],
             middle0[plane + 2],
@@ -639,11 +661,11 @@
         value = out0[plane + 1]
         solved[plane] = value[0:32, 0:128]
         left_over[plane] = residual0(
-            weights0, diagonal0, scaled0, value, out0[plane], out0[plane + 2], plane + 4, 128
+            weights0, diagonal0, scaled0, value, out0[plane], out0[plane + 2], plane + 2, 128
         )
 
 
-def call(body, name, outs, scratch, pos, args):
+def call(body, name, outs, scratch, pos, args, flops=0):
     vmem = pl.BlockSpec(memory_space=pltpu.VMEM)
     smem = [pl.BlockSpec(memory_space=pltpu.SMEM)] if pos is not None else []
     operands = ([pos] if pos is not None else []) + list(args)
@@ -654,6 +676,7 @@
         in_specs=smem + [vmem] * len(args),
         out_specs=[vmem] * len(outs),
         scratch_shapes=[pltpu.VMEM(shape, F32) for shape in scratch],
+        cost_estimate=pl.CostEstimate(flops=flops, bytes_accessed=0, transcendentals=0) if flops else None,
         compiler_params=pltpu.CompilerParams(vmem_limit_bytes=32 * 2**20),
     )(*operands)
 
@@ -688,8 +711,8 @@
     iterate0, message, weights0, diagonal0, scaled0 = call(
         down0,
         "down0",
-        [(depth - 4,) + plane0, (files, 36 * half, 128), (6, depth - 2) + plane0] + [(depth - 2,) + plane0] * 2,
-        [(3, depth) + plane0, (depth - 2,) + plane0, (2, 3 * half, 32, 128)],
+        [(depth - 8,) + plane0, (files, 36 * half, 128), (6, depth - 6) + plane0] + [(depth - 6,) + plane0] * 2,
+        [(3, depth) + plane0, (2, 3 * half, 32, 128)],
         None,
         (whole0, before0, after0),
     )
@@ -697,6 +720,15 @@
     whole1 = lax.all_to_all(message, "gz", 0, 0)
     xb, xa = exchange(whole1, whole1, "gx", True)
     depth1 = files * half
+    outer0 = call(
+        rest0,
+        "rest0",
+        [(4,) + plane0],
+        [(3, depth) + plane0],
+        None,
+        (whole0, before0, after0, weights0, scaled0, whole1),
+        10**9,
+    )[0]
     plane1, plane2 = (48, 128), (24, 128)
     depth2 = depth1 // 2
     group = depth2 // 4
@@ -729,7 +761,7 @@
         + [(8,) + plane1, (depth - 4,) + plane0, (depth - 6,) + plane0, (depth - 6,) + plane0, (depth - 2,) + plane0],
         pos,
         (gathered, weights2, scaled2, iterate2, weights1, scaled1, iterate1)
-        + (weights0, diagonal0, scaled0, iterate0),
+        + (weights0, diagonal0, scaled0, iterate0, outer0),
     )
     return solved, left_over
 

time: 120 us -> 141 us (1.18)
  local copies, waits for them, and re-layouts: 1.63 us -> 28.9 us
  blocking collectives: 53.8 us -> 40.6 us
  starting transfers between devices: 23.7 us -> 28 us
  waiting for transfers between devices: 21.4 us -> 24.6 us
    unnamed x0 -> x58, local copies, waits for them, and re-layouts: none -> 26.4 us
    all_to_all x1 -> x0, blocking collectives: 13.2 us -> none  [on_device(): gathered = lax.all_to_all(gathered, 'gy', 0, 0)]
    all_to_all x0 -> x1, starting transfers between devices: none -> 4.31 us  [on_device(): gathered = lax.all_to_all(gathered, 'gy', 0, 0)]
    all_to_all x0 -> x1, waiting for transfers between devices: none -> 3.15 us  [on_device(): gathered = lax.all_to_all(gathered, 'gy', 0, 0)]
    pallas_call x5 -> x6, Pallas kernels: 17.1 us -> 16.2 us  [call(): pl.pallas_call(body, name=name, out_shape=[jax.ShapeDtypeStruct(shape, F3...]
  transfers between devices with their start and end apart: 8 -> 9, of which waited for: 5 -> 6; matrix products, arithmetic and copies ran while one was open for 1% -> 1% of each run, Pallas kernels for 0% -> 0%
where the time goes in v7:
time: 141 us; the launch traced here: 140 us
  blocking collectives  40.6 us (29%)
  local copies, waits for them, and re-layouts  28.9 us (20%)
  starting transfers between devices  28 us (20%)
  waiting for transfers between devices  24.6 us (17%)
  Pallas kernels  16.2 us (11%)
    unnamed x58, local copies, waits for them, and re-layouts  26.4 us
    all_to_all x1, blocking collectives, on_device(): whole1 = lax.all_to_all(message, 'gz', 0, 0)  23.6 us
    all_to_all x1, blocking collectives, on_device(): gathered = lax.all_to_all(message, 'gx', 0, 0)  16.9 us
    ppermute x4, waiting for transfers between devices, exchange(): lax.ppermute(down_values, axis, down_pairs)  16.7 us
    pallas_call x6, Pallas kernels, call(): pl.pallas_call(body, name=name, out_shape=[jax.ShapeDtypeStruct(shape, F3...  16.2 us
    ppermute x4, starting transfers between devices, exchange(): lax.ppermute(up_values, axis, up_pairs)  12.7 us
    ppermute x4, starting transfers between devices, exchange(): lax.ppermute(down_values, axis, down_pairs)  10.9 us
    ppermute x4, waiting for transfers between devices, exchange(): lax.ppermute(up_values, axis, up_pairs)  4.74 us
  transfers between devices with their start and end apart: 9, of which 6 were waited for; matrix products, arithmetic and copies ran while one was open for 1% of the time, Pallas kernels for 0%

profile of v7, /device:TPU:1, one launch (start us, length us, event | category | flops | bytes accessed | tf_op | source)
XLA Modules:
  0.0 140.2 jit_solution(9994555331151337511)
XLA Ops:
  2.2 2.7 %collective-permute-start = (f32[3,8,8,128]{3,2,1,0:T(8,128)S(1)}, f32[3,8,8,128]{3,2,1,0:T(8,128)S(1)}, u32[]{:S(2)}, u32[]{:S(2)}) collective-permute-start(f32[3,8,8,128]{3,2,1,0:T(8,128)S(1)} %pad_maximum_fusion.1), channel_id=1, source_target_pairs={{0,32},{32,64},{64,96},{96,128},{128,160},{160,192},{192,224},{224... | collective-permute-start | bytes 294920 | tf_op jit(solution)/shard_map/ppermute | solution.py:688
  5.0 4.2 %collective-permute-start.1 = (f32[3,8,8,128]{3,2,1,0:T(8,128)S(1)}, f32[3,8,8,128]{3,2,1,0:T(8,128)S(1)}, u32[]{:S(2)}, u32[]{:S(2)}) collective-permute-start(f32[3,8,8,128]{3,2,1,0:T(8,128)S(1)} %pad_maximum_fusion.2), channel_id=1, source_target_pairs={{32,0},{64,32},{96,64},{128,96},{160,128},{192,160},{224,192},{256... | collective-permute-start | bytes 294920 | tf_op jit(solution)/shard_map/ppermute | solution.py:688
  9.2 1.1 pad_maximum_fusion.own
  10.9 2.7 %collective-permute-start.2 = (f32[13,40,128]{2,1,0:T(8,128)S(1)}, f32[13,40,128]{2,1,0:T(8,128)S(1)}, u32[]{:S(2)}, u32[]{:S(2)}) collective-permute-start(f32[13,40,128]{2,1,0:T(8,128)S(1)} %get-tuple-element.19), channel_id=1, source_target_pairs={{0,1},{1,2},{2,3},{3,4},{4,5},{5,6},{6,7},{8,9},{9,10},{10,11},{11... | collective-permute-start | bytes 798728 | tf_op jit(solution)/shard_map/ppermute | solution.py:688
  13.6 1.3 collective-permute-start.3
  14.9 2.0 %collective-permute-done.2.zb = f32[13,40,128]{2,1,0:T(8,128)S(1)} collective-permute-done((f32[13,40,128]{2,1,0:T(8,128)S(1)}, f32[13,40,128]{2,1,0:T(8,128)S(1)}, u32[]{:S(2)}, u32[]{:S(2)}) %collective-permute-start.2) | collective-permute-done | bytes 266272 | tf_op jit(solution)/shard_map/ppermute | solution.py:688
  16.9 5.0 %collective-permute-done.3.za = f32[13,40,128]{2,1,0:T(8,128)S(1)} collective-permute-done((f32[13,40,128]{2,1,0:T(8,128)S(1)}, f32[13,40,128]{2,1,0:T(8,128)S(1)}, u32[]{:S(2)}, u32[]{:S(2)}) %collective-permute-start.3) | collective-permute-done | bytes 266272 | tf_op jit(solution)/shard_map/ppermute | solution.py:688
  23.0 5.3 %collective-permute-start.4 = (f32[11,40,128]{2,1,0:T(8,128)S(1)}, f32[11,40,128]{2,1,0:T(8,128)S(1)}, u32[]{:S(2)}, u32[]{:S(2)}) collective-permute-start(f32[11,40,128]{2,1,0:T(8,128)S(1)} %get-tuple-element.22), channel_id=1, source_target_pairs={{0,8},{8,16},{16,24},{1,9},{9,17},{17,25},{2,10},{10,18},{18,26},{... | collective-permute-start | bytes 675848 | tf_op jit(solution)/shard_map/ppermute | solution.py:688
  28.3 1.3 collective-permute-start.5
  29.6 2.7 %collective-permute-done.4.before = f32[11,40,128]{2,1,0:T(8,128)S(1)} collective-permute-done((f32[11,40,128]{2,1,0:T(8,128)S(1)}, f32[11,40,128]{2,1,0:T(8,128)S(1)}, u32[]{:S(2)}, u32[]{:S(2)}) %collective-permute-start.4) | collective-permute-done | bytes 225312 | tf_op jit(solution)/shard_map/ppermute | solution.py:688
  32.3 3.8 %collective-permute-done.5.after = f32[11,40,128]{2,1,0:T(8,128)S(1)} collective-permute-done((f32[11,40,128]{2,1,0:T(8,128)S(1)}, f32[11,40,128]{2,1,0:T(8,128)S(1)}, u32[]{:S(2)}, u32[]{:S(2)}) %collective-permute-start.5) | collective-permute-done | bytes 225312 | tf_op jit(solution)/shard_map/ppermute | solution.py:688
  36.1 2.3 %down0.1 = (f32[10,48,256]{2,1,0:T(8,128)S(1)}, f32[8,144,128]{2,1,0:T(8,128)S(1)}, f32[6,12,48,256]{3,2,1,0:T(8,128)S(1)}, f32[12,48,256]{2,1,0:T(8,128)S(1)}, f32[12,48,256]{2,1,0:T(8,128)S(1)}) custom-call(f32[3,18,48,128]{3,2,1,0:T(8,128)S(1)} %get-tuple-element.21.whole, f32[11,40,128]{2,1,0:T(8,128)S(1)} %collective-permute-done.4.before, ...), custom_call_target="tpu_custom_call" | custom-call | tf_op jit(solution)/shard_map/down0/pallas_call | solution.py:672
  39.2 23.6 %all_to_all.15.own.later = f32[8,144,128]{2,1,0:T(8,128)S(1)} all-to-all(f32[8,144,128]{2,1,0:T(8,128)S(1)} %get-tuple-element.24), channel_id=1, replica_groups=mesh['gx'=16,'gy'=4,'gz'=8] {'gz'}, dimensions={0} | all-to-all | bytes 1179648 | tf_op jit(solution)/shard_map/all_to_all | solution.py:720
  62.9 4.1 %collective-permute-start.7 = (f32[8,144,128]{2,1,0:T(8,128)S(1)}, f32[8,144,128]{2,1,0:T(8,128)S(1)}, u32[]{:S(2)}, u32[]{:S(2)}) collective-permute-start(f32[8,144,128]{2,1,0:T(8,128)S(1)} %all_to_all.15.own.later), channel_id=1, source_target_pairs={{32,0},{64,32},{96,64},{128,96},{160,128},{192,160},{224,192},{256... | collective-permute-start | bytes 1769480 | tf_op jit(solution)/shard_map/ppermute | solution.py:688
  67.0 2.0 %collective-permute-start.6 = (f32[8,144,128]{2,1,0:T(8,128)S(1)}, f32[8,144,128]{2,1,0:T(8,128)S(1)}, u32[]{:S(2)}, u32[]{:S(2)}) collective-permute-start(f32[8,144,128]{2,1,0:T(8,128)S(1)} %all_to_all.15.own.later), channel_id=1, source_target_pairs={{0,32},{32,64},{64,96},{96,128},{128,160},{160,192},{192,224},{224... | collective-permute-start | bytes 1769480 | tf_op jit(solution)/shard_map/ppermute | solution.py:688
  69.0 7.9 %collective-permute-done.7.xa = f32[8,144,128]{2,1,0:T(8,128)S(1)} collective-permute-done((f32[8,144,128]{2,1,0:T(8,128)S(1)}, f32[8,144,128]{2,1,0:T(8,128)S(1)}, u32[]{:S(2)}, u32[]{:S(2)}) %collective-permute-start.7) | collective-permute-done | bytes 589856 | tf_op jit(solution)/shard_map/ppermute | solution.py:688
  76.9 5.1 %down1.1 = (f32[16,16,128]{2,1,0:T(8,128)S(1)}, f32[6,40,48,128]{3,2,1,0:T(8,128)S(1)}, f32[40,48,128]{2,1,0:T(8,128)S(1)}, f32[40,48,128]{2,1,0:T(8,128)S(1)}, ...) custom-call(s32[4]{0:T(128)S(1)} %pad_add_fusion.pos, ...), custom_call_target="tpu_custom_call" | custom-call | tf_op jit(solution)/shard_map/down1/pallas_call | solution.py:672
  82.0 2.5 %copy-done = f32[6,40,48,128]{3,2,1,0:T(8,128)} copy-done((f32[6,40,48,128]{3,2,1,0:T(8,128)}, f32[6,40,48,128]{3,2,1,0:T(8,128)S(1)}, u32[]{:S(2)}) %copy-start) | copy-done | bytes 5898264
  84.6 1.2 copy-done.9
  89.1 16.9 %all_to_all.16 = f32[16,16,128]{2,1,0:T(8,128)S(1)} all-to-all(f32[16,16,128]{2,1,0:T(8,128)S(1)} %get-tuple-element.25), channel_id=1, replica_groups=mesh['gx'=16,'gy'=4,'gz'=8] {'gx'}, dimensions={0} | all-to-all | bytes 262144 | tf_op jit(solution)/shard_map/all_to_all | solution.py:747
  106.9 4.3 %all-to-all-start.2 = ((f32[4,256,128]{2,1,0:T(8,128)}), f32[4,256,128]{2,1,0:T(8,128)}, u32[]{:S(2)}, u32[]{:S(2)}) async-start(f32[4,256,128]{2,1,0:T(8,128)} %broadcast_in_dim.8), calls=%async_computation.2 | async-start | bytes 1048576 | tf_op jit(solution)/shard_map/all_to_all | solution.py:750
  111.2 1.3 copy-done.3
  112.5 1.1 copy-done.5
  113.6 1.1 copy-done.7
  117.8 3.1 %all-to-all-done.2.gathered = f32[4,256,128]{2,1,0:T(8,128)} async-done(((f32[4,256,128]{2,1,0:T(8,128)}), f32[4,256,128]{2,1,0:T(8,128)}, u32[]{:S(2)}, u32[]{:S(2)}) %all-to-all-start.2) | async-done | bytes 524320 | tf_op jit(solution)/shard_map/all_to_all | solution.py:750
  121.0 2.7 %copy-done.1 = f32[6,40,48,128]{3,2,1,0:T(8,128)S(1)} copy-done((f32[6,40,48,128]{3,2,1,0:T(8,128)S(1)}, f32[6,40,48,128]{3,2,1,0:T(8,128)}, u32[]{:S(2)}) %copy-start.1) | copy-done | bytes 5898264
  123.6 1.1 copy-done.8
  124.7 1.5 %copy-done.10 = f32[6,24,24,128]{3,2,1,0:T(8,128)S(1)} copy-done((f32[6,24,24,128]{3,2,1,0:T(8,128)S(1)}, f32[6,24,24,128]{3,2,1,0:T(8,128)}, u32[]{:S(2)}) %copy-start.10) | copy-done | bytes 1769496
  126.2 1.2 copy-done.12
  127.4 1.2 copy-done.14
  129.5 1.1 copy-done.22
  133.5 6.7 %up.1 = (f32[8,32,128]{2,1,0:T(8,128)}, f32[8,32,128]{2,1,0:T(8,128)}) custom-call(s32[4]{0:T(128)S(1)} %pad_add_fusion.pos, f32[4,256,128]{2,1,0:T(8,128)} %all-to-all-done.2.gathered, f32[6,24,24,128]{3,2,1,0:T(8,128)S(1)} %copy-done.10, f32[24,24,128]{2,1,0:T(8,128)S(1)} %copy-done.26, f32[24,24,128]{2,1,0:T(8,128)S(1)} %copy-done.28, ...), custom_call_target="tpu_custom_call" | custom-call | tf_op jit(solution)/shard_map/up/pallas_call | solution.py:672
  (59 shorter events, 15.3 us)
Async XLA Ops:
  2.2 8.1 %collective-permute-start = (f32[3,8,8,128]{3,2,1,0:T(8,128)S(1)}, f32[3,8,8,128]{3,2,1,0:T(8,128)S(1)}, u32[]{:S(2)}, u32[]{:S(2)}) collective-permute-start(f32[3,8,8,128]{3,2,1,0:T(8,128)S(1)} %pad_maximum_fusion.1), channel_id=1, source_target_pairs={{0,32},{32,64},{64,96},{96,128},{128,160},{160,192},{192,224},{224... | collective-permute-start | bytes 294920 | tf_op jit(solution)/shard_map/ppermute | solution.py:688
  5.0 5.4 %collective-permute-start.1 = (f32[3,8,8,128]{3,2,1,0:T(8,128)S(1)}, f32[3,8,8,128]{3,2,1,0:T(8,128)S(1)}, u32[]{:S(2)}, u32[]{:S(2)}) collective-permute-start(f32[3,8,8,128]{3,2,1,0:T(8,128)S(1)} %pad_maximum_fusion.2), channel_id=1, source_target_pairs={{32,0},{64,32},{96,64},{128,96},{160,128},{192,160},{224,192},{256... | collective-permute-start | bytes 294920 | tf_op jit(solution)/shard_map/ppermute | solution.py:688
  10.9 6.0 %collective-permute-start.2 = (f32[13,40,128]{2,1,0:T(8,128)S(1)}, f32[13,40,128]{2,1,0:T(8,128)S(1)}, u32[]{:S(2)}, u32[]{:S(2)}) collective-permute-start(f32[13,40,128]{2,1,0:T(8,128)S(1)} %get-tuple-element.19), channel_id=1, source_target_pairs={{0,1},{1,2},{2,3},{3,4},{4,5},{5,6},{6,7},{8,9},{9,10},{10,11},{11... | collective-permute-start | bytes 798728 | tf_op jit(solution)/shard_map/ppermute | solution.py:688
  13.6 8.3 %collective-permute-start.3 = (f32[13,40,128]{2,1,0:T(8,128)S(1)}, f32[13,40,128]{2,1,0:T(8,128)S(1)}, u32[]{:S(2)}, u32[]{:S(2)}) collective-permute-start(f32[13,40,128]{2,1,0:T(8,128)S(1)} %get-tuple-element.20), channel_id=1, source_target_pairs={{1,0},{2,1},{3,2},{4,3},{5,4},{6,5},{7,6},{9,8},{10,9},{11,10},{12... | collective-permute-start | bytes 798728 | tf_op jit(solution)/shard_map/ppermute | solution.py:688
  22.9 53.9 %copy-start.2 = (f32[3,18,48,128]{3,2,1,0:T(8,128)}, f32[3,18,48,128]{3,2,1,0:T(8,128)S(1)}, u32[]{:S(2)}) copy-start(f32[3,18,48,128]{3,2,1,0:T(8,128)S(1)} %get-tuple-element.21.whole) | copy-start | bytes 3981316
  23.0 9.3 %collective-permute-start.4 = (f32[11,40,128]{2,1,0:T(8,128)S(1)}, f32[11,40,128]{2,1,0:T(8,128)S(1)}, u32[]{:S(2)}, u32[]{:S(2)}) collective-permute-start(f32[11,40,128]{2,1,0:T(8,128)S(1)} %get-tuple-element.22), channel_id=1, source_target_pairs={{0,8},{8,16},{16,24},{1,9},{9,17},{17,25},{2,10},{10,18},{18,26},{... | collective-permute-start | bytes 675848 | tf_op jit(solution)/shard_map/ppermute | solution.py:688
  28.3 7.8 %collective-permute-start.5 = (f32[11,40,128]{2,1,0:T(8,128)S(1)}, f32[11,40,128]{2,1,0:T(8,128)S(1)}, u32[]{:S(2)}, u32[]{:S(2)}) collective-permute-start(f32[11,40,128]{2,1,0:T(8,128)S(1)} %get-tuple-element.23), channel_id=1, source_target_pairs={{8,0},{16,8},{24,16},{9,1},{17,9},{25,17},{10,2},{18,10},{26,18},{... | collective-permute-start | bytes 675848 | tf_op jit(solution)/shard_map/ppermute | solution.py:688
  32.3 44.6 %copy-start.15 = (f32[11,40,128]{2,1,0:T(8,128)}, f32[11,40,128]{2,1,0:T(8,128)S(1)}, u32[]{:S(2)}) copy-start(f32[11,40,128]{2,1,0:T(8,128)S(1)} %collective-permute-done.4.before) | copy-start | bytes 675844
  36.1 40.8 %copy-start.17 = (f32[11,40,128]{2,1,0:T(8,128)}, f32[11,40,128]{2,1,0:T(8,128)S(1)}, u32[]{:S(2)}) copy-start(f32[11,40,128]{2,1,0:T(8,128)S(1)} %collective-permute-done.5.after) | copy-start | bytes 675844
  39.2 37.7 %copy-start.6 = (f32[12,48,256]{2,1,0:T(8,128)}, f32[12,48,256]{2,1,0:T(8,128)S(1)}, u32[]{:S(2)}) copy-start(f32[12,48,256]{2,1,0:T(8,128)S(1)} %get-tuple-element.34.scaled.scaled0) | copy-start | bytes 1769476
  39.2 37.7 %copy-start.21 = (f32[12,48,256]{2,1,0:T(8,128)}, f32[12,48,256]{2,1,0:T(8,128)S(1)}, u32[]{:S(2)}) copy-start(f32[12,48,256]{2,1,0:T(8,128)S(1)} %get-tuple-element.33.diagonal0) | copy-start | bytes 1769476
  62.9 19.1 %copy-start.4 = (f32[8,144,128]{2,1,0:T(8,128)}, f32[8,144,128]{2,1,0:T(8,128)S(1)}, u32[]{:S(2)}) copy-start(f32[8,144,128]{2,1,0:T(8,128)S(1)} %all_to_all.15.own.later) | copy-start | bytes 1769476
  62.9 14.0 %collective-permute-start.7 = (f32[8,144,128]{2,1,0:T(8,128)S(1)}, f32[8,144,128]{2,1,0:T(8,128)S(1)}, u32[]{:S(2)}, u32[]{:S(2)}) collective-permute-start(f32[8,144,128]{2,1,0:T(8,128)S(1)} %all_to_all.15.own.later), channel_id=1, source_target_pairs={{32,0},{64,32},{96,64},{128,96},{160,128},{192,160},{224,192},{256... | collective-permute-start | bytes 1769480 | tf_op jit(solution)/shard_map/ppermute | solution.py:688
  67.0 9.9 %collective-permute-start.6 = (f32[8,144,128]{2,1,0:T(8,128)S(1)}, f32[8,144,128]{2,1,0:T(8,128)S(1)}, u32[]{:S(2)}, u32[]{:S(2)}) collective-permute-start(f32[8,144,128]{2,1,0:T(8,128)S(1)} %all_to_all.15.own.later), channel_id=1, source_target_pairs={{0,32},{32,64},{64,96},{96,128},{128,160},{160,192},{192,224},{224... | collective-permute-start | bytes 1769480 | tf_op jit(solution)/shard_map/ppermute | solution.py:688
  82.0 2.5 %copy-start = (f32[6,40,48,128]{3,2,1,0:T(8,128)}, f32[6,40,48,128]{3,2,1,0:T(8,128)S(1)}, u32[]{:S(2)}) copy-start(f32[6,40,48,128]{3,2,1,0:T(8,128)S(1)} %get-tuple-element.29.weights1) | copy-start | bytes 17694724
  84.6 1.2 copy-start.9
  85.8 0.9 copy-start.11
  86.7 1.0 copy-start.13
  106.9 14.1 %all-to-all-start.2 = ((f32[4,256,128]{2,1,0:T(8,128)}), f32[4,256,128]{2,1,0:T(8,128)}, u32[]{:S(2)}, u32[]{:S(2)}) async-start(f32[4,256,128]{2,1,0:T(8,128)} %broadcast_in_dim.8), calls=%async_computation.2 | async-start | bytes 1048576 | tf_op jit(solution)/shard_map/all_to_all | solution.py:750
  111.2 1.3 copy-start.3
  112.5 1.1 copy-start.5
  113.6 1.1 copy-start.7
  115.6 0.9 copy-start.18
  121.0 2.7 %copy-start.1 = (f32[6,40,48,128]{3,2,1,0:T(8,128)S(1)}, f32[6,40,48,128]{3,2,1,0:T(8,128)}, u32[]{:S(2)}) copy-start(f32[6,40,48,128]{3,2,1,0:T(8,128)} %copy-done) | copy-start | bytes 17694724
  123.6 1.1 copy-start.8
  124.7 1.5 %copy-start.10 = (f32[6,24,24,128]{3,2,1,0:T(8,128)S(1)}, f32[6,24,24,128]{3,2,1,0:T(8,128)}, u32[]{:S(2)}) copy-start(f32[6,24,24,128]{3,2,1,0:T(8,128)} %copy-done.9) | copy-start | bytes 5308420
  126.2 1.2 copy-start.12
  127.4 1.2 copy-start.14
  129.5 1.1 copy-start.22
  130.6 1.0 copy-start.24
  131.6 1.0 copy-start.26
  132.6 1.0 copy-start.28
  (6 other events, 4.8 us)

commit v8 on v7

--- a/solution.py
+++ b/solution.py
@@ -323,7 +323,7 @@
 
 
 def down1(
-    pos, own, xb, xa, message, weights1, scaled1, iterate1, weights2, scaled2, iterate2,
+    pos, own, xb, xa, earlier, message, weights1, scaled1, iterate1, weights2, scaled2, iterate2,
     ext1, diagonal1, start1, sums1, ext2, diagonal2, start2, sums2, thin, thick,
 ):
     depth = scaled1.shape[0] - 8
@@ -665,7 +665,7 @@
         )
 
 
-def call(body, name, outs, scratch, pos, args, flops=0):
+def call(body, name, outs, scratch, pos, args):
     vmem = pl.BlockSpec(memory_space=pltpu.VMEM)
     smem = [pl.BlockSpec(memory_space=pltpu.SMEM)] if pos is not None else []
     operands = ([pos] if pos is not None else []) + list(args)
@@ -676,7 +676,6 @@
         in_specs=smem + [vmem] * len(args),
         out_specs=[vmem] * len(outs),
         scratch_shapes=[pltpu.VMEM(shape, F32) for shape in scratch],
-        cost_estimate=pl.CostEstimate(flops=flops, bytes_accessed=0, transcendentals=0) if flops else None,
         compiler_params=pltpu.CompilerParams(vmem_limit_bytes=32 * 2**20),
     )(*operands)
 
@@ -727,7 +726,6 @@
         [(3, depth) + plane0],
         None,
         (whole0, before0, after0, weights0, scaled0, whole1),
-        10**9,
     )[0]
     plane1, plane2 = (48, 128), (24, 128)
     depth2 = depth1 // 2
@@ -741,7 +739,7 @@
         + [(3,) + tall2, tall2, (depth2 + 2,) + plane2, (3 * depth2 // 2, 8, 128)]
         + [(3 * depth2,) + plane2, (6, 4 * group, 128)],
         pos,
-        (whole1, xb, xa),
+        (whole1, xb, xa, outer0),
     )
 
     gathered = lax.all_to_all(message, "gx", 0, 0)

time: 141 us -> 118 us (0.84)
  local copies, waits for them, and re-layouts: 28.9 us -> 1.63 us
  blocking collectives: 40.6 us -> 53.9 us
  starting transfers between devices: 28 us -> 23.7 us
  waiting for transfers between devices: 24.6 us -> 20.8 us
    unnamed x58 -> x0, local copies, waits for them, and re-layouts: 26.4 us -> none
    all_to_all x0 -> x1, blocking collectives: none -> 13.2 us  [on_device(): gathered = lax.all_to_all(gathered, 'gy', 0, 0)]
    all_to_all x1 -> x0, starting transfers between devices: 4.31 us -> none  [on_device(): gathered = lax.all_to_all(gathered, 'gy', 0, 0)]
    all_to_all x1 -> x0, waiting for transfers between devices: 3.15 us -> none  [on_device(): gathered = lax.all_to_all(gathered, 'gy', 0, 0)]
  transfers between devices with their start and end apart: 9 -> 8, of which waited for: 6 -> 5; matrix products, arithmetic and copies ran while one was open for 1% -> 1% of each run, Pallas kernels for 0% -> 1%
where the time goes in v8:
time: 118 us; the launch traced here: 117 us
  blocking collectives  53.9 us (46%)
  starting transfers between devices  23.7 us (20%)
  waiting for transfers between devices  20.8 us (18%)
  Pallas kernels  15.6 us (13%)
  local copies, waits for them, and re-layouts  1.63 us (1%)
    all_to_all x1, blocking collectives, on_device(): whole1 = lax.all_to_all(message, 'gz', 0, 0)  23.7 us
    all_to_all x1, blocking collectives, on_device(): gathered = lax.all_to_all(message, 'gx', 0, 0)  17 us
    ppermute x4, waiting for transfers between devices, exchange(): lax.ppermute(down_values, axis, down_pairs)  16.1 us
    pallas_call x6, Pallas kernels, call(): pl.pallas_call(body, name=name, out_shape=[jax.ShapeDtypeStruct(shape, F3...  15.6 us
    all_to_all x1, blocking collectives, on_device(): gathered = lax.all_to_all(gathered, 'gy', 0, 0)  13.2 us
    ppermute x4, starting transfers between devices, exchange(): lax.ppermute(up_values, axis, up_pairs)  12.7 us
    ppermute x4, starting transfers between devices, exchange(): lax.ppermute(down_values, axis, down_pairs)  10.9 us
    ppermute x4, waiting for transfers between devices, exchange(): lax.ppermute(up_values, axis, up_pairs)  4.74 us
  transfers between devices with their start and end apart: 8, of which 5 were waited for; matrix products, arithmetic and copies ran while one was open for 1% of the time, Pallas kernels for 1%

profile of v8, /device:TPU:1, one launch (start us, length us, event | category | flops | bytes accessed | tf_op | source)
XLA Modules:
  0.0 117.5 jit_solution(16341885511676196379)
XLA Ops:
  0.6 0.8 slice_bitcast_fusion.2
  1.4 0.8 slice_bitcast_fusion
  2.2 2.7 %collective-permute-start = (f32[3,8,8,128]{3,2,1,0:T(8,128)S(1)}, f32[3,8,8,128]{3,2,1,0:T(8,128)S(1)}, u32[]{:S(2)}, u32[]{:S(2)}) collective-permute-start(f32[3,8,8,128]{3,2,1,0:T(8,128)S(1)} %pad_maximum_fusion.1), channel_id=1, source_target_pairs={{0,32},{32,64},{64,96},{96,128},{128,160},{160,192},{192,224},{224... | collective-permute-start | bytes 294920 | tf_op jit(solution)/shard_map/ppermute | solution.py:687
  5.0 4.2 %collective-permute-start.1 = (f32[3,8,8,128]{3,2,1,0:T(8,128)S(1)}, f32[3,8,8,128]{3,2,1,0:T(8,128)S(1)}, u32[]{:S(2)}, u32[]{:S(2)}) collective-permute-start(f32[3,8,8,128]{3,2,1,0:T(8,128)S(1)} %pad_maximum_fusion.2), channel_id=1, source_target_pairs={{32,0},{64,32},{96,64},{128,96},{160,128},{192,160},{224,192},{256... | collective-permute-start | bytes 294920 | tf_op jit(solution)/shard_map/ppermute | solution.py:687
  9.2 1.1 pad_maximum_fusion.own
  10.2 0.1 pad_add_fusion.pos
  10.3 0.0 collective-permute-done.xb
  10.3 0.0 collective-permute-done.1.xa
  10.3 0.6 packz.1
  10.9 2.7 %collective-permute-start.2 = (f32[13,40,128]{2,1,0:T(8,128)S(1)}, f32[13,40,128]{2,1,0:T(8,128)S(1)}, u32[]{:S(2)}, u32[]{:S(2)}) collective-permute-start(f32[13,40,128]{2,1,0:T(8,128)S(1)} %get-tuple-element.19), channel_id=1, source_target_pairs={{0,1},{1,2},{2,3},{3,4},{4,5},{5,6},{6,7},{8,9},{9,10},{10,11},{11... | collective-permute-start | bytes 798728 | tf_op jit(solution)/shard_map/ppermute | solution.py:687
  13.6 1.3 %collective-permute-start.3 = (f32[13,40,128]{2,1,0:T(8,128)S(1)}, f32[13,40,128]{2,1,0:T(8,128)S(1)}, u32[]{:S(2)}, u32[]{:S(2)}) collective-permute-start(f32[13,40,128]{2,1,0:T(8,128)S(1)} %get-tuple-element.20), channel_id=1, source_target_pairs={{1,0},{2,1},{3,2},{4,3},{5,4},{6,5},{7,6},{9,8},{10,9},{11,10},{12... | collective-permute-start | bytes 798728 | tf_op jit(solution)/shard_map/ppermute | solution.py:687
  14.9 2.0 %collective-permute-done.2.zb = f32[13,40,128]{2,1,0:T(8,128)S(1)} collective-permute-done((f32[13,40,128]{2,1,0:T(8,128)S(1)}, f32[13,40,128]{2,1,0:T(8,128)S(1)}, u32[]{:S(2)}, u32[]{:S(2)}) %collective-permute-start.2) | collective-permute-done | bytes 266272 | tf_op jit(solution)/shard_map/ppermute | solution.py:687
  16.9 5.0 %collective-permute-done.3.za = f32[13,40,128]{2,1,0:T(8,128)S(1)} collective-permute-done((f32[13,40,128]{2,1,0:T(8,128)S(1)}, f32[13,40,128]{2,1,0:T(8,128)S(1)}, u32[]{:S(2)}, u32[]{:S(2)}) %collective-permute-start.3) | collective-permute-done | bytes 266272 | tf_op jit(solution)/shard_map/ppermute | solution.py:687
  22.0 1.0 pack0.1
  22.9 5.3 %collective-permute-start.4 = (f32[11,40,128]{2,1,0:T(8,128)S(1)}, f32[11,40,128]{2,1,0:T(8,128)S(1)}, u32[]{:S(2)}, u32[]{:S(2)}) collective-permute-start(f32[11,40,128]{2,1,0:T(8,128)S(1)} %get-tuple-element.22), channel_id=1, source_target_pairs={{0,8},{8,16},{16,24},{1,9},{9,17},{17,25},{2,10},{10,18},{18,26},{... | collective-permute-start | bytes 675848 | tf_op jit(solution)/shard_map/ppermute | solution.py:687
  28.3 1.3 %collective-permute-start.5 = (f32[11,40,128]{2,1,0:T(8,128)S(1)}, f32[11,40,128]{2,1,0:T(8,128)S(1)}, u32[]{:S(2)}, u32[]{:S(2)}) collective-permute-start(f32[11,40,128]{2,1,0:T(8,128)S(1)} %get-tuple-element.23), channel_id=1, source_target_pairs={{8,0},{16,8},{24,16},{9,1},{17,9},{25,17},{10,2},{18,10},{26,18},{... | collective-permute-start | bytes 675848 | tf_op jit(solution)/shard_map/ppermute | solution.py:687
  29.6 2.7 %collective-permute-done.4.before = f32[11,40,128]{2,1,0:T(8,128)S(1)} collective-permute-done((f32[11,40,128]{2,1,0:T(8,128)S(1)}, f32[11,40,128]{2,1,0:T(8,128)S(1)}, u32[]{:S(2)}, u32[]{:S(2)}) %collective-permute-start.4) | collective-permute-done | bytes 225312 | tf_op jit(solution)/shard_map/ppermute | solution.py:687
  32.3 3.8 %collective-permute-done.5.after = f32[11,40,128]{2,1,0:T(8,128)S(1)} collective-permute-done((f32[11,40,128]{2,1,0:T(8,128)S(1)}, f32[11,40,128]{2,1,0:T(8,128)S(1)}, u32[]{:S(2)}, u32[]{:S(2)}) %collective-permute-start.5) | collective-permute-done | bytes 225312 | tf_op jit(solution)/shard_map/ppermute | solution.py:687
  36.1 2.2 %down0.1 = (f32[10,48,256]{2,1,0:T(8,128)S(1)}, f32[8,144,128]{2,1,0:T(8,128)S(1)}, f32[6,12,48,256]{3,2,1,0:T(8,128)S(1)}, f32[12,48,256]{2,1,0:T(8,128)S(1)}, f32[12,48,256]{2,1,0:T(8,128)S(1)}) custom-call(f32[3,18,48,128]{3,2,1,0:T(8,128)S(1)} %get-tuple-element.21.whole, f32[11,40,128]{2,1,0:T(8,128)S(1)} %collective-permute-done.4.before, ...), custom_call_target="tpu_custom_call" | custom-call | tf_op jit(solution)/shard_map/down0/pallas_call | solution.py:672
  38.3 23.7 %all_to_all.15.later.own = f32[8,144,128]{2,1,0:T(8,128)S(1)} all-to-all(f32[8,144,128]{2,1,0:T(8,128)S(1)} %get-tuple-element.24), channel_id=1, replica_groups=mesh['gx'=16,'gy'=4,'gz'=8] {'gz'}, dimensions={0} | all-to-all | bytes 1179648 | tf_op jit(solution)/shard_map/all_to_all | solution.py:719
  62.0 4.1 %collective-permute-start.7 = (f32[8,144,128]{2,1,0:T(8,128)S(1)}, f32[8,144,128]{2,1,0:T(8,128)S(1)}, u32[]{:S(2)}, u32[]{:S(2)}) collective-permute-start(f32[8,144,128]{2,1,0:T(8,128)S(1)} %all_to_all.15.later.own), channel_id=1, source_target_pairs={{32,0},{64,32},{96,64},{128,96},{160,128},{192,160},{224,192},{256... | collective-permute-start | bytes 1769480 | tf_op jit(solution)/shard_map/ppermute | solution.py:687
  66.1 2.0 %collective-permute-start.6 = (f32[8,144,128]{2,1,0:T(8,128)S(1)}, f32[8,144,128]{2,1,0:T(8,128)S(1)}, u32[]{:S(2)}, u32[]{:S(2)}) collective-permute-start(f32[8,144,128]{2,1,0:T(8,128)S(1)} %all_to_all.15.later.own), channel_id=1, source_target_pairs={{0,32},{32,64},{64,96},{96,128},{128,160},{160,192},{192,224},{224... | collective-permute-start | bytes 1769480 | tf_op jit(solution)/shard_map/ppermute | solution.py:687
  68.2 0.6 rest0.1.earlier.outer0
  68.8 7.2 %collective-permute-done.7.xa = f32[8,144,128]{2,1,0:T(8,128)S(1)} collective-permute-done((f32[8,144,128]{2,1,0:T(8,128)S(1)}, f32[8,144,128]{2,1,0:T(8,128)S(1)}, u32[]{:S(2)}, u32[]{:S(2)}) %collective-permute-start.7) | collective-permute-done | bytes 589856 | tf_op jit(solution)/shard_map/ppermute | solution.py:687
  76.0 0.0 collective-permute-done.6.xb
  76.0 5.1 %down1.1 = (f32[16,16,128]{2,1,0:T(8,128)S(1)}, f32[6,40,48,128]{3,2,1,0:T(8,128)S(1)}, f32[40,48,128]{2,1,0:T(8,128)S(1)}, f32[40,48,128]{2,1,0:T(8,128)S(1)}, ...) custom-call(s32[4]{0:T(128)S(1)} %pad_add_fusion.pos, ...), custom_call_target="tpu_custom_call" | custom-call | tf_op jit(solution)/shard_map/down1/pallas_call | solution.py:672
  81.1 17.0 %all_to_all.16 = f32[16,16,128]{2,1,0:T(8,128)S(1)} all-to-all(f32[16,16,128]{2,1,0:T(8,128)S(1)} %get-tuple-element.27), channel_id=1, replica_groups=mesh['gx'=16,'gy'=4,'gz'=8] {'gx'}, dimensions={0} | all-to-all | bytes 262144 | tf_op jit(solution)/shard_map/all_to_all | solution.py:745
  98.1 13.2 %all_to_all.17.gathered = f32[4,256,128]{2,1,0:T(8,128)S(1)} all-to-all(f32[4,256,128]{2,1,0:T(8,128)S(1)} %broadcast_in_dim.8), channel_id=1, replica_groups=mesh['gx'=16,'gy'=4,'gz'=8] {'gy'}, dimensions={0} | all-to-all | bytes 1048576 | tf_op jit(solution)/shard_map/all_to_all | solution.py:748
  111.3 6.1 %up.1 = (f32[8,32,128]{2,1,0:T(8,128)}, f32[8,32,128]{2,1,0:T(8,128)}) custom-call(s32[4]{0:T(128)S(1)} %pad_add_fusion.pos, f32[4,256,128]{2,1,0:T(8,128)S(1)} %all_to_all.17.gathered, f32[6,24,24,128]{3,2,1,0:T(8,128)S(1)} %get-tuple-element.28.weights2, f32[24,24,128]{2,1,0:T(8,128)S(1)} %get-tuple-element.29.scaled2, ...), custom_call_target="tpu_custom_call" | custom-call | tf_op jit(solution)/shard_map/up/pallas_call | solution.py:672
  (3 shorter events, 0.1 us)
Async XLA Ops:
  2.2 8.1 %collective-permute-start = (f32[3,8,8,128]{3,2,1,0:T(8,128)S(1)}, f32[3,8,8,128]{3,2,1,0:T(8,128)S(1)}, u32[]{:S(2)}, u32[]{:S(2)}) collective-permute-start(f32[3,8,8,128]{3,2,1,0:T(8,128)S(1)} %pad_maximum_fusion.1), channel_id=1, source_target_pairs={{0,32},{32,64},{64,96},{96,128},{128,160},{160,192},{192,224},{224... | collective-permute-start | bytes 294920 | tf_op jit(solution)/shard_map/ppermute | solution.py:687
  5.0 5.4 %collective-permute-start.1 = (f32[3,8,8,128]{3,2,1,0:T(8,128)S(1)}, f32[3,8,8,128]{3,2,1,0:T(8,128)S(1)}, u32[]{:S(2)}, u32[]{:S(2)}) collective-permute-start(f32[3,8,8,128]{3,2,1,0:T(8,128)S(1)} %pad_maximum_fusion.2), channel_id=1, source_target_pairs={{32,0},{64,32},{96,64},{128,96},{160,128},{192,160},{224,192},{256... | collective-permute-start | bytes 294920 | tf_op jit(solution)/shard_map/ppermute | solution.py:687
  10.9 6.0 %collective-permute-start.2 = (f32[13,40,128]{2,1,0:T(8,128)S(1)}, f32[13,40,128]{2,1,0:T(8,128)S(1)}, u32[]{:S(2)}, u32[]{:S(2)}) collective-permute-start(f32[13,40,128]{2,1,0:T(8,128)S(1)} %get-tuple-element.19), channel_id=1, source_target_pairs={{0,1},{1,2},{2,3},{3,4},{4,5},{5,6},{6,7},{8,9},{9,10},{10,11},{11... | collective-permute-start | bytes 798728 | tf_op jit(solution)/shard_map/ppermute | solution.py:687
  13.6 8.3 %collective-permute-start.3 = (f32[13,40,128]{2,1,0:T(8,128)S(1)}, f32[13,40,128]{2,1,0:T(8,128)S(1)}, u32[]{:S(2)}, u32[]{:S(2)}) collective-permute-start(f32[13,40,128]{2,1,0:T(8,128)S(1)} %get-tuple-element.20), channel_id=1, source_target_pairs={{1,0},{2,1},{3,2},{4,3},{5,4},{6,5},{7,6},{9,8},{10,9},{11,10},{12... | collective-permute-start | bytes 798728 | tf_op jit(solution)/shard_map/ppermute | solution.py:687
  22.9 9.3 %collective-permute-start.4 = (f32[11,40,128]{2,1,0:T(8,128)S(1)}, f32[11,40,128]{2,1,0:T(8,128)S(1)}, u32[]{:S(2)}, u32[]{:S(2)}) collective-permute-start(f32[11,40,128]{2,1,0:T(8,128)S(1)} %get-tuple-element.22), channel_id=1, source_target_pairs={{0,8},{8,16},{16,24},{1,9},{9,17},{17,25},{2,10},{10,18},{18,26},{... | collective-permute-start | bytes 675848 | tf_op jit(solution)/shard_map/ppermute | solution.py:687
  28.3 7.8 %collective-permute-start.5 = (f32[11,40,128]{2,1,0:T(8,128)S(1)}, f32[11,40,128]{2,1,0:T(8,128)S(1)}, u32[]{:S(2)}, u32[]{:S(2)}) collective-permute-start(f32[11,40,128]{2,1,0:T(8,128)S(1)} %get-tuple-element.23), channel_id=1, source_target_pairs={{8,0},{16,8},{24,16},{9,1},{17,9},{25,17},{10,2},{18,10},{26,18},{... | collective-permute-start | bytes 675848 | tf_op jit(solution)/shard_map/ppermute | solution.py:687
  62.0 14.0 %collective-permute-start.7 = (f32[8,144,128]{2,1,0:T(8,128)S(1)}, f32[8,144,128]{2,1,0:T(8,128)S(1)}, u32[]{:S(2)}, u32[]{:S(2)}) collective-permute-start(f32[8,144,128]{2,1,0:T(8,128)S(1)} %all_to_all.15.later.own), channel_id=1, source_target_pairs={{32,0},{64,32},{96,64},{128,96},{160,128},{192,160},{224,192},{256... | collective-permute-start | bytes 1769480 | tf_op jit(solution)/shard_map/ppermute | solution.py:687
  66.1 9.9 %collective-permute-start.6 = (f32[8,144,128]{2,1,0:T(8,128)S(1)}, f32[8,144,128]{2,1,0:T(8,128)S(1)}, u32[]{:S(2)}, u32[]{:S(2)}) collective-permute-start(f32[8,144,128]{2,1,0:T(8,128)S(1)} %all_to_all.15.later.own), channel_id=1, source_target_pairs={{0,32},{32,64},{64,96},{96,128},{128,160},{160,192},{192,224},{224... | collective-permute-start | bytes 1769480 | tf_op jit(solution)/shard_map/ppermute | solution.py:687

commit v9 on v8

--- a/solution.py
+++ b/solution.py
@@ -114,6 +114,11 @@
 def masked(pos, xb, xa, index):
     before = jnp.where(pos[0] > 0, xb[index], 0.0)
     return before, jnp.where(pos[0] < pos[3] - 1, xa[index], 0.0)
+
+
+def packx(own, last, first):
+    last[...] = own[:, :, 24:]
+    first[...] = own[:, :, :8]
 
 
 def packz(pos, own, xb, xa, last, first):
@@ -410,9 +415,10 @@
     quarter = half // 2
     group = quarter // 2
     place2 = []
-    for at in range(6):
-        to = 64 * (at % 2) + 16 * lax.rem(pos[1] + at // 2, 4)
+    for plane in range(quarter):
+        to = 64 * (plane // group) + 16 * lax.rem(pos[1] + plane % group, 4)
         place2.append(matrix((128, 128), lambda row, lane, to=to: (row < 32) & (lane == row // 2 + to), 0.125))
+        thick[plane] = jnp.zeros((16, 128), F32)
     for index in range(3):
         for plane in range(quarter):
             if index == 0:
@@ -431,33 +437,40 @@
                 total = ext2[index, 2 * plane + 4, 0:8, :] + ext2[index, 2 * plane + 5, 0:8, :]
             at = index * quarter + plane
             sums2[at] = total
-            side, within = divmod(plane, group)
-            thick[index * 2 + side, pl.ds(within, 4, stride=group), :] = (
+            thick[plane, pl.ds(index, 4, stride=3), :] = (
                 sums2[at, pl.ds(0, 4, stride=2), :] + sums2[at, pl.ds(1, 4, stride=2), :]
             )
     result = dot(thick[0], place2[0])
-    for at in range(1, 6):
-        result = result + dot(thick[at], place2[at])
+    for plane in range(1, quarter):
+        result = result + dot(thick[plane], place2[plane])
     copies(message, result)
+
+
+def packy(pieces, message):
+    for at in range(pieces.shape[0]):
+        copies(message.at[:, 12 * at : 12 * at + 12, :], pieces[at, 0:12, :])
 
 
 def bottom(gathered, whole, weights, scaled, update, values):
     group = weights.shape[1]
     rows = weights.shape[2]
-    place = lax.rem(lane_of(gathered.shape[1:]) // 16, 4)
-    for index in range(3):
-        total = gathered[0]
-        for source in range(1, 4):
-            total = jnp.where(place == (source + index) % 4, gathered[source], total)
-        if index:
-            total = jnp.where(place + index < 4, roll(total, -16 * index, 1), roll(total, 64 - 16 * index, 1))
-        whole[index] = total
     shape = (rows, 128)
     row, lane = row_of(shape), lane_of(shape)
     column = lax.rem(lane, 64)
+    quarter = column // 16
+    for index in range(3):
+        pieces = [gathered[source, pl.ds(index, rows, stride=3), :] for source in range(4)]
+        for plane in range(group):
+            total = pieces[0]
+            for source in range(1, 4):
+                total = jnp.where(quarter == (source + plane) % 4, pieces[source], total)
+            if plane:
+                near, far = roll(total, -16 * plane, 1), roll(total, 64 - 16 * plane, 1)
+                total = jnp.where(quarter + plane < 4, near, far)
+            whole[index, plane] = total
 
     def plane_at(index, plane):
-        return whole[index, pl.ds(plane, rows, stride=group), :]
+        return whole[index, plane]
 
     def around(get, plane):
         middle = get(plane)
@@ -693,10 +706,9 @@
     planes = right_side.shape[0]
     arrays = (right_side, acoef, beta)
 
-    last = jnp.stack([value[:, 24:] for value in arrays])
-    first = jnp.stack([value[:, :8] for value in arrays])
+    own = jnp.stack(arrays)
+    last, first = call(packx, "packx", [(3, planes, 8, 128)] * 2, [], None, (own,))
     xb, xa = exchange(last, first, "gx", True)
-    own = jnp.stack(arrays)
     last, first = call(packz, "packz", [(sum(REACH), 40, 128)] * 2, [], pos, (own, xb, xa))
     zb, za = exchange(last, first, "gz", False)
     depth = planes + 2 * DEEP
@@ -734,17 +746,16 @@
     message, weights1, scaled1, iterate1, weights2, scaled2, iterate2 = call(
         down1,
         "down1",
-        [(ranks, 4 * group, 128), (6,) + tall1, tall1, tall1, (6,) + tall2, tall2, tall2],
+        [(ranks, 16, 128), (6,) + tall1, tall1, tall1, (6,) + tall2, tall2, tall2],
         [(3,) + tall1, tall1, (depth1 + 2,) + plane1, (3 * depth2,) + plane1]
         + [(3,) + tall2, tall2, (depth2 + 2,) + plane2, (3 * depth2 // 2, 8, 128)]
-        + [(3 * depth2,) + plane2, (6, 4 * group, 128)],
+        + [(3 * depth2,) + plane2, (2 * group, 16, 128)],
         pos,
         (whole1, xb, xa, outer0),
     )
 
     gathered = lax.all_to_all(message, "gx", 0, 0)
-    gathered = gathered.reshape(1, ranks * 4 * group, 128)
-    gathered = jnp.broadcast_to(gathered, (turns,) + gathered.shape[1:])
+    gathered = call(packy, "packy", [(turns, 12 * ranks, 128)], [], None, (gathered,))[0]
     gathered = lax.all_to_all(gathered, "gy", 0, 0)
 
     rows3 = 4 * ranks
@@ -753,7 +764,7 @@
         up,
         "up",
         [right_side.shape, right_side.shape],
-        [(3, rows3 * group, 128), (6, group) + plane3, (group,) + plane3, (group,) + plane3, (2, group) + plane3]
+        [(3, group) + plane3, (6, group) + plane3, (group,) + plane3, (group,) + plane3, (2, group) + plane3]
         + [(group,) + plane2, (2 * group + 4,) + plane2, (10,) + plane2, (8,) + plane2, (8,) + plane2, (6,) + plane2]
         + [(6,) + plane1, (12,) + plane1, (10,) + plane1, (10,) + plane1, (8,) + plane1]
         + [(8,) + plane1, (depth - 4,) + plane0, (depth - 6,) + plane0, (depth - 6,) + plane0, (depth - 2,) + plane0],

time: 118 us -> 116 us (0.983)
  local copies, waits for them, and re-layouts: 1.63 us -> 0 us
  blocking collectives: 53.9 us -> 52.5 us
    another operation x2 -> x0, local copies, waits for them, and re-layouts: 1.6 us -> none  [on_device(): first = jnp.stack([value[:, :8] for value in arrays])]
    all_to_all x1, blocking collectives: 13.2 us -> 11.8 us  [on_device(): gathered = lax.all_to_all(gathered, 'gy', 0, 0)]
    pallas_call x6 -> x8, Pallas kernels: 15.6 us -> 15.7 us  [call(): pl.pallas_call(body, name=name, out_shape=[jax.ShapeDtypeStruct(shape, F3...]
  transfers between devices with their start and end apart: 8 -> 8, of which waited for: 5 -> 7; matrix products, arithmetic and copies ran while one was open for 1% -> 0% of each run, Pallas kernels for 1% -> 1%
where the time goes in v9:
time: 116 us
  blocking collectives  52.5 us (45%)
  starting transfers between devices  23.9 us (21%)
  waiting for transfers between devices  21.6 us (19%)
  Pallas kernels  15.7 us (14%)
    all_to_all x1, blocking collectives, on_device(): whole1 = lax.all_to_all(message, 'gz', 0, 0)  23.6 us
    all_to_all x1, blocking collectives, on_device(): gathered = lax.all_to_all(message, 'gx', 0, 0)  17 us
    ppermute x4, waiting for transfers between devices, exchange(): lax.ppermute(down_values, axis, down_pairs)  16.2 us
    pallas_call x8, Pallas kernels, call(): pl.pallas_call(body, name=name, out_shape=[jax.ShapeDtypeStruct(shape, F3...  15.7 us
    ppermute x4, starting transfers between devices, exchange(): lax.ppermute(up_values, axis, up_pairs)  13 us
    all_to_all x1, blocking collectives, on_device(): gathered = lax.all_to_all(gathered, 'gy', 0, 0)  11.8 us
    ppermute x4, starting transfers between devices, exchange(): lax.ppermute(down_values, axis, down_pairs)  10.9 us
    ppermute x4, waiting for transfers between devices, exchange(): lax.ppermute(up_values, axis, up_pairs)  5.41 us
  transfers between devices with their start and end apart: 8, of which 7 were waited for; matrix products, arithmetic and copies ran while one was open for 0% of the time, Pallas kernels for 1%

profile of v9, /device:TPU:1, one launch (start us, length us, event | category | flops | bytes accessed | tf_op | source)
XLA Modules:
  0.0 115.5 jit_solution(15238202850369709200)
XLA Ops:
  0.6 1.1 pad_maximum_fusion.own
  1.7 2.7 %collective-permute-start = (f32[3,8,8,128]{3,2,1,0:T(8,128)S(1)}, f32[3,8,8,128]{3,2,1,0:T(8,128)S(1)}, u32[]{:S(2)}, u32[]{:S(2)}) collective-permute-start(f32[3,8,8,128]{3,2,1,0:T(8,128)S(1)} %get-tuple-element.21), channel_id=1, source_target_pairs={{0,32},{32,64},{64,96},{96,128},{128,160},{160,192},{192,224},{224... | collective-permute-start | bytes 294920 | tf_op jit(solution)/shard_map/ppermute | solution.py:700
  4.4 4.2 %collective-permute-start.1 = (f32[3,8,8,128]{3,2,1,0:T(8,128)S(1)}, f32[3,8,8,128]{3,2,1,0:T(8,128)S(1)}, u32[]{:S(2)}, u32[]{:S(2)}) collective-permute-start(f32[3,8,8,128]{3,2,1,0:T(8,128)S(1)} %get-tuple-element.22), channel_id=1, source_target_pairs={{32,0},{64,32},{96,64},{128,96},{160,128},{192,160},{224,192},{256... | collective-permute-start | bytes 294920 | tf_op jit(solution)/shard_map/ppermute | solution.py:700
  8.6 0.1 pad_add_fusion.pos
  8.7 0.7 collective-permute-done.xb
  9.4 0.2 collective-permute-done.1.xa
  9.6 0.6 packz.1
  10.2 2.9 %collective-permute-start.2 = (f32[13,40,128]{2,1,0:T(8,128)S(1)}, f32[13,40,128]{2,1,0:T(8,128)S(1)}, u32[]{:S(2)}, u32[]{:S(2)}) collective-permute-start(f32[13,40,128]{2,1,0:T(8,128)S(1)} %get-tuple-element.23), channel_id=1, source_target_pairs={{0,1},{1,2},{2,3},{3,4},{4,5},{5,6},{6,7},{8,9},{9,10},{10,11},{11... | collective-permute-start | bytes 798728 | tf_op jit(solution)/shard_map/ppermute | solution.py:700
  13.1 1.3 %collective-permute-start.3 = (f32[13,40,128]{2,1,0:T(8,128)S(1)}, f32[13,40,128]{2,1,0:T(8,128)S(1)}, u32[]{:S(2)}, u32[]{:S(2)}) collective-permute-start(f32[13,40,128]{2,1,0:T(8,128)S(1)} %get-tuple-element.24), channel_id=1, source_target_pairs={{1,0},{2,1},{3,2},{4,3},{5,4},{6,5},{7,6},{9,8},{10,9},{11,10},{12... | collective-permute-start | bytes 798728 | tf_op jit(solution)/shard_map/ppermute | solution.py:700
  14.4 2.0 %collective-permute-done.2.zb = f32[13,40,128]{2,1,0:T(8,128)S(1)} collective-permute-done((f32[13,40,128]{2,1,0:T(8,128)S(1)}, f32[13,40,128]{2,1,0:T(8,128)S(1)}, u32[]{:S(2)}, u32[]{:S(2)}) %collective-permute-start.2) | collective-permute-done | bytes 266272 | tf_op jit(solution)/shard_map/ppermute | solution.py:700
  16.4 5.0 %collective-permute-done.3.za = f32[13,40,128]{2,1,0:T(8,128)S(1)} collective-permute-done((f32[13,40,128]{2,1,0:T(8,128)S(1)}, f32[13,40,128]{2,1,0:T(8,128)S(1)}, u32[]{:S(2)}, u32[]{:S(2)}) %collective-permute-start.3) | collective-permute-done | bytes 266272 | tf_op jit(solution)/shard_map/ppermute | solution.py:700
  21.4 1.0 pack0.1
  22.4 5.3 %collective-permute-start.4 = (f32[11,40,128]{2,1,0:T(8,128)S(1)}, f32[11,40,128]{2,1,0:T(8,128)S(1)}, u32[]{:S(2)}, u32[]{:S(2)}) collective-permute-start(f32[11,40,128]{2,1,0:T(8,128)S(1)} %get-tuple-element.26), channel_id=1, source_target_pairs={{0,8},{8,16},{16,24},{1,9},{9,17},{17,25},{2,10},{10,18},{18,26},{... | collective-permute-start | bytes 675848 | tf_op jit(solution)/shard_map/ppermute | solution.py:700
  27.7 1.3 %collective-permute-start.5 = (f32[11,40,128]{2,1,0:T(8,128)S(1)}, f32[11,40,128]{2,1,0:T(8,128)S(1)}, u32[]{:S(2)}, u32[]{:S(2)}) collective-permute-start(f32[11,40,128]{2,1,0:T(8,128)S(1)} %get-tuple-element.27), channel_id=1, source_target_pairs={{8,0},{16,8},{24,16},{9,1},{17,9},{25,17},{10,2},{18,10},{26,18},{... | collective-permute-start | bytes 675848 | tf_op jit(solution)/shard_map/ppermute | solution.py:700
  29.0 2.7 %collective-permute-done.4.before = f32[11,40,128]{2,1,0:T(8,128)S(1)} collective-permute-done((f32[11,40,128]{2,1,0:T(8,128)S(1)}, f32[11,40,128]{2,1,0:T(8,128)S(1)}, u32[]{:S(2)}, u32[]{:S(2)}) %collective-permute-start.4) | collective-permute-done | bytes 225312 | tf_op jit(solution)/shard_map/ppermute | solution.py:700
  31.7 3.8 %collective-permute-done.5.after = f32[11,40,128]{2,1,0:T(8,128)S(1)} collective-permute-done((f32[11,40,128]{2,1,0:T(8,128)S(1)}, f32[11,40,128]{2,1,0:T(8,128)S(1)}, u32[]{:S(2)}, u32[]{:S(2)}) %collective-permute-start.5) | collective-permute-done | bytes 225312 | tf_op jit(solution)/shard_map/ppermute | solution.py:700
  35.5 2.2 %down0.1 = (f32[10,48,256]{2,1,0:T(8,128)S(1)}, f32[8,144,128]{2,1,0:T(8,128)S(1)}, f32[6,12,48,256]{3,2,1,0:T(8,128)S(1)}, f32[12,48,256]{2,1,0:T(8,128)S(1)}, f32[12,48,256]{2,1,0:T(8,128)S(1)}) custom-call(f32[3,18,48,128]{3,2,1,0:T(8,128)S(1)} %get-tuple-element.25.whole, f32[11,40,128]{2,1,0:T(8,128)S(1)} %collective-permute-done.4.before, ...), custom_call_target="tpu_custom_call" | custom-call | tf_op jit(solution)/shard_map/down0/pallas_call | solution.py:685
  37.8 23.6 %all_to_all.15.later.own = f32[8,144,128]{2,1,0:T(8,128)S(1)} all-to-all(f32[8,144,128]{2,1,0:T(8,128)S(1)} %get-tuple-element.28), channel_id=1, replica_groups=mesh['gx'=16,'gy'=4,'gz'=8] {'gz'}, dimensions={0} | all-to-all | bytes 1179648 | tf_op jit(solution)/shard_map/all_to_all | solution.py:731
  61.4 4.1 %collective-permute-start.7 = (f32[8,144,128]{2,1,0:T(8,128)S(1)}, f32[8,144,128]{2,1,0:T(8,128)S(1)}, u32[]{:S(2)}, u32[]{:S(2)}) collective-permute-start(f32[8,144,128]{2,1,0:T(8,128)S(1)} %all_to_all.15.later.own), channel_id=1, source_target_pairs={{32,0},{64,32},{96,64},{128,96},{160,128},{192,160},{224,192},{256... | collective-permute-start | bytes 1769480 | tf_op jit(solution)/shard_map/ppermute | solution.py:700
  65.5 2.1 %collective-permute-start.6 = (f32[8,144,128]{2,1,0:T(8,128)S(1)}, f32[8,144,128]{2,1,0:T(8,128)S(1)}, u32[]{:S(2)}, u32[]{:S(2)}) collective-permute-start(f32[8,144,128]{2,1,0:T(8,128)S(1)} %all_to_all.15.later.own), channel_id=1, source_target_pairs={{0,32},{32,64},{64,96},{96,128},{128,160},{160,192},{192,224},{224... | collective-permute-start | bytes 1769480 | tf_op jit(solution)/shard_map/ppermute | solution.py:700
  67.6 0.6 rest0.1.earlier.outer0
  68.2 7.2 %collective-permute-done.7.xa = f32[8,144,128]{2,1,0:T(8,128)S(1)} collective-permute-done((f32[8,144,128]{2,1,0:T(8,128)S(1)}, f32[8,144,128]{2,1,0:T(8,128)S(1)}, u32[]{:S(2)}, u32[]{:S(2)}) %collective-permute-start.7) | collective-permute-done | bytes 589856 | tf_op jit(solution)/shard_map/ppermute | solution.py:700
  75.5 0.0 collective-permute-done.6.xb
  75.5 5.1 %down1.1 = (f32[16,16,128]{2,1,0:T(8,128)S(1)}, f32[6,40,48,128]{3,2,1,0:T(8,128)S(1)}, f32[40,48,128]{2,1,0:T(8,128)S(1)}, f32[40,48,128]{2,1,0:T(8,128)S(1)}, ...) custom-call(s32[4]{0:T(128)S(1)} %pad_add_fusion.pos, ...), custom_call_target="tpu_custom_call" | custom-call | tf_op jit(solution)/shard_map/down1/pallas_call | solution.py:685
  80.5 17.0 %all_to_all.16.pieces = f32[16,16,128]{2,1,0:T(8,128)S(1)} all-to-all(f32[16,16,128]{2,1,0:T(8,128)S(1)} %get-tuple-element.31), channel_id=1, replica_groups=mesh['gx'=16,'gy'=4,'gz'=8] {'gx'}, dimensions={0} | all-to-all | bytes 262144 | tf_op jit(solution)/shard_map/all_to_all | solution.py:757
  97.6 11.8 %all_to_all.17.gathered = f32[4,192,128]{2,1,0:T(8,128)S(1)} all-to-all(f32[4,192,128]{2,1,0:T(8,128)S(1)} %packy.1), channel_id=1, replica_groups=mesh['gx'=16,'gy'=4,'gz'=8] {'gy'}, dimensions={0} | all-to-all | bytes 786432 | tf_op jit(solution)/shard_map/all_to_all | solution.py:759
  109.4 6.1 %up.1 = (f32[8,32,128]{2,1,0:T(8,128)}, f32[8,32,128]{2,1,0:T(8,128)}) custom-call(s32[4]{0:T(128)S(1)} %pad_add_fusion.pos, f32[4,192,128]{2,1,0:T(8,128)S(1)} %all_to_all.17.gathered, f32[6,24,24,128]{3,2,1,0:T(8,128)S(1)} %get-tuple-element.32.weights2, f32[24,24,128]{2,1,0:T(8,128)S(1)} %get-tuple-element.33.scaled2, ...), custom_call_target="tpu_custom_call" | custom-call | tf_op jit(solution)/shard_map/up/pallas_call | solution.py:685
  (2 shorter events, 0.1 us)
Async XLA Ops:
  1.7 7.7 %collective-permute-start = (f32[3,8,8,128]{3,2,1,0:T(8,128)S(1)}, f32[3,8,8,128]{3,2,1,0:T(8,128)S(1)}, u32[]{:S(2)}, u32[]{:S(2)}) collective-permute-start(f32[3,8,8,128]{3,2,1,0:T(8,128)S(1)} %get-tuple-element.21), channel_id=1, source_target_pairs={{0,32},{32,64},{64,96},{96,128},{128,160},{160,192},{192,224},{224... | collective-permute-start | bytes 294920 | tf_op jit(solution)/shard_map/ppermute | solution.py:700
  4.4 5.2 %collective-permute-start.1 = (f32[3,8,8,128]{3,2,1,0:T(8,128)S(1)}, f32[3,8,8,128]{3,2,1,0:T(8,128)S(1)}, u32[]{:S(2)}, u32[]{:S(2)}) collective-permute-start(f32[3,8,8,128]{3,2,1,0:T(8,128)S(1)} %get-tuple-element.22), channel_id=1, source_target_pairs={{32,0},{64,32},{96,64},{128,96},{160,128},{192,160},{224,192},{256... | collective-permute-start | bytes 294920 | tf_op jit(solution)/shard_map/ppermute | solution.py:700
  10.2 6.2 %collective-permute-start.2 = (f32[13,40,128]{2,1,0:T(8,128)S(1)}, f32[13,40,128]{2,1,0:T(8,128)S(1)}, u32[]{:S(2)}, u32[]{:S(2)}) collective-permute-start(f32[13,40,128]{2,1,0:T(8,128)S(1)} %get-tuple-element.23), channel_id=1, source_target_pairs={{0,1},{1,2},{2,3},{3,4},{4,5},{5,6},{6,7},{8,9},{9,10},{10,11},{11... | collective-permute-start | bytes 798728 | tf_op jit(solution)/shard_map/ppermute | solution.py:700
  13.1 8.3 %collective-permute-start.3 = (f32[13,40,128]{2,1,0:T(8,128)S(1)}, f32[13,40,128]{2,1,0:T(8,128)S(1)}, u32[]{:S(2)}, u32[]{:S(2)}) collective-permute-start(f32[13,40,128]{2,1,0:T(8,128)S(1)} %get-tuple-element.24), channel_id=1, source_target_pairs={{1,0},{2,1},{3,2},{4,3},{5,4},{6,5},{7,6},{9,8},{10,9},{11,10},{12... | collective-permute-start | bytes 798728 | tf_op jit(solution)/shard_map/ppermute | solution.py:700
  22.4 9.3 %collective-permute-start.4 = (f32[11,40,128]{2,1,0:T(8,128)S(1)}, f32[11,40,128]{2,1,0:T(8,128)S(1)}, u32[]{:S(2)}, u32[]{:S(2)}) collective-permute-start(f32[11,40,128]{2,1,0:T(8,128)S(1)} %get-tuple-element.26), channel_id=1, source_target_pairs={{0,8},{8,16},{16,24},{1,9},{9,17},{17,25},{2,10},{10,18},{18,26},{... | collective-permute-start | bytes 675848 | tf_op jit(solution)/shard_map/ppermute | solution.py:700
  27.7 7.8 %collective-permute-start.5 = (f32[11,40,128]{2,1,0:T(8,128)S(1)}, f32[11,40,128]{2,1,0:T(8,128)S(1)}, u32[]{:S(2)}, u32[]{:S(2)}) collective-permute-start(f32[11,40,128]{2,1,0:T(8,128)S(1)} %get-tuple-element.27), channel_id=1, source_target_pairs={{8,0},{16,8},{24,16},{9,1},{17,9},{25,17},{10,2},{18,10},{26,18},{... | collective-permute-start | bytes 675848 | tf_op jit(solution)/shard_map/ppermute | solution.py:700
  61.4 14.0 %collective-permute-start.7 = (f32[8,144,128]{2,1,0:T(8,128)S(1)}, f32[8,144,128]{2,1,0:T(8,128)S(1)}, u32[]{:S(2)}, u32[]{:S(2)}) collective-permute-start(f32[8,144,128]{2,1,0:T(8,128)S(1)} %all_to_all.15.later.own), channel_id=1, source_target_pairs={{32,0},{64,32},{96,64},{128,96},{160,128},{192,160},{224,192},{256... | collective-permute-start | bytes 1769480 | tf_op jit(solution)/shard_map/ppermute | solution.py:700
  65.5 9.9 %collective-permute-start.6 = (f32[8,144,128]{2,1,0:T(8,128)S(1)}, f32[8,144,128]{2,1,0:T(8,128)S(1)}, u32[]{:S(2)}, u32[]{:S(2)}) collective-permute-start(f32[8,144,128]{2,1,0:T(8,128)S(1)} %all_to_all.15.later.own), channel_id=1, source_target_pairs={{0,32},{32,64},{64,96},{96,128},{128,160},{160,192},{192,224},{224... | collective-permute-start | bytes 1769480 | tf_op jit(solution)/shard_map/ppermute | solution.py:700

commit v10 on v9

--- a/solution.py
+++ b/solution.py
@@ -156,10 +156,10 @@
     for index, plane, tile, to, lanes in slots(depth):
         ends = jnp.where(four, whole[index, plane, 32:40, :], whole[index, plane, 40:48, :])
         value = jnp.concatenate([whole[index, plane, 0:32, :], ends], axis=0)
-        here = (lane >= to) & (lane < to + lanes)
+        moved, back = roll(value, to, 1), (to - lanes) % 128
         zero = jnp.zeros((40, 128), F32)
-        low[tile] = jnp.where(here, roll(value, to, 1), low.get(tile, zero))
-        high[tile] = jnp.where(here, roll(value, to + lanes, 1), high.get(tile, zero))
+        low[tile] = jnp.where((lane >= to) & (lane < to + lanes), moved, low.get(tile, zero))
+        high[tile] = jnp.where((lane >= back) & (lane < back + lanes), moved, high.get(tile, zero))
     for tile in low:
         left[tile] = low[tile]
         right[tile] = high[tile]
@@ -174,8 +174,8 @@
             ext[index, plane, :, 128:256] = jnp.zeros((48, 128), F32)
             continue
         tile, to, lanes = there[index, plane]
-        ahead = jnp.where(lane < lanes, roll(after[tile], -to, 1), 0.0)
-        value = jnp.where(lane >= 128 - lanes, roll(before[tile], -lanes - to, 1), ahead)
+        value = roll(jnp.where((lane >= to) & (lane < to + lanes), after[tile], before[tile]), -to, 1)
+        value = jnp.where((lane < lanes) | (lane >= 128 - lanes), value, 0.0)
         ext[index, plane, 0:40, 128:256] = value
         ext[index, plane, 40:48, 128:256] = value[32:40]
 
@@ -251,9 +251,8 @@
     ends = None
     for plane in range(half):
 
-        def rule(row, lane, to=32 * plane):
-            ahead = (row < 32) & (lane == to + row // 2)
-            return ahead | ((row >= 96) & (lane == to + 16 + (row - 96) // 2))
+        def rule(row, lane, ahead=-32 * plane % 128, behind=(48 - 32 * plane) % 128):
+            return ((row < 32) & (lane == ahead + row // 2)) | ((row >= 96) & (lane == behind + (row - 96) // 2))
 
         got = dot(rows_of(1, range(plane, 3 * half, half)), matrix((128, 128), rule, 0.125))
         ends = got if ends is None else ends + got
@@ -288,8 +287,8 @@
             for plane in range(per):
                 at = (2 * index + plane // 2) * 16
                 value = roll(ref[source, at : at + 16, :], 64 * (plane % 2), 1)
-                value = jnp.where(lane < 80, jnp.where(lane < 64, value, roll(ends, 64 - 32 * plane, 1)), 0.0)
-                value = jnp.where(lane >= 112, roll(ends, 96 - 32 * plane, 1), value)
+                halo = jnp.where((lane < 80) | (lane >= 112), roll(ends, 64 + 32 * plane, 1), 0.0)
+                value = jnp.where(lane < 64, value, halo)
                 if there is not None:
                     value = jnp.where(there, value, 0.0)
                 put(index, source * per + plane, value)

time: 116 us -> 116 us (level)
  transfers between devices with their start and end apart: 8 -> 8, of which waited for: 7 -> 7; matrix products, arithmetic and copies ran while one was open for 0% -> 0% of each run, Pallas kernels for 1% -> 0%
where the time goes in v10:
time: 116 us; the launch traced here: 115 us
  blocking collectives  52.5 us (45%)
  starting transfers between devices  23.9 us (21%)
  waiting for transfers between devices  21.7 us (19%)
  Pallas kernels  15.4 us (13%)
    all_to_all x1, blocking collectives, on_device(): whole1 = lax.all_to_all(message, 'gz', 0, 0)  23.6 us
    all_to_all x1, blocking collectives, on_device(): gathered = lax.all_to_all(message, 'gx', 0, 0)  17 us
    ppermute x4, waiting for transfers between devices, exchange(): lax.ppermute(down_values, axis, down_pairs)  16.3 us
    pallas_call x8, Pallas kernels, call(): pl.pallas_call(body, name=name, out_shape=[jax.ShapeDtypeStruct(shape, F3...  15.4 us
    ppermute x4, starting transfers between devices, exchange(): lax.ppermute(up_values, axis, up_pairs)  13 us
    all_to_all x1, blocking collectives, on_device(): gathered = lax.all_to_all(gathered, 'gy', 0, 0)  11.8 us
    ppermute x4, starting transfers between devices, exchange(): lax.ppermute(down_values, axis, down_pairs)  10.9 us
    ppermute x4, waiting for transfers between devices, exchange(): lax.ppermute(up_values, axis, up_pairs)  5.41 us
  transfers between devices with their start and end apart: 8, of which 7 were waited for; matrix products, arithmetic and copies ran while one was open for 0% of the time, Pallas kernels for 0%

profile of v10, /device:TPU:1, one launch (start us, length us, event | category | flops | bytes accessed | tf_op | source)
XLA Modules:
  0.0 115.3 jit_solution(13163577555046620386)
XLA Ops:
  0.6 1.1 pad_maximum_fusion.own
  1.7 2.7 %collective-permute-start = (f32[3,8,8,128]{3,2,1,0:T(8,128)S(1)}, f32[3,8,8,128]{3,2,1,0:T(8,128)S(1)}, u32[]{:S(2)}, u32[]{:S(2)}) collective-permute-start(f32[3,8,8,128]{3,2,1,0:T(8,128)S(1)} %get-tuple-element.21), channel_id=1, source_target_pairs={{0,32},{32,64},{64,96},{96,128},{128,160},{160,192},{192,224},{224... | collective-permute-start | bytes 294920 | tf_op jit(solution)/shard_map/ppermute | solution.py:699
  4.4 4.2 %collective-permute-start.1 = (f32[3,8,8,128]{3,2,1,0:T(8,128)S(1)}, f32[3,8,8,128]{3,2,1,0:T(8,128)S(1)}, u32[]{:S(2)}, u32[]{:S(2)}) collective-permute-start(f32[3,8,8,128]{3,2,1,0:T(8,128)S(1)} %get-tuple-element.22), channel_id=1, source_target_pairs={{32,0},{64,32},{96,64},{128,96},{160,128},{192,160},{224,192},{256... | collective-permute-start | bytes 294920 | tf_op jit(solution)/shard_map/ppermute | solution.py:699
  8.6 0.1 pad_add_fusion.pos
  8.7 0.7 collective-permute-done.xb
  9.4 0.2 collective-permute-done.1.xa
  9.6 0.6 packz.1
  10.2 2.9 %collective-permute-start.2 = (f32[13,40,128]{2,1,0:T(8,128)S(1)}, f32[13,40,128]{2,1,0:T(8,128)S(1)}, u32[]{:S(2)}, u32[]{:S(2)}) collective-permute-start(f32[13,40,128]{2,1,0:T(8,128)S(1)} %get-tuple-element.23), channel_id=1, source_target_pairs={{0,1},{1,2},{2,3},{3,4},{4,5},{5,6},{6,7},{8,9},{9,10},{10,11},{11... | collective-permute-start | bytes 798728 | tf_op jit(solution)/shard_map/ppermute | solution.py:699
  13.1 1.3 %collective-permute-start.3 = (f32[13,40,128]{2,1,0:T(8,128)S(1)}, f32[13,40,128]{2,1,0:T(8,128)S(1)}, u32[]{:S(2)}, u32[]{:S(2)}) collective-permute-start(f32[13,40,128]{2,1,0:T(8,128)S(1)} %get-tuple-element.24), channel_id=1, source_target_pairs={{1,0},{2,1},{3,2},{4,3},{5,4},{6,5},{7,6},{9,8},{10,9},{11,10},{12... | collective-permute-start | bytes 798728 | tf_op jit(solution)/shard_map/ppermute | solution.py:699
  14.4 2.0 %collective-permute-done.2.zb = f32[13,40,128]{2,1,0:T(8,128)S(1)} collective-permute-done((f32[13,40,128]{2,1,0:T(8,128)S(1)}, f32[13,40,128]{2,1,0:T(8,128)S(1)}, u32[]{:S(2)}, u32[]{:S(2)}) %collective-permute-start.2) | collective-permute-done | bytes 266272 | tf_op jit(solution)/shard_map/ppermute | solution.py:699
  16.4 5.0 %collective-permute-done.3.za = f32[13,40,128]{2,1,0:T(8,128)S(1)} collective-permute-done((f32[13,40,128]{2,1,0:T(8,128)S(1)}, f32[13,40,128]{2,1,0:T(8,128)S(1)}, u32[]{:S(2)}, u32[]{:S(2)}) %collective-permute-start.3) | collective-permute-done | bytes 266272 | tf_op jit(solution)/shard_map/ppermute | solution.py:699
  21.4 0.8 pack0.1
  22.2 5.3 %collective-permute-start.4 = (f32[11,40,128]{2,1,0:T(8,128)S(1)}, f32[11,40,128]{2,1,0:T(8,128)S(1)}, u32[]{:S(2)}, u32[]{:S(2)}) collective-permute-start(f32[11,40,128]{2,1,0:T(8,128)S(1)} %get-tuple-element.26), channel_id=1, source_target_pairs={{0,8},{8,16},{16,24},{1,9},{9,17},{17,25},{2,10},{10,18},{18,26},{... | collective-permute-start | bytes 675848 | tf_op jit(solution)/shard_map/ppermute | solution.py:699
  27.5 1.3 %collective-permute-start.5 = (f32[11,40,128]{2,1,0:T(8,128)S(1)}, f32[11,40,128]{2,1,0:T(8,128)S(1)}, u32[]{:S(2)}, u32[]{:S(2)}) collective-permute-start(f32[11,40,128]{2,1,0:T(8,128)S(1)} %get-tuple-element.27), channel_id=1, source_target_pairs={{8,0},{16,8},{24,16},{9,1},{17,9},{25,17},{10,2},{18,10},{26,18},{... | collective-permute-start | bytes 675848 | tf_op jit(solution)/shard_map/ppermute | solution.py:699
  28.8 2.7 %collective-permute-done.4.before = f32[11,40,128]{2,1,0:T(8,128)S(1)} collective-permute-done((f32[11,40,128]{2,1,0:T(8,128)S(1)}, f32[11,40,128]{2,1,0:T(8,128)S(1)}, u32[]{:S(2)}, u32[]{:S(2)}) %collective-permute-start.4) | collective-permute-done | bytes 225312 | tf_op jit(solution)/shard_map/ppermute | solution.py:699
  31.5 3.8 %collective-permute-done.5.after = f32[11,40,128]{2,1,0:T(8,128)S(1)} collective-permute-done((f32[11,40,128]{2,1,0:T(8,128)S(1)}, f32[11,40,128]{2,1,0:T(8,128)S(1)}, u32[]{:S(2)}, u32[]{:S(2)}) %collective-permute-start.5) | collective-permute-done | bytes 225312 | tf_op jit(solution)/shard_map/ppermute | solution.py:699
  35.3 2.1 %down0.1 = (f32[10,48,256]{2,1,0:T(8,128)S(1)}, f32[8,144,128]{2,1,0:T(8,128)S(1)}, f32[6,12,48,256]{3,2,1,0:T(8,128)S(1)}, f32[12,48,256]{2,1,0:T(8,128)S(1)}, f32[12,48,256]{2,1,0:T(8,128)S(1)}) custom-call(f32[3,18,48,128]{3,2,1,0:T(8,128)S(1)} %get-tuple-element.25.whole, f32[11,40,128]{2,1,0:T(8,128)S(1)} %collective-permute-done.4.before, ...), custom_call_target="tpu_custom_call" | custom-call | tf_op jit(solution)/shard_map/down0/pallas_call | solution.py:684
  37.5 23.6 %all_to_all.15.later.own = f32[8,144,128]{2,1,0:T(8,128)S(1)} all-to-all(f32[8,144,128]{2,1,0:T(8,128)S(1)} %get-tuple-element.28), channel_id=1, replica_groups=mesh['gx'=16,'gy'=4,'gz'=8] {'gz'}, dimensions={0} | all-to-all | bytes 1179648 | tf_op jit(solution)/shard_map/all_to_all | solution.py:730
  61.1 4.1 %collective-permute-start.7 = (f32[8,144,128]{2,1,0:T(8,128)S(1)}, f32[8,144,128]{2,1,0:T(8,128)S(1)}, u32[]{:S(2)}, u32[]{:S(2)}) collective-permute-start(f32[8,144,128]{2,1,0:T(8,128)S(1)} %all_to_all.15.later.own), channel_id=1, source_target_pairs={{32,0},{64,32},{96,64},{128,96},{160,128},{192,160},{224,192},{256... | collective-permute-start | bytes 1769480 | tf_op jit(solution)/shard_map/ppermute | solution.py:699
  65.3 2.1 %collective-permute-start.6 = (f32[8,144,128]{2,1,0:T(8,128)S(1)}, f32[8,144,128]{2,1,0:T(8,128)S(1)}, u32[]{:S(2)}, u32[]{:S(2)}) collective-permute-start(f32[8,144,128]{2,1,0:T(8,128)S(1)} %all_to_all.15.later.own), channel_id=1, source_target_pairs={{0,32},{32,64},{64,96},{96,128},{128,160},{160,192},{192,224},{224... | collective-permute-start | bytes 1769480 | tf_op jit(solution)/shard_map/ppermute | solution.py:699
  67.3 0.6 rest0.1.earlier.outer0
  67.9 7.3 %collective-permute-done.7.xa = f32[8,144,128]{2,1,0:T(8,128)S(1)} collective-permute-done((f32[8,144,128]{2,1,0:T(8,128)S(1)}, f32[8,144,128]{2,1,0:T(8,128)S(1)}, u32[]{:S(2)}, u32[]{:S(2)}) %collective-permute-start.7) | collective-permute-done | bytes 589856 | tf_op jit(solution)/shard_map/ppermute | solution.py:699
  75.2 0.0 collective-permute-done.6.xb
  75.2 5.1 %down1.1 = (f32[16,16,128]{2,1,0:T(8,128)S(1)}, f32[6,40,48,128]{3,2,1,0:T(8,128)S(1)}, f32[40,48,128]{2,1,0:T(8,128)S(1)}, f32[40,48,128]{2,1,0:T(8,128)S(1)}, ...) custom-call(s32[4]{0:T(128)S(1)} %pad_add_fusion.pos, ...), custom_call_target="tpu_custom_call" | custom-call | tf_op jit(solution)/shard_map/down1/pallas_call | solution.py:684
  80.3 17.0 %all_to_all.16.pieces = f32[16,16,128]{2,1,0:T(8,128)S(1)} all-to-all(f32[16,16,128]{2,1,0:T(8,128)S(1)} %get-tuple-element.31), channel_id=1, replica_groups=mesh['gx'=16,'gy'=4,'gz'=8] {'gx'}, dimensions={0} | all-to-all | bytes 262144 | tf_op jit(solution)/shard_map/all_to_all | solution.py:756
  97.3 11.8 %all_to_all.17.gathered = f32[4,192,128]{2,1,0:T(8,128)S(1)} all-to-all(f32[4,192,128]{2,1,0:T(8,128)S(1)} %packy.1), channel_id=1, replica_groups=mesh['gx'=16,'gy'=4,'gz'=8] {'gy'}, dimensions={0} | all-to-all | bytes 786432 | tf_op jit(solution)/shard_map/all_to_all | solution.py:758
  109.1 6.1 %up.1 = (f32[8,32,128]{2,1,0:T(8,128)}, f32[8,32,128]{2,1,0:T(8,128)}) custom-call(s32[4]{0:T(128)S(1)} %pad_add_fusion.pos, f32[4,192,128]{2,1,0:T(8,128)S(1)} %all_to_all.17.gathered, f32[6,24,24,128]{3,2,1,0:T(8,128)S(1)} %get-tuple-element.32.weights2, f32[24,24,128]{2,1,0:T(8,128)S(1)} %get-tuple-element.33.scaled2, ...), custom_call_target="tpu_custom_call" | custom-call | tf_op jit(solution)/shard_map/up/pallas_call | solution.py:684
  (2 shorter events, 0.0 us)
Async XLA Ops:
  1.7 7.7 %collective-permute-start = (f32[3,8,8,128]{3,2,1,0:T(8,128)S(1)}, f32[3,8,8,128]{3,2,1,0:T(8,128)S(1)}, u32[]{:S(2)}, u32[]{:S(2)}) collective-permute-start(f32[3,8,8,128]{3,2,1,0:T(8,128)S(1)} %get-tuple-element.21), channel_id=1, source_target_pairs={{0,32},{32,64},{64,96},{96,128},{128,160},{160,192},{192,224},{224... | collective-permute-start | bytes 294920 | tf_op jit(solution)/shard_map/ppermute | solution.py:699
  4.4 5.2 %collective-permute-start.1 = (f32[3,8,8,128]{3,2,1,0:T(8,128)S(1)}, f32[3,8,8,128]{3,2,1,0:T(8,128)S(1)}, u32[]{:S(2)}, u32[]{:S(2)}) collective-permute-start(f32[3,8,8,128]{3,2,1,0:T(8,128)S(1)} %get-tuple-element.22), channel_id=1, source_target_pairs={{32,0},{64,32},{96,64},{128,96},{160,128},{192,160},{224,192},{256... | collective-permute-start | bytes 294920 | tf_op jit(solution)/shard_map/ppermute | solution.py:699
  10.2 6.2 %collective-permute-start.2 = (f32[13,40,128]{2,1,0:T(8,128)S(1)}, f32[13,40,128]{2,1,0:T(8,128)S(1)}, u32[]{:S(2)}, u32[]{:S(2)}) collective-permute-start(f32[13,40,128]{2,1,0:T(8,128)S(1)} %get-tuple-element.23), channel_id=1, source_target_pairs={{0,1},{1,2},{2,3},{3,4},{4,5},{5,6},{6,7},{8,9},{9,10},{10,11},{11... | collective-permute-start | bytes 798728 | tf_op jit(solution)/shard_map/ppermute | solution.py:699
  13.1 8.3 %collective-permute-start.3 = (f32[13,40,128]{2,1,0:T(8,128)S(1)}, f32[13,40,128]{2,1,0:T(8,128)S(1)}, u32[]{:S(2)}, u32[]{:S(2)}) collective-permute-start(f32[13,40,128]{2,1,0:T(8,128)S(1)} %get-tuple-element.24), channel_id=1, source_target_pairs={{1,0},{2,1},{3,2},{4,3},{5,4},{6,5},{7,6},{9,8},{10,9},{11,10},{12... | collective-permute-start | bytes 798728 | tf_op jit(solution)/shard_map/ppermute | solution.py:699
  22.2 9.3 %collective-permute-start.4 = (f32[11,40,128]{2,1,0:T(8,128)S(1)}, f32[11,40,128]{2,1,0:T(8,128)S(1)}, u32[]{:S(2)}, u32[]{:S(2)}) collective-permute-start(f32[11,40,128]{2,1,0:T(8,128)S(1)} %get-tuple-element.26), channel_id=1, source_target_pairs={{0,8},{8,16},{16,24},{1,9},{9,17},{17,25},{2,10},{10,18},{18,26},{... | collective-permute-start | bytes 675848 | tf_op jit(solution)/shard_map/ppermute | solution.py:699
  27.5 7.8 %collective-permute-start.5 = (f32[11,40,128]{2,1,0:T(8,128)S(1)}, f32[11,40,128]{2,1,0:T(8,128)S(1)}, u32[]{:S(2)}, u32[]{:S(2)}) collective-permute-start(f32[11,40,128]{2,1,0:T(8,128)S(1)} %get-tuple-element.27), channel_id=1, source_target_pairs={{8,0},{16,8},{24,16},{9,1},{17,9},{25,17},{10,2},{18,10},{26,18},{... | collective-permute-start | bytes 675848 | tf_op jit(solution)/shard_map/ppermute | solution.py:699
  61.1 14.0 %collective-permute-start.7 = (f32[8,144,128]{2,1,0:T(8,128)S(1)}, f32[8,144,128]{2,1,0:T(8,128)S(1)}, u32[]{:S(2)}, u32[]{:S(2)}) collective-permute-start(f32[8,144,128]{2,1,0:T(8,128)S(1)} %all_to_all.15.later.own), channel_id=1, source_target_pairs={{32,0},{64,32},{96,64},{128,96},{160,128},{192,160},{224,192},{256... | collective-permute-start | bytes 1769480 | tf_op jit(solution)/shard_map/ppermute | solution.py:699
  65.3 9.9 %collective-permute-start.6 = (f32[8,144,128]{2,1,0:T(8,128)S(1)}, f32[8,144,128]{2,1,0:T(8,128)S(1)}, u32[]{:S(2)}, u32[]{:S(2)}) collective-permute-start(f32[8,144,128]{2,1,0:T(8,128)S(1)} %all_to_all.15.later.own), channel_id=1, source_target_pairs={{0,32},{32,64},{64,96},{96,128},{128,160},{160,192},{192,224},{224... | collective-permute-start | bytes 1769480 | tf_op jit(solution)/shard_map/ppermute | solution.py:699

commit v11 on v10

--- a/solution.py
+++ b/solution.py
@@ -442,7 +442,7 @@
     result = dot(thick[0], place2[0])
     for plane in range(1, quarter):
         result = result + dot(thick[plane], place2[plane])
-    copies(message, result)
+    copies(message, result[0:12])
 
 
 def packy(pieces, message):
@@ -745,7 +745,7 @@
     message, weights1, scaled1, iterate1, weights2, scaled2, iterate2 = call(
         down1,
         "down1",
-        [(ranks, 16, 128), (6,) + tall1, tall1, tall1, (6,) + tall2, tall2, tall2],
+        [(ranks, 12, 128), (6,) + tall1, tall1, tall1, (6,) + tall2, tall2, tall2],
         [(3,) + tall1, tall1, (depth1 + 2,) + plane1, (3 * depth2,) + plane1]
         + [(3,) + tall2, tall2, (depth2 + 2,) + plane2, (3 * depth2 // 2, 8, 128)]
         + [(3 * depth2,) + plane2, (2 * group, 16, 128)],

time: 116 us -> 116 us (level)
  no operation moved by 1% of the time
where the time goes in v11:
time: 116 us; the launch traced here: 115 us
  blocking collectives  52.5 us (45%)
  starting transfers between devices  23.9 us (21%)
  waiting for transfers between devices  21.7 us (19%)
  Pallas kernels  15.4 us (13%)
    all_to_all x1, blocking collectives, on_device(): whole1 = lax.all_to_all(message, 'gz', 0, 0)  23.6 us
    all_to_all x1, blocking collectives, on_device(): gathered = lax.all_to_all(message, 'gx', 0, 0)  17 us
    ppermute x4, waiting for transfers between devices, exchange(): lax.ppermute(down_values, axis, down_pairs)  16.3 us
    pallas_call x8, Pallas kernels, call(): pl.pallas_call(body, name=name, out_shape=[jax.ShapeDtypeStruct(shape, F3...  15.4 us
    ppermute x4, starting transfers between devices, exchange(): lax.ppermute(up_values, axis, up_pairs)  13 us
    all_to_all x1, blocking collectives, on_device(): gathered = lax.all_to_all(gathered, 'gy', 0, 0)  11.8 us
    ppermute x4, starting transfers between devices, exchange(): lax.ppermute(down_values, axis, down_pairs)  10.9 us
    ppermute x4, waiting for transfers between devices, exchange(): lax.ppermute(up_values, axis, up_pairs)  5.41 us
  transfers between devices with their start and end apart: 8, of which 7 were waited for; matrix products, arithmetic and copies ran while one was open for 0% of the time, Pallas kernels for 0%

profile of v11, /device:TPU:1, one launch (start us, length us, event | category | flops | bytes accessed | tf_op | source)
XLA Modules:
  0.0 115.3 jit_solution(5413630167428222616)
XLA Ops:
  0.6 1.1 pad_maximum_fusion.own
  1.7 2.7 %collective-permute-start = (f32[3,8,8,128]{3,2,1,0:T(8,128)S(1)}, f32[3,8,8,128]{3,2,1,0:T(8,128)S(1)}, u32[]{:S(2)}, u32[]{:S(2)}) collective-permute-start(f32[3,8,8,128]{3,2,1,0:T(8,128)S(1)} %get-tuple-element.21), channel_id=1, source_target_pairs={{0,32},{32,64},{64,96},{96,128},{128,160},{160,192},{192,224},{224... | collective-permute-start | bytes 294920 | tf_op jit(solution)/shard_map/ppermute | solution.py:699
  4.4 4.2 %collective-permute-start.1 = (f32[3,8,8,128]{3,2,1,0:T(8,128)S(1)}, f32[3,8,8,128]{3,2,1,0:T(8,128)S(1)}, u32[]{:S(2)}, u32[]{:S(2)}) collective-permute-start(f32[3,8,8,128]{3,2,1,0:T(8,128)S(1)} %get-tuple-element.22), channel_id=1, source_target_pairs={{32,0},{64,32},{96,64},{128,96},{160,128},{192,160},{224,192},{256... | collective-permute-start | bytes 294920 | tf_op jit(solution)/shard_map/ppermute | solution.py:699
  8.6 0.1 pad_add_fusion.pos
  8.7 0.7 collective-permute-done.xb
  9.4 0.2 collective-permute-done.1.xa
  9.6 0.6 packz.1
  10.2 2.9 %collective-permute-start.2 = (f32[13,40,128]{2,1,0:T(8,128)S(1)}, f32[13,40,128]{2,1,0:T(8,128)S(1)}, u32[]{:S(2)}, u32[]{:S(2)}) collective-permute-start(f32[13,40,128]{2,1,0:T(8,128)S(1)} %get-tuple-element.23), channel_id=1, source_target_pairs={{0,1},{1,2},{2,3},{3,4},{4,5},{5,6},{6,7},{8,9},{9,10},{10,11},{11... | collective-permute-start | bytes 798728 | tf_op jit(solution)/shard_map/ppermute | solution.py:699
  13.1 1.3 %collective-permute-start.3 = (f32[13,40,128]{2,1,0:T(8,128)S(1)}, f32[13,40,128]{2,1,0:T(8,128)S(1)}, u32[]{:S(2)}, u32[]{:S(2)}) collective-permute-start(f32[13,40,128]{2,1,0:T(8,128)S(1)} %get-tuple-element.24), channel_id=1, source_target_pairs={{1,0},{2,1},{3,2},{4,3},{5,4},{6,5},{7,6},{9,8},{10,9},{11,10},{12... | collective-permute-start | bytes 798728 | tf_op jit(solution)/shard_map/ppermute | solution.py:699
  14.4 2.0 %collective-permute-done.2.zb = f32[13,40,128]{2,1,0:T(8,128)S(1)} collective-permute-done((f32[13,40,128]{2,1,0:T(8,128)S(1)}, f32[13,40,128]{2,1,0:T(8,128)S(1)}, u32[]{:S(2)}, u32[]{:S(2)}) %collective-permute-start.2) | collective-permute-done | bytes 266272 | tf_op jit(solution)/shard_map/ppermute | solution.py:699
  16.4 5.0 %collective-permute-done.3.za = f32[13,40,128]{2,1,0:T(8,128)S(1)} collective-permute-done((f32[13,40,128]{2,1,0:T(8,128)S(1)}, f32[13,40,128]{2,1,0:T(8,128)S(1)}, u32[]{:S(2)}, u32[]{:S(2)}) %collective-permute-start.3) | collective-permute-done | bytes 266272 | tf_op jit(solution)/shard_map/ppermute | solution.py:699
  21.4 0.8 pack0.1
  22.2 5.3 %collective-permute-start.4 = (f32[11,40,128]{2,1,0:T(8,128)S(1)}, f32[11,40,128]{2,1,0:T(8,128)S(1)}, u32[]{:S(2)}, u32[]{:S(2)}) collective-permute-start(f32[11,40,128]{2,1,0:T(8,128)S(1)} %get-tuple-element.26), channel_id=1, source_target_pairs={{0,8},{8,16},{16,24},{1,9},{9,17},{17,25},{2,10},{10,18},{18,26},{... | collective-permute-start | bytes 675848 | tf_op jit(solution)/shard_map/ppermute | solution.py:699
  27.5 1.3 %collective-permute-start.5 = (f32[11,40,128]{2,1,0:T(8,128)S(1)}, f32[11,40,128]{2,1,0:T(8,128)S(1)}, u32[]{:S(2)}, u32[]{:S(2)}) collective-permute-start(f32[11,40,128]{2,1,0:T(8,128)S(1)} %get-tuple-element.27), channel_id=1, source_target_pairs={{8,0},{16,8},{24,16},{9,1},{17,9},{25,17},{10,2},{18,10},{26,18},{... | collective-permute-start | bytes 675848 | tf_op jit(solution)/shard_map/ppermute | solution.py:699
  28.8 2.7 %collective-permute-done.4.before = f32[11,40,128]{2,1,0:T(8,128)S(1)} collective-permute-done((f32[11,40,128]{2,1,0:T(8,128)S(1)}, f32[11,40,128]{2,1,0:T(8,128)S(1)}, u32[]{:S(2)}, u32[]{:S(2)}) %collective-permute-start.4) | collective-permute-done | bytes 225312 | tf_op jit(solution)/shard_map/ppermute | solution.py:699
  31.5 3.8 %collective-permute-done.5.after = f32[11,40,128]{2,1,0:T(8,128)S(1)} collective-permute-done((f32[11,40,128]{2,1,0:T(8,128)S(1)}, f32[11,40,128]{2,1,0:T(8,128)S(1)}, u32[]{:S(2)}, u32[]{:S(2)}) %collective-permute-start.5) | collective-permute-done | bytes 225312 | tf_op jit(solution)/shard_map/ppermute | solution.py:699
  35.3 2.1 %down0.1 = (f32[10,48,256]{2,1,0:T(8,128)S(1)}, f32[8,144,128]{2,1,0:T(8,128)S(1)}, f32[6,12,48,256]{3,2,1,0:T(8,128)S(1)}, f32[12,48,256]{2,1,0:T(8,128)S(1)}, f32[12,48,256]{2,1,0:T(8,128)S(1)}) custom-call(f32[3,18,48,128]{3,2,1,0:T(8,128)S(1)} %get-tuple-element.25.whole, f32[11,40,128]{2,1,0:T(8,128)S(1)} %collective-permute-done.4.before, ...), custom_call_target="tpu_custom_call" | custom-call | tf_op jit(solution)/shard_map/down0/pallas_call | solution.py:684
  37.5 23.6 %all_to_all.15.later.own = f32[8,144,128]{2,1,0:T(8,128)S(1)} all-to-all(f32[8,144,128]{2,1,0:T(8,128)S(1)} %get-tuple-element.28), channel_id=1, replica_groups=mesh['gx'=16,'gy'=4,'gz'=8] {'gz'}, dimensions={0} | all-to-all | bytes 1179648 | tf_op jit(solution)/shard_map/all_to_all | solution.py:730
  61.1 4.1 %collective-permute-start.7 = (f32[8,144,128]{2,1,0:T(8,128)S(1)}, f32[8,144,128]{2,1,0:T(8,128)S(1)}, u32[]{:S(2)}, u32[]{:S(2)}) collective-permute-start(f32[8,144,128]{2,1,0:T(8,128)S(1)} %all_to_all.15.later.own), channel_id=1, source_target_pairs={{32,0},{64,32},{96,64},{128,96},{160,128},{192,160},{224,192},{256... | collective-permute-start | bytes 1769480 | tf_op jit(solution)/shard_map/ppermute | solution.py:699
  65.3 2.1 %collective-permute-start.6 = (f32[8,144,128]{2,1,0:T(8,128)S(1)}, f32[8,144,128]{2,1,0:T(8,128)S(1)}, u32[]{:S(2)}, u32[]{:S(2)}) collective-permute-start(f32[8,144,128]{2,1,0:T(8,128)S(1)} %all_to_all.15.later.own), channel_id=1, source_target_pairs={{0,32},{32,64},{64,96},{96,128},{128,160},{160,192},{192,224},{224... | collective-permute-start | bytes 1769480 | tf_op jit(solution)/shard_map/ppermute | solution.py:699
  67.3 0.6 rest0.1.earlier.outer0
  67.9 7.3 %collective-permute-done.7.xa = f32[8,144,128]{2,1,0:T(8,128)S(1)} collective-permute-done((f32[8,144,128]{2,1,0:T(8,128)S(1)}, f32[8,144,128]{2,1,0:T(8,128)S(1)}, u32[]{:S(2)}, u32[]{:S(2)}) %collective-permute-start.7) | collective-permute-done | bytes 589856 | tf_op jit(solution)/shard_map/ppermute | solution.py:699
  75.2 0.0 collective-permute-done.6.xb
  75.2 5.1 %down1.1 = (f32[16,12,128]{2,1,0:T(8,128)S(1)}, f32[6,40,48,128]{3,2,1,0:T(8,128)S(1)}, f32[40,48,128]{2,1,0:T(8,128)S(1)}, f32[40,48,128]{2,1,0:T(8,128)S(1)}, ...) custom-call(s32[4]{0:T(128)S(1)} %pad_add_fusion.pos, ...), custom_call_target="tpu_custom_call" | custom-call | tf_op jit(solution)/shard_map/down1/pallas_call | solution.py:684
  80.3 17.0 %all_to_all.16.pieces = f32[16,12,128]{2,1,0:T(8,128)S(1)} all-to-all(f32[16,12,128]{2,1,0:T(8,128)S(1)} %get-tuple-element.31), channel_id=1, replica_groups=mesh['gx'=16,'gy'=4,'gz'=8] {'gx'}, dimensions={0} | all-to-all | bytes 196608 | tf_op jit(solution)/shard_map/all_to_all | solution.py:756
  97.3 11.8 %all_to_all.17.gathered = f32[4,192,128]{2,1,0:T(8,128)S(1)} all-to-all(f32[4,192,128]{2,1,0:T(8,128)S(1)} %packy.1), channel_id=1, replica_groups=mesh['gx'=16,'gy'=4,'gz'=8] {'gy'}, dimensions={0} | all-to-all | bytes 786432 | tf_op jit(solution)/shard_map/all_to_all | solution.py:758
  109.1 6.1 %up.1 = (f32[8,32,128]{2,1,0:T(8,128)}, f32[8,32,128]{2,1,0:T(8,128)}) custom-call(s32[4]{0:T(128)S(1)} %pad_add_fusion.pos, f32[4,192,128]{2,1,0:T(8,128)S(1)} %all_to_all.17.gathered, f32[6,24,24,128]{3,2,1,0:T(8,128)S(1)} %get-tuple-element.32.weights2, f32[24,24,128]{2,1,0:T(8,128)S(1)} %get-tuple-element.33.scaled2, ...), custom_call_target="tpu_custom_call" | custom-call | tf_op jit(solution)/shard_map/up/pallas_call | solution.py:684
  (2 shorter events, 0.0 us)
Async XLA Ops:
  1.7 7.7 %collective-permute-start = (f32[3,8,8,128]{3,2,1,0:T(8,128)S(1)}, f32[3,8,8,128]{3,2,1,0:T(8,128)S(1)}, u32[]{:S(2)}, u32[]{:S(2)}) collective-permute-start(f32[3,8,8,128]{3,2,1,0:T(8,128)S(1)} %get-tuple-element.21), channel_id=1, source_target_pairs={{0,32},{32,64},{64,96},{96,128},{128,160},{160,192},{192,224},{224... | collective-permute-start | bytes 294920 | tf_op jit(solution)/shard_map/ppermute | solution.py:699
  4.4 5.2 %collective-permute-start.1 = (f32[3,8,8,128]{3,2,1,0:T(8,128)S(1)}, f32[3,8,8,128]{3,2,1,0:T(8,128)S(1)}, u32[]{:S(2)}, u32[]{:S(2)}) collective-permute-start(f32[3,8,8,128]{3,2,1,0:T(8,128)S(1)} %get-tuple-element.22), channel_id=1, source_target_pairs={{32,0},{64,32},{96,64},{128,96},{160,128},{192,160},{224,192},{256... | collective-permute-start | bytes 294920 | tf_op jit(solution)/shard_map/ppermute | solution.py:699
  10.2 6.2 %collective-permute-start.2 = (f32[13,40,128]{2,1,0:T(8,128)S(1)}, f32[13,40,128]{2,1,0:T(8,128)S(1)}, u32[]{:S(2)}, u32[]{:S(2)}) collective-permute-start(f32[13,40,128]{2,1,0:T(8,128)S(1)} %get-tuple-element.23), channel_id=1, source_target_pairs={{0,1},{1,2},{2,3},{3,4},{4,5},{5,6},{6,7},{8,9},{9,10},{10,11},{11... | collective-permute-start | bytes 798728 | tf_op jit(solution)/shard_map/ppermute | solution.py:699
  13.1 8.3 %collective-permute-start.3 = (f32[13,40,128]{2,1,0:T(8,128)S(1)}, f32[13,40,128]{2,1,0:T(8,128)S(1)}, u32[]{:S(2)}, u32[]{:S(2)}) collective-permute-start(f32[13,40,128]{2,1,0:T(8,128)S(1)} %get-tuple-element.24), channel_id=1, source_target_pairs={{1,0},{2,1},{3,2},{4,3},{5,4},{6,5},{7,6},{9,8},{10,9},{11,10},{12... | collective-permute-start | bytes 798728 | tf_op jit(solution)/shard_map/ppermute | solution.py:699
  22.2 9.3 %collective-permute-start.4 = (f32[11,40,128]{2,1,0:T(8,128)S(1)}, f32[11,40,128]{2,1,0:T(8,128)S(1)}, u32[]{:S(2)}, u32[]{:S(2)}) collective-permute-start(f32[11,40,128]{2,1,0:T(8,128)S(1)} %get-tuple-element.26), channel_id=1, source_target_pairs={{0,8},{8,16},{16,24},{1,9},{9,17},{17,25},{2,10},{10,18},{18,26},{... | collective-permute-start | bytes 675848 | tf_op jit(solution)/shard_map/ppermute | solution.py:699
  27.5 7.8 %collective-permute-start.5 = (f32[11,40,128]{2,1,0:T(8,128)S(1)}, f32[11,40,128]{2,1,0:T(8,128)S(1)}, u32[]{:S(2)}, u32[]{:S(2)}) collective-permute-start(f32[11,40,128]{2,1,0:T(8,128)S(1)} %get-tuple-element.27), channel_id=1, source_target_pairs={{8,0},{16,8},{24,16},{9,1},{17,9},{25,17},{10,2},{18,10},{26,18},{... | collective-permute-start | bytes 675848 | tf_op jit(solution)/shard_map/ppermute | solution.py:699
  61.1 14.0 %collective-permute-start.7 = (f32[8,144,128]{2,1,0:T(8,128)S(1)}, f32[8,144,128]{2,1,0:T(8,128)S(1)}, u32[]{:S(2)}, u32[]{:S(2)}) collective-permute-start(f32[8,144,128]{2,1,0:T(8,128)S(1)} %all_to_all.15.later.own), channel_id=1, source_target_pairs={{32,0},{64,32},{96,64},{128,96},{160,128},{192,160},{224,192},{256... | collective-permute-start | bytes 1769480 | tf_op jit(solution)/shard_map/ppermute | solution.py:699
  65.3 9.9 %collective-permute-start.6 = (f32[8,144,128]{2,1,0:T(8,128)S(1)}, f32[8,144,128]{2,1,0:T(8,128)S(1)}, u32[]{:S(2)}, u32[]{:S(2)}) collective-permute-start(f32[8,144,128]{2,1,0:T(8,128)S(1)} %all_to_all.15.later.own), channel_id=1, source_target_pairs={{0,32},{32,64},{64,96},{96,128},{128,160},{160,192},{192,224},{224... | collective-permute-start | bytes 1769480 | tf_op jit(solution)/shard_map/ppermute | solution.py:699
